TPU v7x, 256 devices: a whole 4x4x8 slice. The times are simulated.
256 devices in a mesh: mode: 64 (over z, x_lo, y), space: 4 (over x_hi, core).
Axes of the slice: x: 4 (x_hi: 2, x_lo: 2; x = x_hi * 2 + x_lo), y: 4, z: 8, core: 2. Of those that a mesh axis runs over, the one named last changes fastest.
Arguments:
- coefs: bfloat16 [4096, 4, 2, 256], P('mode', 'space'), may hold values from -6 to 6
- counts: int32 [4096, 4], P('mode', 'space'), may hold values from 1 to 256
- route: int32 [4096], replicated, may hold values from 0 to 4095, as said below
- basis: bfloat16 [8, 2, 256, 3072], P('space'), may hold values from -0.046875 to 0.046875
- momenta: int32 [4, 3], replicated, may hold values from -3 to 3
- gammas: int32 [4], replicated, may hold values from 0 to 15
Outputs:
- window: float32 [8, 4, 2, 7, 32, 2048], P('space', None, None, None, None, 'mode')
Inputs may be any that keep to these rules, and one draw needn't show every extreme that they name: route is a permutation. The 64 slots of one reader (an aligned block of route, also of coefs and counts) name at most 2 items of any one owner, exactly 2 for 32 owners.
All inputs are finite; a program needn't handle non-finite values.
Results may differ from a plain program's by a relative error of at most 0.0027.
Values may be sent and summed in bfloat16 or wider, within the bound.
No kernel may reach another device: no remote copies, remote signals or barrier semaphores. Data moves between devices by JAX's collectives and lax.ppermute only.
A program may use at most 128 MiB of HBM per device.

v0:
```python
import math

import jax
import jax.numpy as jnp
from jax import lax
from jax.experimental import pallas as pl
from jax.experimental.pallas import tpu as pltpu
from jax.sharding import PartitionSpec as P

LAT = 64
STOPW = 7
PLANES = 8
SPOTS = 8
ITEMS = 64
WIDTH = 256
MODES = 32
ROWS = STOPW * MODES
COLS = 768
OPS = 4
CAND = 128
Z_GROUPS = [[z * SPOTS + p for z in range(PLANES)] for p in range(SPOTS)]
P_GROUPS = [[z * SPOTS + p for p in range(SPOTS)] for z in range(PLANES)]
PAIRS = [(0, 1), (3, 4), (6, 7), (9, 10), (2, 5), (8, 11)]
BF16 = jnp.bfloat16
F32 = jnp.float32


def iota(shape, axis):
    return lax.broadcasted_iota(jnp.int32, shape, axis)


def pack_kernel(route_ref, coefs_ref, counts_ref, out_ref):
    me = lax.axis_index("mode")
    row = route_ref[pl.ds(me // 2, 1), :]
    row = jnp.where(me % 2 == 1, pltpu.roll(row, 64, 1), row)[:, :ITEMS]
    owner = lax.shift_right_logical(row, 6)
    i = iota((ITEMS, ITEMS), 0)
    j = iota((ITEMS, ITEMS), 1)
    owners = jnp.broadcast_to(owner, (ITEMS, ITEMS)).astype(F32)
    column = jnp.sum(jnp.where(i == j, owners, 0.0), axis=1, keepdims=True)
    earlier = jnp.where((owners == column) & (i < j), 1.0, 0.0)
    rank = jnp.max(earlier, axis=0, keepdims=True).astype(jnp.int32)
    target = owner * 2 + rank
    q = iota((PLANES * 32, ITEMS), 0)
    plane = (lax.shift_right_logical(q, 5) - (lax.shift_right_logical(q, 4) & 1)) & 7
    want = plane * 16 + (q & 15)
    outgoing = jnp.where(want == target, 1.0, 0.0).astype(BF16)
    keep = iota((ITEMS, WIDTH), 1) < counts_ref[...]
    for part in range(2):
        block = jnp.where(keep, coefs_ref[:, part, :].astype(F32), 0.0).astype(BF16)
        packed = jnp.dot(outgoing, block, preferred_element_type=F32)
        out_ref[:, part * WIDTH : (part + 1) * WIDTH] = packed.astype(BF16)


def forward_kernel(got_ref, out_ref, sorted_ref):
    n = PLANES * 32
    row = iota((n, n), 0)
    col = iota((n, n), 1)
    source = (lax.shift_right_logical(row, 1) & 7) * 32 + lax.shift_right_logical(row, 4) * 2 + (row & 1)
    order = jnp.where(col == source, 1.0, 0.0).astype(BF16)
    sorted_ref[...] = jnp.dot(order, got_ref[...], preferred_element_type=F32).astype(BF16)
    for spot in range(SPOTS):
        for stop in range(STOPW):
            block = ((spot - stop) % SPOTS) + (SPOTS if spot < stop else 0)
            out_ref[spot, stop * 16 : (stop + 1) * 16, :] = sorted_ref[block * 16 : (block + 1) * 16, :]


def tables_kernel(momenta_ref, gammas_ref, route_ref, placer_ref, table_ref):
    me = lax.axis_index("mode")
    route = route_ref[...]
    owner = lax.shift_right_logical(route, 6)
    key = iota(route.shape, 0) * ITEMS + (route & (ITEMS - 1))
    keyf = key.astype(F32)
    second = (iota((1, CAND), 1) & 1) == 1
    mode = iota((MODES, CAND), 0)
    for stop in range(STOPW):
        hit = owner == ((me - stop) & 63)
        low = jnp.min(jnp.where(hit, keyf, 8192.0), axis=0, keepdims=True)
        high = jnp.max(jnp.where(hit, keyf, -1.0), axis=0, keepdims=True)
        valid = jnp.where(second, high - low, 8000.0 - low) > 0.0
        item = jnp.where(second, high, low).astype(jnp.int32) & (ITEMS - 1)
        item = jnp.where(valid, item, -1)
        for block in range(2):
            placer_ref[block, stop] = jnp.where(mode * 2 + block == item, 1.0, 0.0).astype(BF16)
    place = lax.axis_index("space")
    lane = iota((1, 128), 1)
    site = place * 64 + (lane & 63)
    xs = site & 3
    ys = lax.shift_right_logical(site, 2) & 3
    zs = lax.shift_right_logical(site, 4)
    for op in range(OPS):
        inner = momenta_ref[op, 0] * xs + momenta_ref[op, 1] * ys + momenta_ref[op, 2] * zs
        turn = inner.astype(F32) * (2.0 * math.pi / LAT)
        cosine = jnp.cos(turn)
        sine = jnp.sin(turn)
        bits = lax.shift_right_logical(gammas_ref[op], 2)
        for group in range(6):
            spin = jnp.full((1, 128), group, jnp.int32) if group < 4 else 2 * (group - 4) + lax.shift_right_logical(lane, 6)
            common = spin & bits
            parity = (common ^ lax.shift_right_logical(common, 1)) & 1
            sign = (1 - 2 * parity).astype(F32)
            at = (op * 6 + group) * 2
            table_ref[at : at + 1, :] = cosine * sign
            table_ref[at + 1 : at + 2, :] = sine * sign


def sort_kernel(basis_ref, out_ref):
    low = iota((basis_ref.shape[1], 128), 1) < 64
    for group, (first, second) in enumerate(PAIRS):
        for pair in range(2):
            at = pair * 128
            a = basis_ref[0, :, first * 256 + at : first * 256 + at + 128].astype(F32)
            b = basis_ref[0, :, second * 256 + at : second * 256 + at + 128].astype(F32)
            lanes = slice(group * 128, (group + 1) * 128)
            out_ref[0, 2 * pair, :, lanes] = jnp.where(low, a, pltpu.roll(b, 64, 1)).astype(BF16)
            out_ref[0, 2 * pair + 1, :, lanes] = jnp.where(low, pltpu.roll(a, 64, 1), b).astype(BF16)


def window_kernel(where_ref, gammas_ref, got_ref, placer_ref, table_ref, basis_ref, out_ref, coef_ref, vec_ref, weight_ref):
    @pl.when(pl.program_id(0) == 0)
    def _():
        for stop in range(STOPW):
            rows = got_ref[:, stop * 16 : (stop + 1) * 16, :].reshape(CAND, 2 * WIDTH)
            coef = jnp.dot(placer_ref[0, stop], rows, preferred_element_type=F32)
            re = coef[:, :WIDTH]
            im = coef[:, WIDTH:]
            top = slice(stop * MODES, (stop + 1) * MODES)
            bottom = slice(ROWS + stop * MODES, ROWS + (stop + 1) * MODES)
            coef_ref[top, :WIDTH] = re.astype(BF16)
            coef_ref[top, WIDTH:] = (-im).astype(BF16)
            coef_ref[bottom, :WIDTH] = im.astype(BF16)
            coef_ref[bottom, WIDTH:] = re.astype(BF16)

    vec_ref[...] = jnp.dot(coef_ref[...], basis_ref[0, 0], preferred_element_type=F32).astype(BF16)
    for op in range(OPS):
        flip = gammas_ref[op] & 3
        for group in range(6):
            if group < 4:
                source = group ^ flip
            else:
                source = 4 + ((group - 4) ^ lax.shift_right_logical(flip, 1))
            lanes = pl.ds(pl.multiple_of(source * 128, 128), 128)
            re = vec_ref[0:MODES, lanes].astype(F32)
            im = vec_ref[ROWS : ROWS + MODES, lanes].astype(F32)
            if group >= 4:
                swap = (flip & 1) == 1
                re = jnp.where(swap, pltpu.roll(re, 64, 1), re)
                im = jnp.where(swap, pltpu.roll(im, 64, 1), im)
            at = (op * 6 + group) * 2
            cosine = table_ref[at : at + 1, :]
            sine = table_ref[at + 1 : at + 2, :]
            w_re = cosine * re - sine * im
            w_im = sine * re + cosine * im
            out_lanes = slice(group * 128, (group + 1) * 128)
            weight_ref[op * MODES : (op + 1) * MODES, out_lanes] = w_im.astype(BF16)
            weight_ref[128 + op * MODES : 128 + (op + 1) * MODES, out_lanes] = w_re.astype(BF16)
            weight_ref[256 + op * MODES : 256 + (op + 1) * MODES, out_lanes] = (-w_im).astype(BF16)
    contract = (((1,), (1,)), ((), ()))
    entries = lax.dot_general(vec_ref[:ROWS], weight_ref[128:], contract, preferred_element_type=F32)
    entries += lax.dot_general(vec_ref[ROWS:], weight_ref[:256], contract, preferred_element_type=F32)
    out_ref[0] = entries.astype(out_ref.dtype)


def total_kernel(own_ref, a_ref, b_ref, c_ref, out_ref):
    for t in range(2):
        total = own_ref[t] + a_ref[t].astype(F32) + b_ref[t].astype(F32) + c_ref[t].astype(F32)
        for r in range(2):
            for op in range(OPS):
                at = (r * OPS + op) * MODES
                out_ref[t, op, r] = total[:, at : at + MODES].reshape(STOPW, MODES, MODES)


VMEM = pl.BlockSpec(memory_space=pltpu.VMEM)
SMEM = pl.BlockSpec(memory_space=pltpu.SMEM)


def cost(flops, moved):
    return pl.CostEstimate(flops=flops, bytes_accessed=moved, transcendentals=0)


def window_part(where, gammas, got, placer, table, basis, dtype):
    spec = pltpu.PrefetchScalarGridSpec(
        num_scalar_prefetch=1,
        grid=(2,),
        in_specs=[
            SMEM,
            pl.BlockSpec((SPOTS, STOPW * 16, 2 * WIDTH), lambda i, w: (0, 0, 0)),
            pl.BlockSpec((1, STOPW, MODES, CAND), lambda i, w: (w[0] // 2, 0, 0, 0)),
            pl.BlockSpec((OPS * 12, 128), lambda i, w: (0, 0)),
            pl.BlockSpec((1, 1, 2 * WIDTH, COLS), lambda i, w: (w[0] // 2, 2 * (w[0] % 2) + i, 0, 0)),
        ],
        out_specs=pl.BlockSpec((1, ROWS, 256), lambda i, w: (i, 0, 0)),
        scratch_shapes=[
            pltpu.VMEM((2 * ROWS, 2 * WIDTH), BF16),
            pltpu.VMEM((2 * ROWS, COLS), BF16),
            pltpu.VMEM((384, COLS), BF16),
        ],
    )
    return pl.pallas_call(
        window_kernel,
        out_shape=jax.ShapeDtypeStruct((2, ROWS, 256), dtype),
        grid_spec=spec,
        compiler_params=pltpu.CompilerParams(vmem_limit_bytes=32 * 1024 * 1024),
        cost_estimate=cost(1_100_000_000, 3_000_000),
    )(where, gammas, got, placer, table, basis)


def per_device(coefs, counts, route, basis, momenta, gammas):
    place = lax.axis_index("space")
    packed = pl.pallas_call(
        pack_kernel,
        out_shape=jax.ShapeDtypeStruct((PLANES * 32, 2 * WIDTH), BF16),
        in_specs=[VMEM, VMEM, VMEM],
        out_specs=VMEM,
        cost_estimate=cost(20_000_000, 400_000),
    )(route.reshape(32, 128), coefs.reshape(ITEMS, 2, WIDTH), counts)
    first = lax.all_to_all(
        packed.reshape(PLANES, 32, 2 * WIDTH), "mode", 0, 0, tiled=True, axis_index_groups=Z_GROUPS
    )
    by_reader = route.reshape(PLANES, SPOTS, ITEMS).transpose(2, 1, 0).reshape(ITEMS, 64)
    by_reader = jnp.repeat(by_reader, 2, axis=1)
    placer, table = pl.pallas_call(
        tables_kernel,
        out_shape=(
            jax.ShapeDtypeStruct((2, STOPW, MODES, CAND), BF16),
            jax.ShapeDtypeStruct((OPS * 12, 128), F32),
        ),
        in_specs=[SMEM, SMEM, VMEM],
        out_specs=(VMEM, VMEM),
        cost_estimate=cost(2_000_000, 200_000),
    )(momenta, gammas, by_reader)
    sorted_basis = pl.pallas_call(
        sort_kernel,
        grid=(2, 4),
        out_shape=jax.ShapeDtypeStruct((2, 4, 2 * WIDTH, COLS), BF16),
        in_specs=[pl.BlockSpec((1, 128, 4 * COLS), lambda b, i: (b, i, 0))],
        out_specs=pl.BlockSpec((1, 4, 128, COLS), lambda b, i: (b, 0, i, 0)),
        cost_estimate=cost(10_000_000, 13_000_000),
    )(basis.reshape(2, 2 * WIDTH, 4 * COLS))
    onward = pl.pallas_call(
        forward_kernel,
        out_shape=jax.ShapeDtypeStruct((SPOTS, STOPW * 16, 2 * WIDTH), BF16),
        in_specs=[VMEM],
        out_specs=VMEM,
        scratch_shapes=[pltpu.VMEM((PLANES * 32, 2 * WIDTH), BF16)],
        cost_estimate=cost(70_000_000, 1_200_000),
    )(first.reshape(PLANES * 32, 2 * WIDTH))
    got = lax.all_to_all(onward, "mode", 0, 0, tiled=True, axis_index_groups=P_GROUPS)
    arrived = []
    for mask in (3, 2, 1):
        target = jnp.bitwise_xor(place, mask).reshape(1)
        part = window_part(target, gammas, got, placer, table, sorted_basis, BF16)
        arrived.append(lax.ppermute(part, "space", [(i, i ^ mask) for i in range(4)]))
    own = window_part(place.reshape(1), gammas, got, placer, table, sorted_basis, F32)
    return pl.pallas_call(
        total_kernel,
        out_shape=jax.ShapeDtypeStruct((2, OPS, 2, STOPW, MODES, MODES), F32),
        in_specs=[VMEM] * 4,
        out_specs=VMEM,
        cost_estimate=cost(1_000_000, 3_000_000),
    )(own, *arrived)


def solution(mesh):
    in_specs = (
        P("mode", "space", None, None),
        P("mode", "space"),
        P(),
        P("space", None, None, None),
        P(),
        P(),
    )
    out_specs = P("space", None, None, None, None, "mode")
    return jax.shard_map(
        per_device, mesh=mesh, in_specs=in_specs, out_specs=out_specs, check_vma=False
    )
```

profile of v0, /device:TPU:1, one launch (start us, length us, event | category | flops | bytes accessed | tf_op | source)
XLA Modules:
  0.0 70.1 jit_solution(10418679874476316625)
XLA Ops:
  0.0 1.3 %copy.8.counts_ref = s32[64,1]{1,0:T(8,128)} copy(s32[64,1]{0,1:T(1,128)} %param.7) | data formatting | bytes 512 | tf_op args[1]
  1.3 1.9 %shard_map.64 = bf16[256,512]{1,0:T(8,128)(2,1)} custom-call(s32[32,128]{1,0:T(8,128)} %bitcast.20, bf16[64,2,256]{2,1,0:T(2,128)(2,1)} %bitcast.21, s32[64,1]{1,0:T(8,128)} %copy.8.counts_ref), custom_call_target="tpu_custom_call" | custom-call | flops 20000000 | bytes 400000 | tf_op jit(solution)/shard_map/pallas_call | solution.py:210
  3.3 19.5 %all_to_all.10 = bf16[8,32,512]{2,1,0:T(8,128)(2,1)} all-to-all(bf16[8,32,512]{2,1,0:T(8,128)(2,1)} %bitcast.15), channel_id=1, replica_groups={{0,32,64,96,128,160,192,224},{4,36,68,100,132,164,196,228},{8,40,72,104..., dimensions={0} | all-to-all | bytes 524288 | tf_op jit(solution)/shard_map/all_to_all | solution.py:217
  22.8 2.1 %shard_map.65 = bf16[8,112,512]{2,1,0:T(8,128)(2,1)} custom-call(bf16[256,512]{1,0:T(8,128)(2,1)} %bitcast.16), custom_call_target="tpu_custom_call" | custom-call | flops 70000000 | bytes 1200000 | tf_op jit(solution)/shard_map/pallas_call | solution.py:240
  24.9 5.1 %all-to-all-start.1 = ((bf16[8,112,512]{2,1,0:T(8,128)(2,1)}), bf16[8,112,512]{2,1,0:T(8,128)(2,1)S(1)}, u32[]{:S(2)}, u32[]{:S(2)}) async-start(bf16[8,112,512]{2,1,0:T(8,128)(2,1)} %shard_map.65), calls=%async_computation.1 | async-start | bytes 1835008 | tf_op jit(solution)/shard_map/all_to_all | solution.py:248
  30.0 0.8 %reshape.41 = s32[8,8,64]{2,1,0:T(8,128)S(1)} reshape(s32[4096]{0:T(1024)} %param.8) | data formatting | bytes 32768 | tf_op jit(solution)/shard_map/reshape | solution.py:220
  30.8 0.7 copy.10.route_ref
  31.5 1.6 %shard_map.66 = (bf16[2,7,32,128]{3,2,1,0:T(8,128)(2,1)}, f32[48,128]{1,0:T(8,128)}) custom-call(s32[4,3]{1,0:T(4,128)} %momenta_ref.1, s32[4]{0:T(128)} %gammas_ref.9, s32[64,128]{1,0:T(8,128)} %copy.10.route_ref), custom_call_target="tpu_custom_call" | custom-call | flops 2000000 | bytes 200000 | tf_op jit(solution)/shard_map/pallas_call | solution.py:222
  33.1 0.0 copy-start.1
  33.1 0.0 copy-start.3
  33.1 0.0 copy-start.4
  33.1 9.0 %shard_map.67.basis_ref = bf16[2,4,512,768]{3,2,1,0:T(8,128)(2,1)} custom-call(bf16[2,512,3072]{2,1,0:T(8,128)(2,1)} %bitcast.14), custom_call_target="tpu_custom_call" | custom-call | flops 10000000 | bytes 13000000 | tf_op jit(solution)/shard_map/pallas_call | solution.py:232
  42.1 0.0 all-to-all-done.1.got_ref
  42.1 0.0 copy-done.1
  42.1 0.0 copy-done.3
  42.1 0.0 copy-done.4
  42.1 0.0 copy-start
  42.1 2.8 %copy-done = bf16[2,4,512,768]{3,2,1,0:T(8,128)(2,1)S(1)} copy-done((bf16[2,4,512,768]{3,2,1,0:T(8,128)(2,1)S(1)}, bf16[2,4,512,768]{3,2,1,0:T(8,128)(2,1)}, u32[]{:S(2)}) %copy-start) | copy-done | bytes 6291480
  44.9 3.5 %shard_map.69 = bf16[2,224,256]{2,1,0:T(8,128)(2,1)S(1)} custom-call(s32[1]{0:T(128)} %bitcast.9.where_ref, s32[4]{0:T(128)S(1)} %copy-done.4, bf16[8,112,512]{2,1,0:T(8,128)(2,1)S(1)} %all-to-all-done.1.got_ref, bf16[2,7,32,128]{3,2,1,0:T(8,128)(2,1)S(1)} %copy-done.1, f32[48,128]{1,0:T(8,128)S(1)} %copy-done.3, bf16[2,4,512,768]{3,2,1,0:T(8,128)(2,1)S(1)} %copy-done), custom_call_target="tpu_custom_call" | custom-call | flops 1100000000 | bytes 3000000 | tf_op jit(solution)/shard_map/pallas_call | solution.py:199
  48.4 5.2 %collective-permute-start = (bf16[2,224,256]{2,1,0:T(8,128)(2,1)S(1)}, bf16[2,224,256]{2,1,0:T(8,128)(2,1)S(1)}, u32[]{:S(2)}, u32[]{:S(2)}) collective-permute-start(bf16[2,224,256]{2,1,0:T(8,128)(2,1)S(1)} %shard_map.69), channel_id=1, source_target_pairs={{0,3},{1,2},{2,1},{3,0},{4,7},{5,6},{6,5},{7,4},{8,11},{9,10},{10,... | collective-permute-start | bytes 688136 | tf_op jit(solution)/shard_map/ppermute | solution.py:253
  53.6 3.5 %shard_map.70 = bf16[2,224,256]{2,1,0:T(8,128)(2,1)S(1)} custom-call(s32[1]{0:T(128)} %bitcast.10.where_ref, s32[4]{0:T(128)S(1)} %copy-done.4, bf16[8,112,512]{2,1,0:T(8,128)(2,1)S(1)} %all-to-all-done.1.got_ref, bf16[2,7,32,128]{3,2,1,0:T(8,128)(2,1)S(1)} %copy-done.1, f32[48,128]{1,0:T(8,128)S(1)} %copy-done.3, bf16[2,4,512,768]{3,2,1,0:T(8,128)(2,1)S(1)} %copy-done), custom_call_target="tpu_custom_call" | custom-call | flops 1100000000 | bytes 3000000 | tf_op jit(solution)/shard_map/pallas_call | solution.py:199
  57.1 0.6 collective-permute-start.1
  57.7 3.5 %shard_map.71 = bf16[2,224,256]{2,1,0:T(8,128)(2,1)S(1)} custom-call(s32[1]{0:T(128)} %bitcast.11.where_ref, s32[4]{0:T(128)S(1)} %copy-done.4, bf16[8,112,512]{2,1,0:T(8,128)(2,1)S(1)} %all-to-all-done.1.got_ref, bf16[2,7,32,128]{3,2,1,0:T(8,128)(2,1)S(1)} %copy-done.1, f32[48,128]{1,0:T(8,128)S(1)} %copy-done.3, bf16[2,4,512,768]{3,2,1,0:T(8,128)(2,1)S(1)} %copy-done), custom_call_target="tpu_custom_call" | custom-call | flops 1100000000 | bytes 3000000 | tf_op jit(solution)/shard_map/pallas_call | solution.py:199
  61.3 0.1 collective-permute-start.2
  61.4 3.5 %shard_map.68.own_ref = f32[2,224,256]{2,1,0:T(8,128)S(1)} custom-call(s32[1]{0:T(128)} %bitcast.where_ref, s32[4]{0:T(128)S(1)} %copy-done.4, bf16[8,112,512]{2,1,0:T(8,128)(2,1)S(1)} %all-to-all-done.1.got_ref, bf16[2,7,32,128]{3,2,1,0:T(8,128)(2,1)S(1)} %copy-done.1, f32[48,128]{1,0:T(8,128)S(1)} %copy-done.3, bf16[2,4,512,768]{3,2,1,0:T(8,128)(2,1)S(1)} %copy-done), custom_call_target="tpu_custom_call" | custom-call | flops 1100000000 | bytes 3000000 | tf_op jit(solution)/shard_map/pallas_call | solution.py:199
  64.9 0.0 copy-start.2
  64.9 0.8 %copy-done.2 = f32[2,224,256]{2,1,0:T(8,128)} copy-done((f32[2,224,256]{2,1,0:T(8,128)}, f32[2,224,256]{2,1,0:T(8,128)S(1)}, u32[]{:S(2)}) %copy-start.2) | copy-done | bytes 458776
  65.7 0.0 collective-permute-done.a_ref
  65.7 0.0 copy-start.5
  65.7 0.0 collective-permute-done.1.b_ref
  65.7 0.0 copy-start.6
  65.7 0.0 collective-permute-done.2.c_ref
  65.7 0.7 copy-done.5
  66.4 0.1 copy-done.6
  66.5 0.0 copy-start.7
  66.5 0.7 copy-done.7
  67.1 2.9 %shard_map.72 = f32[2,4,2,7,32,32]{5,4,3,2,1,0:T(8,128)} custom-call(f32[2,224,256]{2,1,0:T(8,128)} %copy-done.2, bf16[2,224,256]{2,1,0:T(8,128)(2,1)} %copy-done.5, bf16[2,224,256]{2,1,0:T(8,128)(2,1)} %copy-done.6, bf16[2,224,256]{2,1,0:T(8,128)(2,1)} %copy-done.7), custom_call_target="tpu_custom_call" | custom-call | flops 1000000 | bytes 3000000 | tf_op jit(solution)/shard_map/pallas_call | solution.py:255
  (2 shorter events, 0.0 us)
Async XLA Ops:
  24.9 17.2 %all-to-all-start.1 = ((bf16[8,112,512]{2,1,0:T(8,128)(2,1)}), bf16[8,112,512]{2,1,0:T(8,128)(2,1)S(1)}, u32[]{:S(2)}, u32[]{:S(2)}) async-start(bf16[8,112,512]{2,1,0:T(8,128)(2,1)} %shard_map.65), calls=%async_computation.1 | async-start | bytes 1835008 | tf_op jit(solution)/shard_map/all_to_all | solution.py:248
  33.1 9.0 %copy-start.1 = (bf16[2,7,32,128]{3,2,1,0:T(8,128)(2,1)S(1)}, bf16[2,7,32,128]{3,2,1,0:T(8,128)(2,1)}, u32[]{:S(2)}) copy-start(bf16[2,7,32,128]{3,2,1,0:T(8,128)(2,1)} %get-tuple-element.7.placer_ref) | copy-start | bytes 344068
  33.1 9.0 %copy-start.3 = (f32[48,128]{1,0:T(8,128)S(1)}, f32[48,128]{1,0:T(8,128)}, u32[]{:S(2)}) copy-start(f32[48,128]{1,0:T(8,128)} %get-tuple-element.8.table_ref) | copy-start | bytes 73732
  33.1 9.0 %copy-start.4 = (s32[4]{0:T(128)S(1)}, s32[4]{0:T(128)}, u32[]{:S(2)}) copy-start(s32[4]{0:T(128)} %gammas_ref.9) | copy-start | bytes 52
  42.1 2.8 %copy-start = (bf16[2,4,512,768]{3,2,1,0:T(8,128)(2,1)S(1)}, bf16[2,4,512,768]{3,2,1,0:T(8,128)(2,1)}, u32[]{:S(2)}) copy-start(bf16[2,4,512,768]{3,2,1,0:T(8,128)(2,1)} %shard_map.67.basis_ref) | copy-start | bytes 18874372
  48.4 17.3 %collective-permute-start = (bf16[2,224,256]{2,1,0:T(8,128)(2,1)S(1)}, bf16[2,224,256]{2,1,0:T(8,128)(2,1)S(1)}, u32[]{:S(2)}, u32[]{:S(2)}) collective-permute-start(bf16[2,224,256]{2,1,0:T(8,128)(2,1)S(1)} %shard_map.69), channel_id=1, source_target_pairs={{0,3},{1,2},{2,1},{3,0},{4,7},{5,6},{6,5},{7,4},{8,11},{9,10},{10,... | collective-permute-start | bytes 688136 | tf_op jit(solution)/shard_map/ppermute | solution.py:253
  57.1 8.6 %collective-permute-start.1 = (bf16[2,224,256]{2,1,0:T(8,128)(2,1)S(1)}, bf16[2,224,256]{2,1,0:T(8,128)(2,1)S(1)}, u32[]{:S(2)}, u32[]{:S(2)}) collective-permute-start(bf16[2,224,256]{2,1,0:T(8,128)(2,1)S(1)} %shard_map.70), channel_id=1, source_target_pairs={{0,2},{1,3},{2,0},{3,1},{4,6},{5,7},{6,4},{7,5},{8,10},{9,11},{10,... | collective-permute-start | bytes 688136 | tf_op jit(solution)/shard_map/ppermute | solution.py:253
  61.3 4.5 %collective-permute-start.2 = (bf16[2,224,256]{2,1,0:T(8,128)(2,1)S(1)}, bf16[2,224,256]{2,1,0:T(8,128)(2,1)S(1)}, u32[]{:S(2)}, u32[]{:S(2)}) collective-permute-start(bf16[2,224,256]{2,1,0:T(8,128)(2,1)S(1)} %shard_map.71), channel_id=1, source_target_pairs={{0,1},{1,0},{2,3},{3,2},{4,5},{5,4},{6,7},{7,6},{8,9},{9,8},{10,11... | collective-permute-start | bytes 688136 | tf_op jit(solution)/shard_map/ppermute | solution.py:253
  64.9 0.8 %copy-start.2 = (f32[2,224,256]{2,1,0:T(8,128)}, f32[2,224,256]{2,1,0:T(8,128)S(1)}, u32[]{:S(2)}) copy-start(f32[2,224,256]{2,1,0:T(8,128)S(1)} %shard_map.68.own_ref) | copy-start | bytes 1376260
  65.7 0.7 copy-start.5
  65.7 0.8 %copy-start.6 = (bf16[2,224,256]{2,1,0:T(8,128)(2,1)}, bf16[2,224,256]{2,1,0:T(8,128)(2,1)S(1)}, u32[]{:S(2)}) copy-start(bf16[2,224,256]{2,1,0:T(8,128)(2,1)S(1)} %collective-permute-done.1.b_ref) | copy-start | bytes 688132
  66.5 0.7 copy-start.7
where the time goes:
time: 70.8 us; the launch traced here: 70.1 us
  Pallas kernels  31.7 us (45%)
  blocking collectives  19.5 us (28%)
  starting transfers between devices  11 us (16%)
  local copies, waits for them, and re-layouts  7.83 us (11%)
    all_to_all x1, blocking collectives, per_device(): lax.all_to_all(packed.reshape(PLANES, 32, 2 * WIDTH), 'mode', 0, 0, tiled...  19.5 us
    pallas_call x4, Pallas kernels, window_part(): pl.pallas_call(window_kernel, out_shape=jax.ShapeDtypeStruct((2, ROWS, 25...  14.1 us
    pallas_call x1, Pallas kernels, per_device(): pl.pallas_call(sort_kernel, grid=(2, 4), out_shape=jax.ShapeDtypeStruct((...  9.01 us
    unnamed x17, local copies, waits for them, and re-layouts  6.32 us
    ppermute x3, starting transfers between devices, per_device(): lax.ppermute(part, 'space', [(i, i ^ mask) for i in range(4)])  5.87 us
    all_to_all x1, starting transfers between devices, per_device(): lax.all_to_all(onward, 'mode', 0, 0, tiled=True, axis_index_groups=P_GROUPS)  5.12 us
    pallas_call x1, Pallas kernels, per_device(): pl.pallas_call(total_kernel, out_shape=jax.ShapeDtypeStruct((2, OPS, 2, S...  2.92 us
    pallas_call x1, Pallas kernels, per_device(): pl.pallas_call(forward_kernel, out_shape=jax.ShapeDtypeStruct((SPOTS, STO...  2.11 us
  transfers between devices with their start and end apart: 4, of which 0 were waited for; matrix products, arithmetic and copies ran while one was open for 2% of the time, Pallas kernels for 30%

commit v1 on v0

v1 whole, which is shorter than its diff:
```python
import functools
import math

import jax
import jax.numpy as jnp
from jax import lax
from jax.experimental import pallas as pl
from jax.experimental.pallas import tpu as pltpu
from jax.sharding import PartitionSpec as P

LAT = 64
STOPW = 7
PLANES = 8
SPOTS = 8
ITEMS = 64
WIDTH = 256
MODES = 32
ROWS = STOPW * MODES
COLS = 768
OPS = 4
CAND = 128
SPARE = 4
Z_GROUPS = [[z * SPOTS + p for z in range(PLANES)] for p in range(SPOTS)]
P_GROUPS = [[z * SPOTS + p for p in range(SPOTS)] for z in range(PLANES)]
PAIRS = [(0, 1), (3, 4), (6, 7), (9, 10), (2, 5), (8, 11)]
BF16 = jnp.bfloat16
F32 = jnp.float32


def iota(shape, axis):
    return lax.broadcasted_iota(jnp.int32, shape, axis)


def pack_kernel(route_ref, coefs_ref, counts_ref, out_ref):
    me = lax.axis_index("mode")
    row = route_ref[pl.ds(me // 2, 1), :]
    row = jnp.where(me % 2 == 1, pltpu.roll(row, 64, 1), row)[:, :ITEMS]
    owner = lax.shift_right_logical(row, 6)
    i = iota((ITEMS, ITEMS), 0)
    j = iota((ITEMS, ITEMS), 1)
    owners = jnp.broadcast_to(owner, (ITEMS, ITEMS)).astype(F32)
    column = jnp.sum(jnp.where(i == j, owners, 0.0), axis=1, keepdims=True)
    earlier = jnp.where((owners == column) & (i < j), 1.0, 0.0)
    rank = jnp.max(earlier, axis=0, keepdims=True).astype(jnp.int32)
    target = owner * 2 + rank
    q = iota((PLANES * 32, ITEMS), 0)
    plane = (lax.shift_right_logical(q, 5) - (lax.shift_right_logical(q, 4) & 1)) & 7
    want = plane * 16 + (q & 15)
    outgoing = jnp.where(want == target, 1.0, 0.0).astype(BF16)
    counts = jnp.broadcast_to(counts_ref[...], (ITEMS, ITEMS)).astype(F32)
    limit = jnp.sum(jnp.where(i == j, counts, 0.0), axis=1, keepdims=True).astype(jnp.int32)
    keep = iota((ITEMS, WIDTH), 1) < limit
    for part in range(2):
        block = jnp.where(keep, coefs_ref[:, part, :].astype(F32), 0.0).astype(BF16)
        packed = jnp.dot(outgoing, block, preferred_element_type=F32)
        out_ref[:, part * WIDTH : (part + 1) * WIDTH] = packed.astype(BF16)


def forward_kernel(got_ref, done_ref, out_ref, sorted_ref, sems):
    n = (SPOTS + STOPW - 1) * 16
    row = iota((n, PLANES * 32), 0)
    col = iota((n, PLANES * 32), 1)
    block = (SPOTS - 1 - lax.shift_right_logical(row, 4)) & 15
    source = (lax.shift_right_logical(row, 1) & 7) * 32 + block * 2 + (row & 1)
    order = jnp.where(col == source, 1.0, 0.0).astype(BF16)
    sorted_ref[...] = jnp.dot(order, got_ref[...], preferred_element_type=F32).astype(BF16)
    copies = []
    for spot in range(SPOTS):
        at = (SPOTS - 1 - spot) * 16
        copies.append(pltpu.make_async_copy(sorted_ref.at[at : at + STOPW * 16], out_ref.at[spot], sems.at[spot]))
    for copy in copies:
        copy.start()
    for copy in copies:
        copy.wait()


def tables_kernel(momenta_ref, gammas_ref, route_ref, placer_ref, table_ref):
    me = lax.axis_index("mode")
    route = route_ref[...]
    owner = lax.shift_right_logical(route, 6)
    key = iota(route.shape, 0) * ITEMS + (route & (ITEMS - 1))
    keyf = key.astype(F32)
    second = (iota((1, CAND), 1) & 1) == 1
    mode = iota((MODES, CAND), 0)
    for stop in range(STOPW):
        hit = owner == ((me - stop) & 63)
        low = jnp.min(jnp.where(hit, keyf, 8192.0), axis=0, keepdims=True)
        high = jnp.max(jnp.where(hit, keyf, -1.0), axis=0, keepdims=True)
        valid = jnp.where(second, high - low, 8000.0 - low) > 0.0
        item = jnp.where(second, high, low).astype(jnp.int32) & (ITEMS - 1)
        item = jnp.where(valid, item, -1)
        for block in range(2):
            placer_ref[stop, block * MODES : (block + 1) * MODES] = jnp.where(mode * 2 + block == item, 1.0, 0.0).astype(BF16)
    place = lax.axis_index("space")
    lane = iota((1, 128), 1)
    site = place * 64 + (lane & 63)
    xs = site & 3
    ys = lax.shift_right_logical(site, 2) & 3
    zs = lax.shift_right_logical(site, 4)
    for op in range(OPS):
        inner = momenta_ref[op, 0] * xs + momenta_ref[op, 1] * ys + momenta_ref[op, 2] * zs
        turn = inner.astype(F32) * (2.0 * math.pi / LAT)
        cosine = jnp.cos(turn)
        sine = jnp.sin(turn)
        bits = lax.shift_right_logical(gammas_ref[op], 2)
        for group in range(6):
            spin = jnp.full((1, 128), group, jnp.int32) if group < 4 else 2 * (group - 4) + lax.shift_right_logical(lane, 6)
            common = spin & bits
            parity = (common ^ lax.shift_right_logical(common, 1)) & 1
            sign = (1 - 2 * parity).astype(F32)
            at = (op * 6 + group) * 2
            table_ref[at : at + 1, :] = cosine * sign
            table_ref[at + 1 : at + 2, :] = sine * sign


def sort_kernel(basis_ref, out_ref, done_ref, slots_ref, sems):
    done_ref[...] = jnp.zeros(done_ref.shape, F32)
    step = 64
    low = iota((step, 128), 1) < 64

    def leave(chunk, slot):
        rows = pl.ds(pl.multiple_of(chunk * step, step), step)
        return pltpu.make_async_copy(slots_ref.at[slot], out_ref.at[0:2, :, rows, :], sems.at[slot])

    @pl.loop(0, 2 * WIDTH // step // 2)
    def _(turn):
        for slot in range(2):
            chunk = turn * 2 + slot

            @pl.when(turn > 0)
            def _():
                leave(chunk - 2, slot).wait()

            rows = pl.ds(pl.multiple_of(chunk * step, step), step)
            for block in range(2):
                for group, (first, second) in enumerate(PAIRS):
                    lanes = slice(group * 128, (group + 1) * 128)
                    for pair in range(2):
                        at = pair * 128
                        a = basis_ref[block, rows, first * 256 + at : first * 256 + at + 128].astype(F32)
                        b = basis_ref[block, rows, second * 256 + at : second * 256 + at + 128].astype(F32)
                        even = jnp.where(low, a, pltpu.roll(b, 64, 1))
                        odd = jnp.where(low, pltpu.roll(a, 64, 1), b)
                        slots_ref[slot, block, 2 * pair, :, lanes] = even.astype(BF16)
                        slots_ref[slot, block, 2 * pair + 1, :, lanes] = odd.astype(BF16)
            leave(chunk, slot).start()

    for slot in range(2):
        leave(2 * WIDTH // step - 2 + slot, slot).wait()


def fetch(sorted_ref, slab_ref, sems, mask):
    target = lax.axis_index("space") ^ mask
    block = lax.shift_right_logical(target, 1)
    first = 2 * (target & 1)
    return [
        pltpu.make_async_copy(sorted_ref.at[block, first + t], slab_ref.at[t], sems.at[t]) for t in range(2)
    ]


def place(got_ref, placer_ref, coef_ref):
    for stop in range(STOPW):
        rows = got_ref[:, stop * 16 : (stop + 1) * 16, :].reshape(CAND, 2 * WIDTH)
        coef = jnp.dot(placer_ref[stop], rows, preferred_element_type=F32)
        for block in range(2):
            re = coef[block * MODES : (block + 1) * MODES, :WIDTH]
            im = coef[block * MODES : (block + 1) * MODES, WIDTH:]
            top = slice(stop * MODES, (stop + 1) * MODES)
            bottom = slice(ROWS + stop * MODES, ROWS + (stop + 1) * MODES)
            coef_ref[block, top, :WIDTH] = re.astype(BF16)
            coef_ref[block, top, WIDTH:] = (-im).astype(BF16)
            coef_ref[block, bottom, :WIDTH] = im.astype(BF16)
            coef_ref[block, bottom, WIDTH:] = re.astype(BF16)


def first_kernel(mask, after, gammas_ref, table_ref, got_ref, placer_ref, sorted_ref, out_ref, coef_ref, next_ref, slab_ref, vec_ref, weight_ref, sems, next_sems):
    now = fetch(sorted_ref, slab_ref, sems, mask)
    later = fetch(sorted_ref, next_ref, next_sems, after)
    for copy in now + later:
        copy.start()
    place(got_ref, placer_ref, coef_ref)
    for copy in now:
        copy.wait()
    entries(mask, gammas_ref, table_ref, coef_ref, slab_ref, out_ref, vec_ref, weight_ref)
    for copy in later:
        copy.wait()


def middle_kernel(mask, after, gammas_ref, table_ref, coef_ref, slab_ref, sorted_ref, out_ref, next_ref, vec_ref, weight_ref, next_sems):
    later = fetch(sorted_ref, next_ref, next_sems, after)
    for copy in later:
        copy.start()
    entries(mask, gammas_ref, table_ref, coef_ref, slab_ref, out_ref, vec_ref, weight_ref)
    for copy in later:
        copy.wait()


def last_kernel(mask, after, gammas_ref, table_ref, coef_ref, slab_ref, sorted_ref, chip_ref, out_ref, own_ref, next_ref, vec_ref, weight_ref, next_sems):
    later = fetch(sorted_ref, next_ref, next_sems, after)
    for copy in later:
        copy.start()
    entries(mask, gammas_ref, table_ref, coef_ref, slab_ref, out_ref, vec_ref, weight_ref)
    for copy in later:
        copy.wait()
    entries(after, gammas_ref, table_ref, coef_ref, next_ref, own_ref, vec_ref, weight_ref)


def entries(mask, gammas_ref, table_ref, coef_ref, slab_ref, out_ref, vec_ref, weight_ref):
    block = lax.shift_right_logical(lax.axis_index("space") ^ mask, 1)
    for t in range(2):
        vec_ref[t] = jnp.dot(coef_ref[block], slab_ref[t], preferred_element_type=F32).astype(BF16)
    for t in range(2):
        for op in range(OPS):
            flip = gammas_ref[op] & 3
            for group in range(6):
                if group < 4:
                    source = group ^ flip
                else:
                    source = 4 + ((group - 4) ^ lax.shift_right_logical(flip, 1))
                lanes = pl.ds(pl.multiple_of(source * 128, 128), 128)
                re = vec_ref[t, 0:MODES, lanes].astype(F32)
                im = vec_ref[t, ROWS : ROWS + MODES, lanes].astype(F32)
                if group >= 4:
                    swap = (flip & 1) == 1
                    re = jnp.where(swap, pltpu.roll(re, 64, 1), re)
                    im = jnp.where(swap, pltpu.roll(im, 64, 1), im)
                at = (op * 6 + group) * 2
                cosine = table_ref[at : at + 1, :]
                sine = table_ref[at + 1 : at + 2, :]
                w_re = cosine * re - sine * im
                w_im = sine * re + cosine * im
                out_lanes = slice(group * 128, (group + 1) * 128)
                weight_ref[t, op * MODES : (op + 1) * MODES, out_lanes] = w_im.astype(BF16)
                weight_ref[t, 128 + op * MODES : 128 + (op + 1) * MODES, out_lanes] = w_re.astype(BF16)
                weight_ref[t, 256 + op * MODES : 256 + (op + 1) * MODES, out_lanes] = (-w_im).astype(BF16)
        contract = (((1,), (1,)), ((), ()))
        part = lax.dot_general(vec_ref[t, :ROWS], weight_ref[t, 128:], contract, preferred_element_type=F32)
        part += lax.dot_general(vec_ref[t, ROWS:], weight_ref[t, :256], contract, preferred_element_type=F32)
        out_ref[t] = part.astype(out_ref.dtype)


def pair_kernel(own_ref, other_ref, out_ref):
    out_ref[...] = (own_ref[...] + other_ref[...].astype(F32)).astype(BF16)


def total_kernel(own_ref, a_ref, b_ref, out_ref, total_ref, sems):
    copies = []
    for t in range(2):
        total = own_ref[t] + a_ref[t].astype(F32) + b_ref[t].astype(F32)
        for op in range(OPS):
            for r in range(2):
                at = (r * OPS + op) * MODES
                total_ref[t, op, r] = total[:, at : at + MODES].reshape(STOPW, MODES, MODES)
            copy = pltpu.make_async_copy(total_ref.at[t, op], out_ref.at[t, op], sems.at[t, op])
            copy.start()
            copies.append(copy)
    for copy in copies:
        copy.wait()


VMEM = pl.BlockSpec(memory_space=pltpu.VMEM)
SMEM = pl.BlockSpec(memory_space=pltpu.SMEM)
HBM = pl.BlockSpec(memory_space=pltpu.HBM)
DMA = pltpu.SemaphoreType.DMA


def kernel_call(kernel, out_shape, in_specs, flops, moved, scratch=(), limit=8, out_specs=None):
    many = isinstance(out_shape, tuple)
    return pl.pallas_call(
        kernel,
        out_shape=out_shape,
        in_specs=in_specs,
        out_specs=out_specs or ((VMEM,) * len(out_shape) if many else VMEM),
        scratch_shapes=list(scratch),
        compiler_params=pltpu.CompilerParams(vmem_limit_bytes=limit * 1024 * 1024),
        cost_estimate=pl.CostEstimate(flops=flops, bytes_accessed=moved, transcendentals=0),
    )


def shape(dims, dtype=BF16):
    return jax.ShapeDtypeStruct(dims, dtype)


def per_device(coefs, counts, route, basis, momenta, gammas):
    packed = kernel_call(
        pack_kernel, shape((PLANES * 32, 2 * WIDTH)), [VMEM] * 3, 20_000_000, 400_000
    )(route.reshape(32, 128), coefs.reshape(ITEMS, 2, WIDTH), counts.reshape(1, ITEMS))
    first = lax.all_to_all(
        packed.reshape(PLANES, 32, 2 * WIDTH), "mode", 0, 0, tiled=True, axis_index_groups=Z_GROUPS
    )
    by_reader = route.reshape(PLANES, SPOTS, ITEMS).transpose(2, 1, 0).reshape(ITEMS, 64)
    by_reader = jnp.repeat(by_reader, 2, axis=1)
    placer, table = kernel_call(
        tables_kernel,
        (shape((STOPW, ITEMS, CAND)), shape((OPS * 12, 128), F32)),
        [SMEM, SMEM, VMEM],
        2_000_000,
        200_000,
    )(momenta, gammas, by_reader)
    sorted_basis, done = kernel_call(
        sort_kernel,
        (shape((SPARE * 2, 4, 2 * WIDTH, COLS)), shape((8, 128), F32)),
        [VMEM],
        10_000_000,
        13_000_000,
        [pltpu.VMEM((2, 2, 4, 64, COLS), BF16), DMA((2,))],
        limit=44,
        out_specs=(HBM, VMEM),
    )(basis.reshape(2, 2 * WIDTH, 4 * COLS))
    onward = kernel_call(
        forward_kernel,
        shape((SPOTS, STOPW * 16, 2 * WIDTH)),
        [VMEM, VMEM],
        70_000_000,
        1_200_000,
        [pltpu.VMEM(((SPOTS + STOPW - 1) * 16, 2 * WIDTH), BF16), DMA((SPOTS,))],
        out_specs=HBM,
    )(first.reshape(PLANES * 32, 2 * WIDTH), done)
    got = lax.all_to_all(onward, "mode", 0, 0, tiled=True, axis_index_groups=P_GROUPS)
    part_shape = shape((2, ROWS, 256))
    coef_shape = shape((2, 2 * ROWS, 2 * WIDTH))
    slab_shape = shape((2, 2 * WIDTH, COLS))
    work = [pltpu.VMEM((2, 2 * ROWS, COLS), BF16), pltpu.VMEM((2, 384, COLS), BF16)]
    part_3, coef, slab = kernel_call(
        functools.partial(first_kernel, 3, 2),
        (part_shape, coef_shape, slab_shape),
        [SMEM, VMEM, VMEM, VMEM, HBM],
        1_100_000_000,
        5_000_000,
        [pltpu.VMEM((2, 2 * WIDTH, COLS), BF16)] + work + [DMA((2,)), DMA((2,))],
        limit=44,
    )(gammas, table, got, placer, sorted_basis)
    def between(pair, part):
        return lax.ppermute(part, "space", [(i, i ^ pair) for i in range(4)])

    part_2, slab = kernel_call(
        functools.partial(middle_kernel, 2, 1),
        (shape((2, ROWS, 256), F32), slab_shape),
        [SMEM, VMEM, VMEM, VMEM, HBM],
        1_100_000_000,
        4_000_000,
        work + [DMA((2,))],
        limit=44,
    )(gammas, table, coef, slab, sorted_basis)
    chip = kernel_call(pair_kernel, part_shape, [VMEM] * 2, 200_000, 900_000)(part_2, between(1, part_3))
    far = between(2, chip)
    part_1, own = kernel_call(
        functools.partial(last_kernel, 1, 0),
        (part_shape, shape((2, ROWS, 256), F32)),
        [SMEM, VMEM, VMEM, VMEM, HBM, VMEM],
        2_200_000_000,
        4_000_000,
        [pltpu.VMEM((2, 2 * WIDTH, COLS), BF16)] + work + [DMA((2,))],
        limit=44,
    )(gammas, table, coef, slab, sorted_basis, chip)
    part_1, far = lax.optimization_barrier((part_1, far))
    near = between(1, part_1)
    return kernel_call(
        total_kernel,
        shape((2, OPS, 2, STOPW, MODES, MODES), F32),
        [VMEM] * 3,
        1_000_000,
        3_000_000,
        [pltpu.VMEM((2, OPS, 2, STOPW, MODES, MODES), F32), DMA((2, OPS))],
        out_specs=HBM,
    )(own, far, near)


def solution(mesh):
    in_specs = (
        P("mode", "space", None, None),
        P("mode", "space"),
        P(),
        P("space", None, None, None),
        P(),
        P(),
    )
    out_specs = P("space", None, None, None, None, "mode")
    return jax.shard_map(
        per_device, mesh=mesh, in_specs=in_specs, out_specs=out_specs, check_vma=False
    )
```

time: 70.8 us -> 63.4 us (0.90)
  blocking collectives: 19.5 us -> 0 us
  waiting for transfers between devices: 0.01 us -> 13.4 us
  starting transfers between devices: 11 us -> 22.5 us
  Pallas kernels: 31.7 us -> 21.8 us
  local copies, waits for them, and re-layouts: 7.83 us -> 5.19 us
    all_to_all x1 -> x0, blocking collectives: 19.5 us -> none  [per_device(): lax.all_to_all(packed.reshape(PLANES, 32, 2 * WIDTH), 'mode', 0, 0, tiled...]
    pallas_call x9, Pallas kernels: 31.7 us -> 21.8 us  [the longest x1 5.32 us: per_device(): kernel_call(sort_kernel, (shape((SPARE * 2, 4, 2 * WIDTH, COLS)), shape((...]
    all_to_all x0 -> x1, starting transfers between devices: none -> 9.02 us  [per_device(): lax.all_to_all(packed.reshape(PLANES, 32, 2 * WIDTH), 'mode', 0, 0, tiled...]
    all_to_all x1, waiting for transfers between devices: 0.01 us -> 8.59 us  [per_device(): lax.all_to_all(onward, 'mode', 0, 0, tiled=True, axis_index_groups=P_GROUPS)]
    ppermute x3, waiting for transfers between devices: 0.01 us -> 2.55 us  [between(): return lax.ppermute(part, 'space', [(i, i ^ pair) for i in range(4)])]
    ppermute x3, starting transfers between devices: 5.87 us -> 8.35 us  [between(): return lax.ppermute(part, 'space', [(i, i ^ pair) for i in range(4)])]
    all_to_all x0 -> x1, waiting for transfers between devices: none -> 2.22 us  [per_device(): lax.all_to_all(packed.reshape(PLANES, 32, 2 * WIDTH), 'mode', 0, 0, tiled...]
    unnamed x17 -> x14, local copies, waits for them, and re-layouts: 6.32 us -> 5.02 us
  transfers between devices with their start and end apart: 4 -> 5, of which waited for: 0 -> 4; matrix products, arithmetic and copies ran while one was open for 2% -> 0% of each run, Pallas kernels for 30% -> 22%
where the time goes in v1:
time: 63.4 us; the launch traced here: 63 us
  starting transfers between devices  22.5 us (35%)
  Pallas kernels  21.8 us (34%)
  waiting for transfers between devices  13.4 us (21%)
  local copies, waits for them, and re-layouts  5.19 us (8%)
    all_to_all x1, starting transfers between devices, per_device(): lax.all_to_all(packed.reshape(PLANES, 32, 2 * WIDTH), 'mode', 0, 0, tiled...  9.02 us
    all_to_all x1, waiting for transfers between devices, per_device(): lax.all_to_all(onward, 'mode', 0, 0, tiled=True, axis_index_groups=P_GROUPS)  8.59 us
    ppermute x3, starting transfers between devices, between(): return lax.ppermute(part, 'space', [(i, i ^ pair) for i in range(4)])  8.35 us
    pallas_call x1, Pallas kernels, per_device(): kernel_call(sort_kernel, (shape((SPARE * 2, 4, 2 * WIDTH, COLS)), shape((...  5.32 us
    all_to_all x1, starting transfers between devices, per_device(): lax.all_to_all(onward, 'mode', 0, 0, tiled=True, axis_index_groups=P_GROUPS)  5.13 us
    unnamed x14, local copies, waits for them, and re-layouts  5.02 us
    pallas_call x1, Pallas kernels, per_device(): kernel_call(functools.partial(last_kernel, 1, 0), (part_shape, shape((2,...  4.84 us
    pallas_call x1, Pallas kernels, per_device(): kernel_call(functools.partial(first_kernel, 3, 2), (part_shape, coef_shap...  4.06 us
  transfers between devices with their start and end apart: 5, of which 4 were waited for; matrix products, arithmetic and copies ran while one was open for 0% of the time, Pallas kernels for 22%

profile of v1, /device:TPU:1, one launch (start us, length us, event | category | flops | bytes accessed | tf_op | source)
XLA Modules:
  0.0 63.0 jit_solution(13030150858369927359)
XLA Ops:
  0.0 0.0 copy-start.1
  0.0 0.8 %copy-done.1 = bf16[64,1,2,256]{3,2,1,0:T(2,128)(2,1)S(1)} copy-done((bf16[64,1,2,256]{3,2,1,0:T(2,128)(2,1)S(1)}, bf16[64,1,2,256]{3,2,1,0:T(2,128)(2,1)}, u32[]{:S(2)}) %copy-start.1) | copy-done | bytes 65560
  0.8 0.0 copy-start.2
  0.8 0.7 %copy-done.2 = s32[4096]{0:T(1024)S(1)} copy-done((s32[4096]{0:T(1024)S(1)}, s32[4096]{0:T(1024)}, u32[]{:S(2)}) %copy-start.2) | copy-done | bytes 16408
  1.6 0.0 copy-start.6
  1.6 0.7 %copy-done.6 = s32[64,1]{0,1:T(1,128)S(1)} copy-done((s32[64,1]{0,1:T(1,128)S(1)}, s32[64,1]{0,1:T(1,128)}, u32[]{:S(2)}) %copy-start.6) | copy-done | bytes 280
  2.2 1.1 %shard_map.65 = bf16[256,512]{1,0:T(8,128)(2,1)} custom-call(s32[32,128]{1,0:T(8,128)S(1)} %bitcast.14, bf16[64,2,256]{2,1,0:T(2,128)(2,1)S(1)} %bitcast.13, s32[1,64]{1,0:T(1,128)S(1)} %bitcast.15), custom_call_target="tpu_custom_call" | custom-call | flops 20000000 | bytes 400000 | tf_op jit(solution)/shard_map/pallas_call | solution.py:285
  3.3 9.0 %all-to-all-start = ((bf16[8,32,512]{2,1,0:T(8,128)(2,1)}), bf16[8,32,512]{2,1,0:T(8,128)(2,1)S(1)}, u32[]{:S(2)}, u32[]{:S(2)}) async-start(bf16[8,32,512]{2,1,0:T(8,128)(2,1)} %bitcast.6), calls=%async_computation | async-start | bytes 524288 | tf_op jit(solution)/shard_map/all_to_all | solution.py:288
  12.3 0.0 copy-start
  12.3 2.8 %copy-done = bf16[2,2,256,3072]{3,2,1,0:T(8,128)(2,1)S(1)} copy-done((bf16[2,2,256,3072]{3,2,1,0:T(8,128)(2,1)S(1)}, bf16[2,2,256,3072]{3,2,1,0:T(8,128)(2,1)}, u32[]{:S(2)}) %copy-start) | copy-done | bytes 6291480
  15.1 5.3 %shard_map.66 = (bf16[8,4,512,768]{3,2,1,0:T(8,128)(2,1)}, f32[8,128]{1,0:T(8,128)S(1)}) custom-call(bf16[2,512,3072]{2,1,0:T(8,128)(2,1)S(1)} %bitcast.11), custom_call_target="tpu_custom_call" | custom-call | flops 10000000 | bytes 13000000 | tf_op jit(solution)/shard_map/pallas_call | solution.py:300
  20.4 0.0 copy-start.3
  20.5 0.0 copy-start.4
  20.5 0.0 copy-start.5
  20.5 2.2 %all-to-all-done = bf16[8,32,512]{2,1,0:T(8,128)(2,1)S(1)} async-done(((bf16[8,32,512]{2,1,0:T(8,128)(2,1)}), bf16[8,32,512]{2,1,0:T(8,128)(2,1)S(1)}, u32[]{:S(2)}, u32[]{:S(2)}) %all-to-all-start) | async-done | bytes 262176 | tf_op jit(solution)/shard_map/all_to_all | solution.py:288
  22.7 1.2 %shard_map.67 = bf16[8,112,512]{2,1,0:T(8,128)(2,1)} custom-call(bf16[256,512]{1,0:T(8,128)(2,1)S(1)} %bitcast.12, f32[8,128]{1,0:T(8,128)S(1)} %get-tuple-element.19.done_ref), custom_call_target="tpu_custom_call" | custom-call | flops 70000000 | bytes 1200000 | tf_op jit(solution)/shard_map/pallas_call | solution.py:310
  23.9 5.1 %all-to-all-start.1 = ((bf16[8,112,512]{2,1,0:T(8,128)(2,1)}), bf16[8,112,512]{2,1,0:T(8,128)(2,1)S(1)}, u32[]{:S(2)}, u32[]{:S(2)}) async-start(bf16[8,112,512]{2,1,0:T(8,128)(2,1)} %shard_map.67), calls=%async_computation.1 | async-start | bytes 1835008 | tf_op jit(solution)/shard_map/all_to_all | solution.py:319
  29.0 0.0 copy-done.3
  29.0 0.1 reshape.27
  29.2 0.1 copy.8.route_ref
  29.2 0.0 copy-done.4
  29.2 0.0 copy-done.5
  29.3 0.8 %shard_map.64 = (bf16[7,64,128]{2,1,0:T(8,128)(2,1)S(1)}, f32[48,128]{1,0:T(8,128)S(1)}) custom-call(s32[4,3]{1,0:T(4,128)S(1)} %copy-done.5, s32[4]{0:T(128)S(1)} %copy-done.4, s32[64,128]{1,0:T(8,128)S(1)} %copy.8.route_ref), custom_call_target="tpu_custom_call" | custom-call | flops 2000000 | bytes 200000 | tf_op jit(solution)/shard_map/pallas_call | solution.py:293
  30.0 8.6 %all-to-all-done.1.got_ref = bf16[8,112,512]{2,1,0:T(8,128)(2,1)S(1)} async-done(((bf16[8,112,512]{2,1,0:T(8,128)(2,1)}), bf16[8,112,512]{2,1,0:T(8,128)(2,1)S(1)}, u32[]{:S(2)}, u32[]{:S(2)}) %all-to-all-start.1) | async-done | bytes 917536 | tf_op jit(solution)/shard_map/all_to_all | solution.py:319
  38.6 4.1 %shard_map.68 = (bf16[2,224,256]{2,1,0:T(8,128)(2,1)S(1)}, bf16[2,448,512]{2,1,0:T(8,128)(2,1)S(1)}, bf16[2,512,768]{2,1,0:T(8,128)(2,1)S(1)}) custom-call(s32[4]{0:T(128)S(1)} %copy-done.4, f32[48,128]{1,0:T(8,128)S(1)} %get-tuple-element.18.table_ref, bf16[8,112,512]{2,1,0:T(8,128)(2,1)S(1)} %all-to-all-done.1.got_ref, ...), custom_call_target="tpu_custom_call" | custom-call | flops 1100000000 | bytes 5000000 | tf_op jit(solution)/shard_map/pallas_call | solution.py:324
  42.7 5.0 %collective-permute-start = (bf16[2,224,256]{2,1,0:T(8,128)(2,1)S(1)}, bf16[2,224,256]{2,1,0:T(8,128)(2,1)S(1)}, u32[]{:S(2)}, u32[]{:S(2)}) collective-permute-start(bf16[2,224,256]{2,1,0:T(8,128)(2,1)S(1)} %get-tuple-element.26), channel_id=1, source_target_pairs={{0,1},{1,0},{2,3},{3,2},{4,5},{5,4},{6,7},{7,6},{8,9},{9,8},{10,11... | collective-permute-start | bytes 688136 | tf_op jit(solution)/shard_map/ppermute | solution.py:334
  47.7 3.2 %shard_map.69 = (f32[2,224,256]{2,1,0:T(8,128)S(1)}, bf16[2,512,768]{2,1,0:T(8,128)(2,1)S(1)}) custom-call(s32[4]{0:T(128)S(1)} %copy-done.4, f32[48,128]{1,0:T(8,128)S(1)} %get-tuple-element.18.table_ref, bf16[2,448,512]{2,1,0:T(8,128)(2,1)S(1)} %get-tuple-element.22.coef_ref, bf16[2,512,768]{2,1,0:T(8,128)(2,1)S(1)} %get-tuple-element.23.slab_ref, ...), custom_call_target="tpu_custom_call" | custom-call | flops 1100000000 | bytes 4000000 | tf_op jit(solution)/shard_map/pallas_call | solution.py:336
  50.9 0.0 collective-permute-done.other_ref
  50.9 2.5 %collective-permute-start.1 = (bf16[2,224,256]{2,1,0:T(8,128)(2,1)S(1)}, bf16[2,224,256]{2,1,0:T(8,128)(2,1)S(1)}, u32[]{:S(2)}, u32[]{:S(2)}) collective-permute-start(bf16[2,224,256]{2,1,0:T(8,128)(2,1)S(1)} %shard_map.70.chip_ref), channel_id=1, source_target_pairs={{0,2},{1,3},{2,0},{3,1},{4,6},{5,7},{6,4},{7,5},{8,10},{9,11},{10,... | collective-permute-start | bytes 688136 | tf_op jit(solution)/shard_map/ppermute | solution.py:334
  53.5 4.8 %shard_map.71 = (bf16[2,224,256]{2,1,0:T(8,128)(2,1)S(1)}, f32[2,224,256]{2,1,0:T(8,128)S(1)}) custom-call(s32[4]{0:T(128)S(1)} %copy-done.4, f32[48,128]{1,0:T(8,128)S(1)} %get-tuple-element.18.table_ref, bf16[2,448,512]{2,1,0:T(8,128)(2,1)S(1)} %get-tuple-element.22.coef_ref, bf16[2,512,768]{2,1,0:T(8,128)(2,1)S(1)} %get-tuple-element.24.slab_ref, ...), custom_call_target="tpu_custom_call" | custom-call | flops 2200000000 | bytes 4000000 | tf_op jit(solution)/shard_map/pallas_call | solution.py:347
  58.3 1.4 %collective-permute-done.1.a_ref = bf16[2,224,256]{2,1,0:T(8,128)(2,1)S(1)} collective-permute-done((bf16[2,224,256]{2,1,0:T(8,128)(2,1)S(1)}, bf16[2,224,256]{2,1,0:T(8,128)(2,1)S(1)}, u32[]{:S(2)}, u32[]{:S(2)}) %collective-permute-start.1) | collective-permute-done | bytes 229408 | tf_op jit(solution)/shard_map/ppermute | solution.py:334
  59.7 0.8 %collective-permute-start.2 = (bf16[2,224,256]{2,1,0:T(8,128)(2,1)S(1)}, bf16[2,224,256]{2,1,0:T(8,128)(2,1)S(1)}, u32[]{:S(2)}, u32[]{:S(2)}) collective-permute-start(bf16[2,224,256]{2,1,0:T(8,128)(2,1)S(1)} %get-tuple-element.30), channel_id=1, source_target_pairs={{0,1},{1,0},{2,3},{3,2},{4,5},{5,4},{6,7},{7,6},{8,9},{9,8},{10,11... | collective-permute-start | bytes 688136 | tf_op jit(solution)/shard_map/ppermute | solution.py:334
  60.5 1.1 %collective-permute-done.2.b_ref = bf16[2,224,256]{2,1,0:T(8,128)(2,1)S(1)} collective-permute-done((bf16[2,224,256]{2,1,0:T(8,128)(2,1)S(1)}, bf16[2,224,256]{2,1,0:T(8,128)(2,1)S(1)}, u32[]{:S(2)}, u32[]{:S(2)}) %collective-permute-start.2) | collective-permute-done | bytes 229408 | tf_op jit(solution)/shard_map/ppermute | solution.py:334
  61.6 1.3 %shard_map.72 = f32[2,4,2,7,32,32]{5,4,3,2,1,0:T(8,128)} custom-call(f32[2,224,256]{2,1,0:T(8,128)S(1)} %get-tuple-element.27.own_ref, bf16[2,224,256]{2,1,0:T(8,128)(2,1)S(1)} %collective-permute-done.1.a_ref, bf16[2,224,256]{2,1,0:T(8,128)(2,1)S(1)} %collective-permute-done.2.b_ref), custom_call_target="tpu_custom_call" | custom-call | flops 1000000 | bytes 3000000 | tf_op jit(solution)/shard_map/pallas_call | solution.py:358
  (3 shorter events, 0.1 us)
Async XLA Ops:
  0.0 0.8 %copy-start.1 = (bf16[64,1,2,256]{3,2,1,0:T(2,128)(2,1)S(1)}, bf16[64,1,2,256]{3,2,1,0:T(2,128)(2,1)}, u32[]{:S(2)}) copy-start(bf16[64,1,2,256]{3,2,1,0:T(2,128)(2,1)} %param.6) | copy-start | bytes 196612
  0.8 0.7 %copy-start.2 = (s32[4096]{0:T(1024)S(1)}, s32[4096]{0:T(1024)}, u32[]{:S(2)}) copy-start(s32[4096]{0:T(1024)} %param.8) | copy-start | bytes 49156
  1.6 0.7 %copy-start.6 = (s32[64,1]{0,1:T(1,128)S(1)}, s32[64,1]{0,1:T(1,128)}, u32[]{:S(2)}) copy-start(s32[64,1]{0,1:T(1,128)} %param.7) | copy-start | bytes 772
  3.3 19.4 %all-to-all-start = ((bf16[8,32,512]{2,1,0:T(8,128)(2,1)}), bf16[8,32,512]{2,1,0:T(8,128)(2,1)S(1)}, u32[]{:S(2)}, u32[]{:S(2)}) async-start(bf16[8,32,512]{2,1,0:T(8,128)(2,1)} %bitcast.6), calls=%async_computation | async-start | bytes 524288 | tf_op jit(solution)/shard_map/all_to_all | solution.py:288
  12.3 2.8 %copy-start = (bf16[2,2,256,3072]{3,2,1,0:T(8,128)(2,1)S(1)}, bf16[2,2,256,3072]{3,2,1,0:T(8,128)(2,1)}, u32[]{:S(2)}) copy-start(bf16[2,2,256,3072]{3,2,1,0:T(8,128)(2,1)} %param.9) | copy-start | bytes 18874372
  20.4 8.6 %copy-start.3 = (s32[4096]{0:T(1024)S(1)}, s32[4096]{0:T(1024)}, u32[]{:S(2)}) copy-start(s32[4096]{0:T(1024)} %param.8) | copy-start | bytes 49156
  20.5 8.8 %copy-start.4 = (s32[4]{0:T(128)S(1)}, s32[4]{0:T(128)}, u32[]{:S(2)}) copy-start(s32[4]{0:T(128)} %gammas_ref.7) | copy-start | bytes 52
  20.5 8.8 %copy-start.5 = (s32[4,3]{1,0:T(4,128)S(1)}, s32[4,3]{1,0:T(4,128)}, u32[]{:S(2)}) copy-start(s32[4,3]{1,0:T(4,128)} %momenta_ref.1) | copy-start | bytes 148
  23.9 14.7 %all-to-all-start.1 = ((bf16[8,112,512]{2,1,0:T(8,128)(2,1)}), bf16[8,112,512]{2,1,0:T(8,128)(2,1)S(1)}, u32[]{:S(2)}, u32[]{:S(2)}) async-start(bf16[8,112,512]{2,1,0:T(8,128)(2,1)} %shard_map.67), calls=%async_computation.1 | async-start | bytes 1835008 | tf_op jit(solution)/shard_map/all_to_all | solution.py:319
  42.7 8.2 %collective-permute-start = (bf16[2,224,256]{2,1,0:T(8,128)(2,1)S(1)}, bf16[2,224,256]{2,1,0:T(8,128)(2,1)S(1)}, u32[]{:S(2)}, u32[]{:S(2)}) collective-permute-start(bf16[2,224,256]{2,1,0:T(8,128)(2,1)S(1)} %get-tuple-element.26), channel_id=1, source_target_pairs={{0,1},{1,0},{2,3},{3,2},{4,5},{5,4},{6,7},{7,6},{8,9},{9,8},{10,11... | collective-permute-start | bytes 688136 | tf_op jit(solution)/shard_map/ppermute | solution.py:334
  50.9 8.8 %collective-permute-start.1 = (bf16[2,224,256]{2,1,0:T(8,128)(2,1)S(1)}, bf16[2,224,256]{2,1,0:T(8,128)(2,1)S(1)}, u32[]{:S(2)}, u32[]{:S(2)}) collective-permute-start(bf16[2,224,256]{2,1,0:T(8,128)(2,1)S(1)} %shard_map.70.chip_ref), channel_id=1, source_target_pairs={{0,2},{1,3},{2,0},{3,1},{4,6},{5,7},{6,4},{7,5},{8,10},{9,11},{10,... | collective-permute-start | bytes 688136 | tf_op jit(solution)/shard_map/ppermute | solution.py:334
  59.7 1.9 %collective-permute-start.2 = (bf16[2,224,256]{2,1,0:T(8,128)(2,1)S(1)}, bf16[2,224,256]{2,1,0:T(8,128)(2,1)S(1)}, u32[]{:S(2)}, u32[]{:S(2)}) collective-permute-start(bf16[2,224,256]{2,1,0:T(8,128)(2,1)S(1)} %get-tuple-element.30), channel_id=1, source_target_pairs={{0,1},{1,0},{2,3},{3,2},{4,5},{5,4},{6,7},{7,6},{8,9},{9,8},{10,11... | collective-permute-start | bytes 688136 | tf_op jit(solution)/shard_map/ppermute | solution.py:334

commit v2 on v1

v2 whole, which is shorter than its diff:
```python
import functools
import math

import jax
import jax.numpy as jnp
from jax import lax
from jax.experimental import pallas as pl
from jax.experimental.pallas import tpu as pltpu
from jax.sharding import PartitionSpec as P

LAT = 64
STOPW = 7
PLANES = 8
SPOTS = 8
ITEMS = 64
WIDTH = 256
MODES = 32
ROWS = STOPW * MODES
COLS = 768
OPS = 4
CAND = 128
SPARE = 4
Z_GROUPS = [[z * SPOTS + p for z in range(PLANES)] for p in range(SPOTS)]
P_GROUPS = [[z * SPOTS + p for p in range(SPOTS)] for z in range(PLANES)]
PAIRS = [(0, 1), (3, 4), (6, 7), (9, 10), (2, 5), (8, 11)]
BF16 = jnp.bfloat16
F32 = jnp.float32


def iota(shape, axis):
    return lax.broadcasted_iota(jnp.int32, shape, axis)


def pack_kernel(route_ref, coefs_ref, counts_ref, out_ref):
    me = lax.axis_index("mode")
    row = route_ref[pl.ds(me // 2, 1), :]
    row = jnp.where(me % 2 == 1, pltpu.roll(row, 64, 1), row)[:, :ITEMS]
    owner = lax.shift_right_logical(row, 6)
    i = iota((ITEMS, ITEMS), 0)
    j = iota((ITEMS, ITEMS), 1)
    owners = jnp.broadcast_to(owner, (ITEMS, ITEMS)).astype(F32)
    column = jnp.sum(jnp.where(i == j, owners, 0.0), axis=1, keepdims=True)
    earlier = jnp.where((owners == column) & (i < j), 1.0, 0.0)
    rank = jnp.max(earlier, axis=0, keepdims=True).astype(jnp.int32)
    target = owner * 2 + rank
    q = iota((PLANES * 32, ITEMS), 0)
    plane = (lax.shift_right_logical(q, 5) - (lax.shift_right_logical(q, 4) & 1)) & 7
    want = plane * 16 + (q & 15)
    outgoing = jnp.where(want == target, 1.0, 0.0).astype(BF16)
    counts = jnp.broadcast_to(counts_ref[...], (ITEMS, ITEMS)).astype(F32)
    limit = jnp.sum(jnp.where(i == j, counts, 0.0), axis=1, keepdims=True).astype(jnp.int32)
    keep = iota((ITEMS, WIDTH), 1) < limit
    for part in range(2):
        block = jnp.where(keep, coefs_ref[:, part, :].astype(F32), 0.0).astype(BF16)
        packed = jnp.dot(outgoing, block, preferred_element_type=F32)
        out_ref[:, part * WIDTH : (part + 1) * WIDTH] = packed.astype(BF16)


def forward_kernel(got_ref, done_ref, table_ref, out_ref, sorted_ref, sems):
    n = (SPOTS + STOPW - 1) * 16
    row = iota((n, PLANES * 32), 0)
    col = iota((n, PLANES * 32), 1)
    block = (SPOTS - 1 - lax.shift_right_logical(row, 4)) & 15
    source = (lax.shift_right_logical(row, 1) & 7) * 32 + block * 2 + (row & 1)
    order = jnp.where(col == source, 1.0, 0.0).astype(BF16)
    sorted_ref[...] = jnp.dot(order, got_ref[...], preferred_element_type=F32).astype(BF16)
    copies = []
    for spot in range(SPOTS):
        at = (SPOTS - 1 - spot) * 16
        copies.append(pltpu.make_async_copy(sorted_ref.at[at : at + STOPW * 16], out_ref.at[spot], sems.at[spot]))
    for copy in copies:
        copy.start()
    for copy in copies:
        copy.wait()


def tables_kernel(momenta_ref, gammas_ref, route_ref, placer_ref, table_ref):
    me = lax.axis_index("mode")
    route = route_ref[...]
    owner = lax.shift_right_logical(route, 6)
    key = iota(route.shape, 0) * ITEMS + (route & (ITEMS - 1))
    keyf = key.astype(F32)
    second = (iota((1, CAND), 1) & 1) == 1
    mode = iota((MODES, CAND), 0)
    for stop in range(STOPW):
        hit = owner == ((me - stop) & 63)
        low = jnp.min(jnp.where(hit, keyf, 8192.0), axis=0, keepdims=True)
        high = jnp.max(jnp.where(hit, keyf, -1.0), axis=0, keepdims=True)
        valid = jnp.where(second, high - low, 8000.0 - low) > 0.0
        item = jnp.where(second, high, low).astype(jnp.int32) & (ITEMS - 1)
        item = jnp.where(valid, item, -1)
        for block in range(2):
            placer_ref[block, stop] = jnp.where(mode * 2 + block == item, 1.0, 0.0).astype(BF16)
    place = lax.axis_index("space")
    lane = iota((1, 128), 1)
    site = place * 64 + (lane & 63)
    xs = site & 3
    ys = lax.shift_right_logical(site, 2) & 3
    zs = lax.shift_right_logical(site, 4)
    for op in range(OPS):
        inner = momenta_ref[op, 0] * xs + momenta_ref[op, 1] * ys + momenta_ref[op, 2] * zs
        turn = inner.astype(F32) * (2.0 * math.pi / LAT)
        cosine = jnp.cos(turn)
        sine = jnp.sin(turn)
        bits = lax.shift_right_logical(gammas_ref[op], 2)
        for group in range(6):
            spin = jnp.full((1, 128), group, jnp.int32) if group < 4 else 2 * (group - 4) + lax.shift_right_logical(lane, 6)
            common = spin & bits
            parity = (common ^ lax.shift_right_logical(common, 1)) & 1
            sign = (1 - 2 * parity).astype(F32)
            at = (op * 6 + group) * 2
            table_ref[at : at + 1, :] = cosine * sign
            table_ref[at + 1 : at + 2, :] = sine * sign


def sort_kernel(basis_ref, out_ref, done_ref, reads_ref, slots_ref, in_sems, sems):
    done_ref[...] = jnp.zeros(done_ref.shape, F32)
    step = 64
    chunks = 2 * WIDTH // step
    low = iota((step, 128), 1) < 64

    def take(chunk, slot):
        rows = pl.ds(pl.multiple_of(chunk * step, step), step)
        return pltpu.make_async_copy(basis_ref.at[:, rows, :], reads_ref.at[slot], in_sems.at[slot])

    def leave(chunk, slot):
        rows = pl.ds(pl.multiple_of(chunk * step, step), step)
        return pltpu.make_async_copy(slots_ref.at[slot], out_ref.at[0:2, :, rows, :], sems.at[slot])

    for slot in range(2):
        take(slot, slot).start()

    @pl.loop(0, chunks // 2)
    def _(turn):
        for slot in range(2):
            chunk = turn * 2 + slot
            take(chunk, slot).wait()

            @pl.when(turn > 0)
            def _():
                leave(chunk - 2, slot).wait()

            for block in range(2):
                for group, (first, second) in enumerate(PAIRS):
                    lanes = slice(group * 128, (group + 1) * 128)
                    for pair in range(2):
                        at = pair * 128
                        a = reads_ref[slot, block, :, first * 256 + at : first * 256 + at + 128]
                        b = reads_ref[slot, block, :, second * 256 + at : second * 256 + at + 128]
                        slots_ref[slot, block, 2 * pair, :, lanes] = jnp.where(low, a, pltpu.roll(b, 64, 1))
                        slots_ref[slot, block, 2 * pair + 1, :, lanes] = jnp.where(low, pltpu.roll(a, 64, 1), b)
            leave(chunk, slot).start()

            @pl.when(turn < chunks // 2 - 1)
            def _():
                take(chunk + 2, slot).start()

    for slot in range(2):
        leave(chunks - 2 + slot, slot).wait()


def block_of(mask):
    return lax.shift_right_logical(lax.axis_index("space") ^ mask, 1)


def fetch(sorted_ref, slab_ref, sem, mask, t):
    target = lax.axis_index("space") ^ mask
    return pltpu.make_async_copy(sorted_ref.at[block_of(mask), 2 * (target & 1) + t], slab_ref, sem)


def place(block, got_ref, placer_ref, coef_ref):
    for stop in range(STOPW):
        rows = got_ref[:, stop * 16 : (stop + 1) * 16, :].reshape(CAND, 2 * WIDTH)
        coef = jnp.dot(placer_ref[block, stop], rows, preferred_element_type=F32)
        re = coef[:, :WIDTH]
        im = coef[:, WIDTH:]
        top = slice(stop * MODES, (stop + 1) * MODES)
        bottom = slice(ROWS + stop * MODES, ROWS + (stop + 1) * MODES)
        coef_ref[top, :WIDTH] = re.astype(BF16)
        coef_ref[top, WIDTH:] = (-im).astype(BF16)
        coef_ref[bottom, :WIDTH] = im.astype(BF16)
        coef_ref[bottom, WIDTH:] = re.astype(BF16)


def entries(gammas_ref, table_ref, coef_ref, slab_ref, vec_ref, weight_ref):
    vec = jnp.dot(coef_ref[...], slab_ref[...], preferred_element_type=F32).astype(BF16)
    vec_ref[:, :COLS] = vec[:ROWS]
    vec_ref[:, COLS:] = vec[ROWS:]
    for op in range(OPS):
        flip = gammas_ref[op] & 3
        for group in range(6):
            if group < 4:
                source = group ^ flip
            else:
                source = 4 + ((group - 4) ^ lax.shift_right_logical(flip, 1))
            start = pl.multiple_of(source * 128, 128)
            re = vec_ref[0:MODES, pl.ds(start, 128)].astype(F32)
            im = vec_ref[0:MODES, pl.ds(start + COLS, 128)].astype(F32)
            if group >= 4:
                swap = (flip & 1) == 1
                re = jnp.where(swap, pltpu.roll(re, 64, 1), re)
                im = jnp.where(swap, pltpu.roll(im, 64, 1), im)
            at = (op * 6 + group) * 2
            cosine = table_ref[at : at + 1, :]
            sine = table_ref[at + 1 : at + 2, :]
            w_re = cosine * re - sine * im
            w_im = sine * re + cosine * im
            real = slice(op * MODES, (op + 1) * MODES)
            imag = slice(128 + op * MODES, 128 + (op + 1) * MODES)
            left = slice(group * 128, (group + 1) * 128)
            right = slice(COLS + group * 128, COLS + (group + 1) * 128)
            weight_ref[real, left] = w_re.astype(BF16)
            weight_ref[real, right] = w_im.astype(BF16)
            weight_ref[imag, left] = (-w_im).astype(BF16)
            weight_ref[imag, right] = w_re.astype(BF16)
    return lax.dot_general(vec_ref[...], weight_ref[...], (((1,), (1,)), ((), ())), preferred_element_type=F32)


def first_kernel(now, after, gammas_ref, table_ref, got_ref, placer_ref, sorted_ref, out_ref, coef_ref, next_ref, slab_ref, vec_ref, weight_ref, sems):
    slab = fetch(sorted_ref, slab_ref, sems.at[0], *now)
    later = fetch(sorted_ref, next_ref, sems.at[1], *after)
    slab.start()
    later.start()
    place(block_of(now[0]), got_ref, placer_ref, coef_ref)
    slab.wait()
    out_ref[...] = entries(gammas_ref, table_ref, coef_ref, slab_ref, vec_ref, weight_ref).astype(BF16)
    later.wait()


def middle_kernel(after, gammas_ref, table_ref, coef_ref, slab_ref, sorted_ref, *rest):
    out_ref, next_ref, vec_ref, weight_ref, sem = rest[-5:]
    later = fetch(sorted_ref, next_ref, sem, *after)
    later.start()
    total = entries(gammas_ref, table_ref, coef_ref, slab_ref, vec_ref, weight_ref)
    if len(rest) > 5:
        total = total + rest[0][...].astype(F32)
    out_ref[...] = total.astype(BF16)
    later.wait()


def last_kernel(steps, gammas_ref, table_ref, got_ref, placer_ref, slab_ref, sorted_ref, before_ref, part_a_ref, part_b_ref, own_ref, coef_ref, slabs_ref, vec_ref, weight_ref, sems):
    place(block_of(0), got_ref, placer_ref, coef_ref)
    copies = [None] + [
        fetch(sorted_ref, slabs_ref.at[n % 2], sems.at[n % 2], *step) for n, step in enumerate(steps) if n > 0
    ]
    copies[1].start()
    for n, (mask, t) in enumerate(steps):
        if n > 0:
            copies[n].wait()
        if 0 < n < len(steps) - 1:
            copies[n + 1].start()
        slab = slab_ref if n == 0 else slabs_ref.at[n % 2]
        total = entries(gammas_ref, table_ref, coef_ref, slab, vec_ref.at[n % 2], weight_ref.at[n % 2])
        if mask == 1:
            (part_a_ref, part_b_ref)[t][...] = total.astype(BF16)
        else:
            own_ref[t] = total


def total_kernel(own_ref, near_a_ref, near_b_ref, far_a_ref, far_b_ref, out_ref, total_ref, sems):
    copies = []
    for t, (near_ref, far_ref) in enumerate(((near_a_ref, far_a_ref), (near_b_ref, far_b_ref))):
        total = own_ref[t] + near_ref[...].astype(F32) + far_ref[...].astype(F32)
        for op in range(OPS):
            for r in range(2):
                at = (r * OPS + op) * MODES
                total_ref[t, op, r] = total[:, at : at + MODES].reshape(STOPW, MODES, MODES)
            copy = pltpu.make_async_copy(total_ref.at[t, op], out_ref.at[t, op], sems.at[t, op])
            copy.start()
            copies.append(copy)
    for copy in copies:
        copy.wait()


VMEM = pl.BlockSpec(memory_space=pltpu.VMEM)
SMEM = pl.BlockSpec(memory_space=pltpu.SMEM)
HBM = pl.BlockSpec(memory_space=pltpu.HBM)
DMA = pltpu.SemaphoreType.DMA


def kernel_call(kernel, out_shape, in_specs, flops, moved, scratch=(), limit=8, out_specs=None):
    many = isinstance(out_shape, tuple)
    return pl.pallas_call(
        kernel,
        out_shape=out_shape,
        in_specs=in_specs,
        out_specs=out_specs or ((VMEM,) * len(out_shape) if many else VMEM),
        scratch_shapes=list(scratch),
        compiler_params=pltpu.CompilerParams(vmem_limit_bytes=limit * 1024 * 1024),
        cost_estimate=pl.CostEstimate(flops=flops, bytes_accessed=moved, transcendentals=0),
    )


def shape(dims, dtype=BF16):
    return jax.ShapeDtypeStruct(dims, dtype)


def per_device(coefs, counts, route, basis, momenta, gammas):
    packed = kernel_call(
        pack_kernel, shape((PLANES * 32, 2 * WIDTH)), [VMEM] * 3, 20_000_000, 400_000, limit=60
    )(route.reshape(32, 128), coefs.reshape(ITEMS, 2, WIDTH), counts.reshape(1, ITEMS))
    first = lax.all_to_all(
        packed.reshape(PLANES, 32, 2 * WIDTH), "mode", 0, 0, tiled=True, axis_index_groups=Z_GROUPS
    )
    by_reader = route.reshape(PLANES, SPOTS, ITEMS).transpose(2, 1, 0).reshape(ITEMS, 64)
    by_reader = jnp.repeat(by_reader, 2, axis=1)
    placer, table = kernel_call(
        tables_kernel,
        (shape((2, STOPW, MODES, CAND)), shape((OPS * 12, 128), F32)),
        [SMEM, SMEM, VMEM],
        2_000_000,
        200_000,
    )(momenta, gammas, by_reader)
    sorted_basis, done = kernel_call(
        sort_kernel,
        (shape((SPARE * 2, 4, 2 * WIDTH, COLS)), shape((8, 128), F32)),
        [HBM],
        10_000_000,
        13_000_000,
        [
            pltpu.VMEM((2, 2, 64, 4 * COLS), BF16),
            pltpu.VMEM((2, 2, 4, 64, COLS), BF16),
            DMA((2,)),
            DMA((2,)),
        ],
        limit=60,
        out_specs=(HBM, VMEM),
    )(basis.reshape(2, 2 * WIDTH, 4 * COLS))
    onward = kernel_call(
        forward_kernel,
        shape((SPOTS, STOPW * 16, 2 * WIDTH)),
        [VMEM, VMEM, VMEM],
        70_000_000,
        1_200_000,
        [pltpu.VMEM(((SPOTS + STOPW - 1) * 16, 2 * WIDTH), BF16), DMA((SPOTS,))],
        out_specs=HBM,
    )(first.reshape(PLANES * 32, 2 * WIDTH), done, table)
    got = lax.all_to_all(onward, "mode", 0, 0, tiled=True, axis_index_groups=P_GROUPS)
    part_shape = shape((ROWS, 256))
    slab_shape = shape((2 * WIDTH, COLS))
    vec_shape = (ROWS, 2 * COLS)
    weight_shape = (256, 2 * COLS)
    work = [pltpu.VMEM(vec_shape, BF16), pltpu.VMEM(weight_shape, BF16)]

    def between(pair, part):
        return lax.ppermute(part, "space", [(i, i ^ pair) for i in range(4)])

    def middle(slab, after, *extra):
        return kernel_call(
            functools.partial(middle_kernel, after),
            (part_shape, slab_shape),
            [SMEM, VMEM, VMEM, VMEM, HBM] + [VMEM] * len(extra),
            550_000_000,
            2_000_000,
            work + [DMA],
            limit=44,
        )(gammas, table, coef, slab, sorted_basis, *extra)

    other_a, coef, slab = kernel_call(
        functools.partial(first_kernel, (3, 0), (3, 1)),
        (part_shape, shape((2 * ROWS, 2 * WIDTH)), slab_shape),
        [SMEM, VMEM, VMEM, VMEM, HBM],
        600_000_000,
        3_000_000,
        [pltpu.VMEM((2 * WIDTH, COLS), BF16)] + work + [DMA((2,))],
        limit=44,
    )(gammas, table, got, placer, sorted_basis)
    other_b, slab = middle(slab, (2, 0))
    chip_a, slab = middle(slab, (2, 1), between(1, other_a))
    far_a = between(2, chip_a)
    chip_b, slab = middle(slab, (1, 0), between(1, other_b))
    far_b = between(2, chip_b)
    part_a, part_b, own = kernel_call(
        functools.partial(last_kernel, ((1, 0), (1, 1), (0, 0), (0, 1))),
        (part_shape, part_shape, shape((2, ROWS, 256), F32)),
        [SMEM, VMEM, VMEM, VMEM, VMEM, HBM, VMEM],
        2_200_000_000,
        6_000_000,
        [
            pltpu.VMEM((2 * ROWS, 2 * WIDTH), BF16),
            pltpu.VMEM((2, 2 * WIDTH, COLS), BF16),
            pltpu.VMEM((2, *vec_shape), BF16),
            pltpu.VMEM((2, *weight_shape), BF16),
            DMA((2,)),
        ],
        limit=44,
    )(gammas, table, got, placer, slab, sorted_basis, chip_b)
    part_a, part_b, far_a = lax.optimization_barrier((part_a, part_b, far_a))
    near_a = between(1, part_a)
    near_b = between(1, part_b)
    return kernel_call(
        total_kernel,
        shape((2, OPS, 2, STOPW, MODES, MODES), F32),
        [VMEM] * 5,
        1_000_000,
        3_000_000,
        [pltpu.VMEM((2, OPS, 2, STOPW, MODES, MODES), F32), DMA((2, OPS))],
        out_specs=HBM,
    )(own, near_a, near_b, far_a, far_b)


def solution(mesh):
    in_specs = (
        P("mode", "space", None, None),
        P("mode", "space"),
        P(),
        P("space", None, None, None),
        P(),
        P(),
    )
    out_specs = P("space", None, None, None, None, "mode")
    return jax.shard_map(
        per_device, mesh=mesh, in_specs=in_specs, out_specs=out_specs, check_vma=False
    )
```

time: 63.4 us -> 70.3 us (1.11)
  blocking collectives: 0 us -> 17.1 us
  waiting for transfers between devices: 13.4 us -> 1.23 us
  Pallas kernels: 21.8 us -> 31.7 us
  starting transfers between devices: 22.5 us -> 16.5 us
  local copies, waits for them, and re-layouts: 5.19 us -> 2.9 us
    all_to_all x0 -> x1, blocking collectives: none -> 17.1 us  [per_device(): lax.all_to_all(onward, 'mode', 0, 0, tiled=True, axis_index_groups=P_GROUPS)]
    all_to_all x1 -> x0, waiting for transfers between devices: 8.59 us -> none  [per_device(): lax.all_to_all(onward, 'mode', 0, 0, tiled=True, axis_index_groups=P_GROUPS)]
    pallas_call x5 -> x6, Pallas kernels: 12.9 us -> 18.3 us  [the longest x3 7.9 us: middle(): kernel_call(functools.partial(middle_kernel, after), (part_shape, slab_sh...]
    all_to_all x1 -> x0, starting transfers between devices: 5.13 us -> none  [per_device(): lax.all_to_all(onward, 'mode', 0, 0, tiled=True, axis_index_groups=P_GROUPS)]
    pallas_call x1, Pallas kernels: 5.32 us -> 8.56 us  [per_device(): kernel_call(sort_kernel, (shape((SPARE * 2, 4, 2 * WIDTH, COLS)), shape((...]
    unnamed x14 -> x8, local copies, waits for them, and re-layouts: 5.02 us -> 2.02 us
    all_to_all x1, waiting for transfers between devices: 2.22 us -> 0.01 us  [per_device(): lax.all_to_all(packed.reshape(PLANES, 32, 2 * WIDTH), 'mode', 0, 0, tiled...]
    ppermute x3 -> x6, waiting for transfers between devices: 2.55 us -> 1.23 us  [between(): return lax.ppermute(part, 'space', [(i, i ^ pair) for i in range(4)])]
  transfers between devices with their start and end apart: 5 -> 7, of which waited for: 4 -> 2; matrix products, arithmetic and copies ran while one was open for 0% -> 1% of each run, Pallas kernels for 22% -> 30%
where the time goes in v2:
time: 70.3 us; the launch traced here: 69.6 us
  Pallas kernels  31.7 us (45%)
  blocking collectives  17.1 us (24%)
  starting transfers between devices  16.5 us (23%)
  local copies, waits for them, and re-layouts  2.9 us (4%)
  waiting for transfers between devices  1.23 us (2%)
    all_to_all x1, blocking collectives, per_device(): lax.all_to_all(onward, 'mode', 0, 0, tiled=True, axis_index_groups=P_GROUPS)  17.1 us
    all_to_all x1, starting transfers between devices, per_device(): lax.all_to_all(packed.reshape(PLANES, 32, 2 * WIDTH), 'mode', 0, 0, tiled...  9.01 us
    pallas_call x1, Pallas kernels, per_device(): kernel_call(sort_kernel, (shape((SPARE * 2, 4, 2 * WIDTH, COLS)), shape((...  8.56 us
    pallas_call x3, Pallas kernels, middle(): kernel_call(functools.partial(middle_kernel, after), (part_shape, slab_sh...  7.9 us
    ppermute x6, starting transfers between devices, between(): return lax.ppermute(part, 'space', [(i, i ^ pair) for i in range(4)])  7.53 us
    pallas_call x1, Pallas kernels, per_device(): kernel_call(functools.partial(last_kernel, ((1, 0), (1, 1), (0, 0), (0, 1...  6.61 us
    pallas_call x1, Pallas kernels, per_device(): kernel_call(functools.partial(first_kernel, (3, 0), (3, 1)), (part_shape,...  3.09 us
    unnamed x8, local copies, waits for them, and re-layouts  2.02 us
  transfers between devices with their start and end apart: 7, of which 2 were waited for; matrix products, arithmetic and copies ran while one was open for 1% of the time, Pallas kernels for 30%

profile of v2, /device:TPU:1, one launch (start us, length us, event | category | flops | bytes accessed | tf_op | source)
XLA Modules:
  0.0 69.6 jit_solution(14979440071386275448)
XLA Ops:
  0.0 0.0 copy-start.1
  0.0 1.9 %shard_map.65 = bf16[256,512]{1,0:T(8,128)(2,1)} custom-call(s32[32,128]{1,0:T(8,128)} %bitcast.18, bf16[64,2,256]{2,1,0:T(2,128)(2,1)} %bitcast.17, s32[1,64]{1,0:T(1,128)} %bitcast.19), custom_call_target="tpu_custom_call" | custom-call | flops 20000000 | bytes 400000 | tf_op jit(solution)/shard_map/pallas_call | solution.py:299
  1.9 9.0 %all-to-all-start = ((bf16[8,32,512]{2,1,0:T(8,128)(2,1)}), bf16[8,32,512]{2,1,0:T(8,128)(2,1)S(1)}, u32[]{:S(2)}, u32[]{:S(2)}) async-start(bf16[8,32,512]{2,1,0:T(8,128)(2,1)} %bitcast.13), calls=%async_computation | async-start | bytes 524288 | tf_op jit(solution)/shard_map/all_to_all | solution.py:302
  11.0 0.8 %reshape.27 = s32[8,8,64]{2,1,0:T(8,128)S(1)} reshape(s32[4096]{0:T(1024)} %param.8) | data formatting | bytes 32768 | tf_op jit(solution)/shard_map/reshape | solution.py:305
  11.8 0.1 copy.8.route_ref
  11.9 0.0 copy-start
  11.9 0.7 copy-done
  12.5 0.0 copy-start.3
  12.5 0.7 copy-done.3
  13.2 0.8 %shard_map.64 = (bf16[2,7,32,128]{3,2,1,0:T(8,128)(2,1)S(1)}, f32[48,128]{1,0:T(8,128)S(1)}) custom-call(s32[4,3]{1,0:T(4,128)S(1)} %copy-done.3, s32[4]{0:T(128)S(1)} %copy-done, s32[64,128]{1,0:T(8,128)S(1)} %copy.8.route_ref), custom_call_target="tpu_custom_call" | custom-call | flops 2000000 | bytes 200000 | tf_op jit(solution)/shard_map/pallas_call | solution.py:307
  14.0 8.6 %shard_map.66 = (bf16[8,4,512,768]{3,2,1,0:T(8,128)(2,1)}, f32[8,128]{1,0:T(8,128)}) custom-call(bf16[2,512,3072]{2,1,0:T(8,128)(2,1)} %bitcast.12), custom_call_target="tpu_custom_call" | custom-call | flops 10000000 | bytes 13000000 | tf_op jit(solution)/shard_map/pallas_call | solution.py:314
  22.5 0.0 all-to-all-done
  22.6 0.0 copy-start.2
  22.6 0.7 copy-done.2
  23.2 1.5 %shard_map.67 = bf16[8,112,512]{2,1,0:T(8,128)(2,1)S(1)} custom-call(bf16[256,512]{1,0:T(8,128)(2,1)S(1)} %bitcast.11, f32[8,128]{1,0:T(8,128)S(1)} %copy-done.2, f32[48,128]{1,0:T(8,128)S(1)} %get-tuple-element.24.table_ref), custom_call_target="tpu_custom_call" | custom-call | flops 70000000 | bytes 1200000 | tf_op jit(solution)/shard_map/pallas_call | solution.py:329
  24.7 17.1 %all_to_all.10.got_ref = bf16[8,112,512]{2,1,0:T(8,128)(2,1)S(1)} all-to-all(bf16[8,112,512]{2,1,0:T(8,128)(2,1)S(1)} %shard_map.67), channel_id=1, replica_groups={{0,4,8,12,16,20,24,28},{32,36,40,44,48,52,56,60},{64,68,72,76,80,84,88,..., dimensions={0} | all-to-all | bytes 1835008 | tf_op jit(solution)/shard_map/all_to_all | solution.py:338
  41.8 0.0 copy-done.1
  41.8 3.1 %shard_map.68 = (bf16[224,256]{1,0:T(8,128)(2,1)S(1)}, bf16[448,512]{1,0:T(8,128)(2,1)S(1)}, bf16[512,768]{1,0:T(8,128)(2,1)S(1)}) custom-call(s32[4]{0:T(128)S(1)} %copy-done.1, f32[48,128]{1,0:T(8,128)S(1)} %get-tuple-element.24.table_ref, bf16[8,112,512]{2,1,0:T(8,128)(2,1)S(1)} %all_to_all.10.got_ref, ...), custom_call_target="tpu_custom_call" | custom-call | flops 600000000 | bytes 3000000 | tf_op jit(solution)/shard_map/pallas_call | solution.py:359
  44.9 3.1 %collective-permute-start = (bf16[224,256]{1,0:T(8,128)(2,1)S(1)}, bf16[224,256]{1,0:T(8,128)(2,1)S(1)}, u32[]{:S(2)}, u32[]{:S(2)}) collective-permute-start(bf16[224,256]{1,0:T(8,128)(2,1)S(1)} %get-tuple-element.31), channel_id=1, source_target_pairs={{0,1},{1,0},{2,3},{3,2},{4,5},{5,4},{6,7},{7,6},{8,9},{9,8},{10,11... | collective-permute-start | bytes 344072 | tf_op jit(solution)/shard_map/ppermute | solution.py:346
  48.1 2.6 %shard_map.69 = (bf16[224,256]{1,0:T(8,128)(2,1)S(1)}, bf16[512,768]{1,0:T(8,128)(2,1)S(1)}) custom-call(s32[4]{0:T(128)S(1)} %copy-done.1, f32[48,128]{1,0:T(8,128)S(1)} %get-tuple-element.24.table_ref, bf16[448,512]{1,0:T(8,128)(2,1)S(1)} %get-tuple-element.28.coef_ref, bf16[512,768]{1,0:T(8,128)(2,1)S(1)} %get-tuple-element.29.slab_ref, ...), custom_call_target="tpu_custom_call" | custom-call | flops 550000000 | bytes 2000000 | tf_op jit(solution)/shard_map/pallas_call | solution.py:349
  50.7 0.1 collective-permute-start.1
  50.8 0.0 collective-permute-done.rest_0_
  50.8 2.6 %shard_map.70 = (bf16[224,256]{1,0:T(8,128)(2,1)S(1)}, bf16[512,768]{1,0:T(8,128)(2,1)S(1)}) custom-call(s32[4]{0:T(128)S(1)} %copy-done.1, f32[48,128]{1,0:T(8,128)S(1)} %get-tuple-element.24.table_ref, bf16[448,512]{1,0:T(8,128)(2,1)S(1)} %get-tuple-element.28.coef_ref, bf16[512,768]{1,0:T(8,128)(2,1)S(1)} %get-tuple-element.30.slab_ref, ...), custom_call_target="tpu_custom_call" | custom-call | flops 550000000 | bytes 2000000 | tf_op jit(solution)/shard_map/pallas_call | solution.py:349
  53.5 0.0 collective-permute-done.1.rest_0_
  53.5 2.6 %shard_map.71 = (bf16[224,256]{1,0:T(8,128)(2,1)S(1)}, bf16[512,768]{1,0:T(8,128)(2,1)S(1)}) custom-call(s32[4]{0:T(128)S(1)} %copy-done.1, f32[48,128]{1,0:T(8,128)S(1)} %get-tuple-element.24.table_ref, bf16[448,512]{1,0:T(8,128)(2,1)S(1)} %get-tuple-element.28.coef_ref, bf16[512,768]{1,0:T(8,128)(2,1)S(1)} %get-tuple-element.32.slab_ref, ...), custom_call_target="tpu_custom_call" | custom-call | flops 550000000 | bytes 2000000 | tf_op jit(solution)/shard_map/pallas_call | solution.py:349
  56.1 2.5 %collective-permute-start.5 = (bf16[224,256]{1,0:T(8,128)(2,1)S(1)}, bf16[224,256]{1,0:T(8,128)(2,1)S(1)}, u32[]{:S(2)}, u32[]{:S(2)}) collective-permute-start(bf16[224,256]{1,0:T(8,128)(2,1)S(1)} %get-tuple-element.35.before_ref), channel_id=1, source_target_pairs={{0,2},{1,3},{2,0},{3,1},{4,6},{5,7},{6,4},{7,5},{8,10},{9,11},{10,... | collective-permute-start | bytes 344072 | tf_op jit(solution)/shard_map/ppermute | solution.py:346
  58.6 0.5 collective-permute-start.2
  59.2 6.6 %shard_map.72 = (bf16[224,256]{1,0:T(8,128)(2,1)S(1)}, bf16[224,256]{1,0:T(8,128)(2,1)S(1)}, f32[2,224,256]{2,1,0:T(8,128)S(1)}) custom-call(s32[4]{0:T(128)S(1)} %copy-done.1, f32[48,128]{1,0:T(8,128)S(1)} %get-tuple-element.24.table_ref, bf16[8,112,512]{2,1,0:T(8,128)(2,1)S(1)} %all_to_all.10.got_ref, ...), custom_call_target="tpu_custom_call" | custom-call | flops 2200000000 | bytes 6000000 | tf_op jit(solution)/shard_map/pallas_call | solution.py:373
  65.8 0.0 collective-permute-done.2.far_a_ref
  65.8 1.1 %collective-permute-start.3 = (bf16[224,256]{1,0:T(8,128)(2,1)S(1)}, bf16[224,256]{1,0:T(8,128)(2,1)S(1)}, u32[]{:S(2)}, u32[]{:S(2)}) collective-permute-start(bf16[224,256]{1,0:T(8,128)(2,1)S(1)} %get-tuple-element.40), channel_id=1, source_target_pairs={{0,1},{1,0},{2,3},{3,2},{4,5},{5,4},{6,7},{7,6},{8,9},{9,8},{10,11... | collective-permute-start | bytes 344072 | tf_op jit(solution)/shard_map/ppermute | solution.py:346
  66.9 0.1 collective-permute-start.4
  67.0 0.0 collective-permute-done.5.far_b_ref
  67.0 0.9 %collective-permute-done.3.near_a_ref = bf16[224,256]{1,0:T(8,128)(2,1)S(1)} collective-permute-done((bf16[224,256]{1,0:T(8,128)(2,1)S(1)}, bf16[224,256]{1,0:T(8,128)(2,1)S(1)}, u32[]{:S(2)}, u32[]{:S(2)}) %collective-permute-start.3) | collective-permute-done | bytes 114720 | tf_op jit(solution)/shard_map/ppermute | solution.py:346
  67.9 0.4 collective-permute-done.4.near_b_ref
  68.3 1.4 %shard_map.73 = f32[2,4,2,7,32,32]{5,4,3,2,1,0:T(8,128)} custom-call(f32[2,224,256]{2,1,0:T(8,128)S(1)} %get-tuple-element.36.own_ref, bf16[224,256]{1,0:T(8,128)(2,1)S(1)} %collective-permute-done.3.near_a_ref, bf16[224,256]{1,0:T(8,128)(2,1)S(1)} %collective-permute-done.4.near_b_ref, bf16[224,256]{1,0:T(8,128)(2,1)S(1)} %collective-permute-done.2.far_a_ref, ...), custom_call_target="tpu_custom_call" | custom-call | flops 1000000 | bytes 3000000 | tf_op jit(solution)/shard_map/pallas_call | solution.py:391
  (2 shorter events, 0.0 us)
Async XLA Ops:
  0.0 41.8 %copy-start.1 = (s32[4]{0:T(128)S(1)}, s32[4]{0:T(128)}, u32[]{:S(2)}) copy-start(s32[4]{0:T(128)} %gammas_ref.11) | copy-start | bytes 52
  1.9 20.6 %all-to-all-start = ((bf16[8,32,512]{2,1,0:T(8,128)(2,1)}), bf16[8,32,512]{2,1,0:T(8,128)(2,1)S(1)}, u32[]{:S(2)}, u32[]{:S(2)}) async-start(bf16[8,32,512]{2,1,0:T(8,128)(2,1)} %bitcast.13), calls=%async_computation | async-start | bytes 524288 | tf_op jit(solution)/shard_map/all_to_all | solution.py:302
  11.9 0.7 copy-start
  12.5 0.7 copy-start.3
  22.6 0.7 copy-start.2
  44.9 5.9 %collective-permute-start = (bf16[224,256]{1,0:T(8,128)(2,1)S(1)}, bf16[224,256]{1,0:T(8,128)(2,1)S(1)}, u32[]{:S(2)}, u32[]{:S(2)}) collective-permute-start(bf16[224,256]{1,0:T(8,128)(2,1)S(1)} %get-tuple-element.31), channel_id=1, source_target_pairs={{0,1},{1,0},{2,3},{3,2},{4,5},{5,4},{6,7},{7,6},{8,9},{9,8},{10,11... | collective-permute-start | bytes 344072 | tf_op jit(solution)/shard_map/ppermute | solution.py:346
  50.7 2.8 %collective-permute-start.1 = (bf16[224,256]{1,0:T(8,128)(2,1)S(1)}, bf16[224,256]{1,0:T(8,128)(2,1)S(1)}, u32[]{:S(2)}, u32[]{:S(2)}) collective-permute-start(bf16[224,256]{1,0:T(8,128)(2,1)S(1)} %get-tuple-element.33), channel_id=1, source_target_pairs={{0,1},{1,0},{2,3},{3,2},{4,5},{5,4},{6,7},{7,6},{8,9},{9,8},{10,11... | collective-permute-start | bytes 344072 | tf_op jit(solution)/shard_map/ppermute | solution.py:346
  56.1 10.9 %collective-permute-start.5 = (bf16[224,256]{1,0:T(8,128)(2,1)S(1)}, bf16[224,256]{1,0:T(8,128)(2,1)S(1)}, u32[]{:S(2)}, u32[]{:S(2)}) collective-permute-start(bf16[224,256]{1,0:T(8,128)(2,1)S(1)} %get-tuple-element.35.before_ref), channel_id=1, source_target_pairs={{0,2},{1,3},{2,0},{3,1},{4,6},{5,7},{6,4},{7,5},{8,10},{9,11},{10,... | collective-permute-start | bytes 344072 | tf_op jit(solution)/shard_map/ppermute | solution.py:346
  58.6 7.1 %collective-permute-start.2 = (bf16[224,256]{1,0:T(8,128)(2,1)S(1)}, bf16[224,256]{1,0:T(8,128)(2,1)S(1)}, u32[]{:S(2)}, u32[]{:S(2)}) collective-permute-start(bf16[224,256]{1,0:T(8,128)(2,1)S(1)} %get-tuple-element.39), channel_id=1, source_target_pairs={{0,2},{1,3},{2,0},{3,1},{4,6},{5,7},{6,4},{7,5},{8,10},{9,11},{10,... | collective-permute-start | bytes 344072 | tf_op jit(solution)/shard_map/ppermute | solution.py:346
  65.8 2.1 %collective-permute-start.3 = (bf16[224,256]{1,0:T(8,128)(2,1)S(1)}, bf16[224,256]{1,0:T(8,128)(2,1)S(1)}, u32[]{:S(2)}, u32[]{:S(2)}) collective-permute-start(bf16[224,256]{1,0:T(8,128)(2,1)S(1)} %get-tuple-element.40), channel_id=1, source_target_pairs={{0,1},{1,0},{2,3},{3,2},{4,5},{5,4},{6,7},{7,6},{8,9},{9,8},{10,11... | collective-permute-start | bytes 344072 | tf_op jit(solution)/shard_map/ppermute | solution.py:346
  66.9 1.3 %collective-permute-start.4 = (bf16[224,256]{1,0:T(8,128)(2,1)S(1)}, bf16[224,256]{1,0:T(8,128)(2,1)S(1)}, u32[]{:S(2)}, u32[]{:S(2)}) collective-permute-start(bf16[224,256]{1,0:T(8,128)(2,1)S(1)} %get-tuple-element.41), channel_id=1, source_target_pairs={{0,1},{1,0},{2,3},{3,2},{4,5},{5,4},{6,7},{7,6},{8,9},{9,8},{10,11... | collective-permute-start | bytes 344072 | tf_op jit(solution)/shard_map/ppermute | solution.py:346

commit v3 on v2

--- a/solution.py
+++ b/solution.py
@@ -19,7 +19,6 @@
 COLS = 768
 OPS = 4
 CAND = 128
-SPARE = 4
 Z_GROUPS = [[z * SPOTS + p for z in range(PLANES)] for p in range(SPOTS)]
 P_GROUPS = [[z * SPOTS + p for p in range(SPOTS)] for z in range(PLANES)]
 PAIRS = [(0, 1), (3, 4), (6, 7), (9, 10), (2, 5), (8, 11)]
@@ -103,6 +102,10 @@
         cosine = jnp.cos(turn)
         sine = jnp.sin(turn)
         bits = lax.shift_right_logical(gammas_ref[op], 2)
+        for flag in range(2):
+            at = OPS * 12 + op * 2 + flag
+            on = lax.shift_right_logical(gammas_ref[op], flag) & 1
+            table_ref[at : at + 1, :] = jnp.full((1, 128), on, jnp.int32).astype(F32)
         for group in range(6):
             spin = jnp.full((1, 128), group, jnp.int32) if group < 4 else 2 * (group - 4) + lax.shift_right_logical(lane, 6)
             common = spin & bits
@@ -113,59 +116,37 @@
             table_ref[at + 1 : at + 2, :] = sine * sign
 
 
-def sort_kernel(basis_ref, out_ref, done_ref, reads_ref, slots_ref, in_sems, sems):
-    done_ref[...] = jnp.zeros(done_ref.shape, F32)
-    step = 64
+def block_of(mask):
+    return lax.shift_right_logical(lax.axis_index("space") ^ mask, 1)
+
+
+def sort_kernel(mask, basis_ref, after_ref, far_ref, near_ref, done_ref, reads_ref, in_sems, done_sem):
+    step = 128
     chunks = 2 * WIDTH // step
     low = iota((step, 128), 1) < 64
-
-    def take(chunk, slot):
-        rows = pl.ds(pl.multiple_of(chunk * step, step), step)
-        return pltpu.make_async_copy(basis_ref.at[:, rows, :], reads_ref.at[slot], in_sems.at[slot])
-
-    def leave(chunk, slot):
-        rows = pl.ds(pl.multiple_of(chunk * step, step), step)
-        return pltpu.make_async_copy(slots_ref.at[slot], out_ref.at[0:2, :, rows, :], sems.at[slot])
-
-    for slot in range(2):
-        take(slot, slot).start()
-
-    @pl.loop(0, chunks // 2)
-    def _(turn):
-        for slot in range(2):
-            chunk = turn * 2 + slot
-            take(chunk, slot).wait()
-
-            @pl.when(turn > 0)
-            def _():
-                leave(chunk - 2, slot).wait()
-
-            for block in range(2):
-                for group, (first, second) in enumerate(PAIRS):
-                    lanes = slice(group * 128, (group + 1) * 128)
-                    for pair in range(2):
-                        at = pair * 128
-                        a = reads_ref[slot, block, :, first * 256 + at : first * 256 + at + 128]
-                        b = reads_ref[slot, block, :, second * 256 + at : second * 256 + at + 128]
-                        slots_ref[slot, block, 2 * pair, :, lanes] = jnp.where(low, a, pltpu.roll(b, 64, 1))
-                        slots_ref[slot, block, 2 * pair + 1, :, lanes] = jnp.where(low, pltpu.roll(a, 64, 1), b)
-            leave(chunk, slot).start()
-
-            @pl.when(turn < chunks // 2 - 1)
-            def _():
-                take(chunk + 2, slot).start()
-
-    for slot in range(2):
-        leave(chunks - 2 + slot, slot).wait()
-
-
-def block_of(mask):
-    return lax.shift_right_logical(lax.axis_index("space") ^ mask, 1)
-
-
-def fetch(sorted_ref, slab_ref, sem, mask, t):
-    target = lax.axis_index("space") ^ mask
-    return pltpu.make_async_copy(sorted_ref.at[block_of(mask), 2 * (target & 1) + t], slab_ref, sem)
+    block = block_of(mask)
+    core = lax.axis_index("space") & 1
+    reads = []
+    for chunk in range(chunks):
+        rows = slice(chunk * step, (chunk + 1) * step)
+        reads.append(pltpu.make_async_copy(basis_ref.at[block, rows, :], reads_ref.at[rows, :], in_sems.at[chunk]))
+    for read in reads:
+        read.start()
+    for chunk, read in enumerate(reads):
+        read.wait()
+        if chunk == 0:
+            done = pltpu.make_async_copy(reads_ref.at[:16, :128], done_ref, done_sem)
+            done.start()
+        rows = slice(chunk * step, (chunk + 1) * step)
+        for out_ref, half in ((far_ref, 1 - core), (near_ref, core)):
+            for group, (first, second) in enumerate(PAIRS):
+                lanes = slice(group * 128, (group + 1) * 128)
+                at = pl.multiple_of(half * 128, 128)
+                a = reads_ref[rows, pl.ds(first * 256 + at, 128)]
+                b = reads_ref[rows, pl.ds(second * 256 + at, 128)]
+                out_ref[0, rows, lanes] = jnp.where(low, a, pltpu.roll(b, 64, 1))
+                out_ref[1, rows, lanes] = jnp.where(low, pltpu.roll(a, 64, 1), b)
+    done.wait()
 
 
 def place(block, got_ref, placer_ref, coef_ref):
@@ -182,24 +163,33 @@
         coef_ref[bottom, WIDTH:] = re.astype(BF16)
 
 
-def entries(gammas_ref, table_ref, coef_ref, slab_ref, vec_ref, weight_ref):
-    vec = jnp.dot(coef_ref[...], slab_ref[...], preferred_element_type=F32).astype(BF16)
+def entries(table_ref, coef_ref, slab, vec_ref, weight_ref):
+    vec = jnp.dot(coef_ref[...], slab, preferred_element_type=F32).astype(BF16)
     vec_ref[:, :COLS] = vec[:ROWS]
     vec_ref[:, COLS:] = vec[ROWS:]
+    own = []
+    for part in range(2):
+        lanes = [slice(part * COLS + group * 128, part * COLS + (group + 1) * 128) for group in range(6)]
+        own.append([vec_ref[0:MODES, at].astype(F32) for at in lanes])
+    rolled = [[pltpu.roll(own[part][4 + half], 64, 1) for half in range(2)] for part in range(2)]
     for op in range(OPS):
-        flip = gammas_ref[op] & 3
+        at = OPS * 12 + op * 2
+        swap = jnp.broadcast_to(table_ref[at : at + 1, :], (MODES, 128)) > 0.5
+        cross = jnp.broadcast_to(table_ref[at + 1 : at + 2, :], (MODES, 128)) > 0.5
+        spun = []
+        for part in range(2):
+            v = own[part]
+            r = rolled[part]
+            crossed = [jnp.where(cross, v[spin ^ 2], v[spin]) for spin in range(4)]
+            whole = [jnp.where(cross, v[4 + (half ^ 1)], v[4 + half]) for half in range(2)]
+            turned = [jnp.where(cross, r[half ^ 1], r[half]) for half in range(2)]
+            spun.append(
+                [jnp.where(swap, crossed[spin ^ 1], crossed[spin]) for spin in range(4)]
+                + [jnp.where(swap, turned[half], whole[half]) for half in range(2)]
+            )
         for group in range(6):
-            if group < 4:
-                source = group ^ flip
-            else:
-                source = 4 + ((group - 4) ^ lax.shift_right_logical(flip, 1))
-            start = pl.multiple_of(source * 128, 128)
-            re = vec_ref[0:MODES, pl.ds(start, 128)].astype(F32)
-            im = vec_ref[0:MODES, pl.ds(start + COLS, 128)].astype(F32)
-            if group >= 4:
-                swap = (flip & 1) == 1
-                re = jnp.where(swap, pltpu.roll(re, 64, 1), re)
-                im = jnp.where(swap, pltpu.roll(im, 64, 1), im)
+            re = spun[0][group]
+            im = spun[1][group]
             at = (op * 6 + group) * 2
             cosine = table_ref[at : at + 1, :]
             sine = table_ref[at + 1 : at + 2, :]
@@ -216,45 +206,28 @@
     return lax.dot_general(vec_ref[...], weight_ref[...], (((1,), (1,)), ((), ())), preferred_element_type=F32)
 
 
-def first_kernel(now, after, gammas_ref, table_ref, got_ref, placer_ref, sorted_ref, out_ref, coef_ref, next_ref, slab_ref, vec_ref, weight_ref, sems):
-    slab = fetch(sorted_ref, slab_ref, sems.at[0], *now)
-    later = fetch(sorted_ref, next_ref, sems.at[1], *after)
-    slab.start()
-    later.start()
-    place(block_of(now[0]), got_ref, placer_ref, coef_ref)
-    slab.wait()
-    out_ref[...] = entries(gammas_ref, table_ref, coef_ref, slab_ref, vec_ref, weight_ref).astype(BF16)
-    later.wait()
-
-
-def middle_kernel(after, gammas_ref, table_ref, coef_ref, slab_ref, sorted_ref, *rest):
-    out_ref, next_ref, vec_ref, weight_ref, sem = rest[-5:]
-    later = fetch(sorted_ref, next_ref, sem, *after)
-    later.start()
-    total = entries(gammas_ref, table_ref, coef_ref, slab_ref, vec_ref, weight_ref)
-    if len(rest) > 5:
-        total = total + rest[0][...].astype(F32)
-    out_ref[...] = total.astype(BF16)
-    later.wait()
-
-
-def last_kernel(steps, gammas_ref, table_ref, got_ref, placer_ref, slab_ref, sorted_ref, before_ref, part_a_ref, part_b_ref, own_ref, coef_ref, slabs_ref, vec_ref, weight_ref, sems):
+def first_kernel(mask, table_ref, got_ref, placer_ref, slab_ref, out_ref, coef_ref, *work):
+    place(block_of(mask), got_ref, placer_ref, coef_ref)
+    for t in range(2):
+        out_ref[t] = entries(table_ref, coef_ref, slab_ref[t], *work[2 * t : 2 * t + 2]).astype(BF16)
+
+
+def second_kernel(table_ref, coef_ref, slab_ref, out_ref, *work):
+    for t in range(2):
+        out_ref[t] = entries(table_ref, coef_ref, slab_ref[t], *work[2 * t : 2 * t + 2])
+
+
+def pair_kernel(own_ref, other_ref, out_a_ref, out_b_ref):
+    for t, out_ref in enumerate((out_a_ref, out_b_ref)):
+        out_ref[...] = (own_ref[t] + other_ref[t].astype(F32)).astype(BF16)
+
+
+def last_kernel(table_ref, got_ref, placer_ref, far_ref, near_ref, before_ref, part_a_ref, part_b_ref, own_ref, coef_ref, *work):
     place(block_of(0), got_ref, placer_ref, coef_ref)
-    copies = [None] + [
-        fetch(sorted_ref, slabs_ref.at[n % 2], sems.at[n % 2], *step) for n, step in enumerate(steps) if n > 0
-    ]
-    copies[1].start()
-    for n, (mask, t) in enumerate(steps):
-        if n > 0:
-            copies[n].wait()
-        if 0 < n < len(steps) - 1:
-            copies[n + 1].start()
-        slab = slab_ref if n == 0 else slabs_ref.at[n % 2]
-        total = entries(gammas_ref, table_ref, coef_ref, slab, vec_ref.at[n % 2], weight_ref.at[n % 2])
-        if mask == 1:
-            (part_a_ref, part_b_ref)[t][...] = total.astype(BF16)
-        else:
-            own_ref[t] = total
+    for t, part_ref in enumerate((part_a_ref, part_b_ref)):
+        part_ref[...] = entries(table_ref, coef_ref, far_ref[t], *work[2 * t : 2 * t + 2]).astype(BF16)
+    for t in range(2):
+        own_ref[t] = entries(table_ref, coef_ref, near_ref[t], *work[2 * t : 2 * t + 2])
 
 
 def total_kernel(own_ref, near_a_ref, near_b_ref, far_a_ref, far_b_ref, out_ref, total_ref, sems):
@@ -306,85 +279,70 @@
     by_reader = jnp.repeat(by_reader, 2, axis=1)
     placer, table = kernel_call(
         tables_kernel,
-        (shape((2, STOPW, MODES, CAND)), shape((OPS * 12, 128), F32)),
+        (shape((2, STOPW, MODES, CAND)), shape((OPS * 14, 128), F32)),
         [SMEM, SMEM, VMEM],
         2_000_000,
         200_000,
     )(momenta, gammas, by_reader)
-    sorted_basis, done = kernel_call(
-        sort_kernel,
-        (shape((SPARE * 2, 4, 2 * WIDTH, COLS)), shape((8, 128), F32)),
-        [HBM],
-        10_000_000,
-        13_000_000,
-        [
-            pltpu.VMEM((2, 2, 64, 4 * COLS), BF16),
-            pltpu.VMEM((2, 2, 4, 64, COLS), BF16),
-            DMA((2,)),
-            DMA((2,)),
-        ],
-        limit=60,
-        out_specs=(HBM, VMEM),
-    )(basis.reshape(2, 2 * WIDTH, 4 * COLS))
+    slab_shape = shape((2, 2 * WIDTH, COLS))
+    token = shape((16, 128))
+
+    def sort(mask, after, limit):
+        return kernel_call(
+            functools.partial(sort_kernel, mask),
+            (slab_shape, slab_shape, token),
+            [HBM, HBM],
+            5_000_000,
+            6_000_000,
+            [pltpu.VMEM((2 * WIDTH, 4 * COLS), BF16), DMA((4,)), DMA],
+            limit=limit,
+            out_specs=(VMEM, VMEM, HBM),
+        )(basis.reshape(2, 2 * WIDTH, 4 * COLS), after)
+
+    slab_3, slab_2, done = sort(2, table, 52)
     onward = kernel_call(
         forward_kernel,
         shape((SPOTS, STOPW * 16, 2 * WIDTH)),
-        [VMEM, VMEM, VMEM],
+        [VMEM, HBM, VMEM],
         70_000_000,
         1_200_000,
         [pltpu.VMEM(((SPOTS + STOPW - 1) * 16, 2 * WIDTH), BF16), DMA((SPOTS,))],
         out_specs=HBM,
     )(first.reshape(PLANES * 32, 2 * WIDTH), done, table)
     got = lax.all_to_all(onward, "mode", 0, 0, tiled=True, axis_index_groups=P_GROUPS)
+    slab_1, slab_0, _ = sort(0, onward, 59)
+    got, slab_1, slab_0 = lax.optimization_barrier((got, slab_1, slab_0))
     part_shape = shape((ROWS, 256))
-    slab_shape = shape((2 * WIDTH, COLS))
-    vec_shape = (ROWS, 2 * COLS)
-    weight_shape = (256, 2 * COLS)
-    work = [pltpu.VMEM(vec_shape, BF16), pltpu.VMEM(weight_shape, BF16)]
+    pair_shape = shape((2, ROWS, 256))
+    wide_shape = shape((2, ROWS, 256), F32)
+    coef_shape = (2 * ROWS, 2 * WIDTH)
+    work = [pltpu.VMEM((ROWS, 2 * COLS), BF16), pltpu.VMEM((256, 2 * COLS), BF16)] * 2
 
     def between(pair, part):
         return lax.ppermute(part, "space", [(i, i ^ pair) for i in range(4)])
 
-    def middle(slab, after, *extra):
-        return kernel_call(
-            functools.partial(middle_kernel, after),
-            (part_shape, slab_shape),
-            [SMEM, VMEM, VMEM, VMEM, HBM] + [VMEM] * len(extra),
-            550_000_000,
-            2_000_000,
-            work + [DMA],
-            limit=44,
-        )(gammas, table, coef, slab, sorted_basis, *extra)
-
-    other_a, coef, slab = kernel_call(
-        functools.partial(first_kernel, (3, 0), (3, 1)),
-        (part_shape, shape((2 * ROWS, 2 * WIDTH)), slab_shape),
-        [SMEM, VMEM, VMEM, VMEM, HBM],
-        600_000_000,
+    part_3, coef = kernel_call(
+        functools.partial(first_kernel, 3),
+        (pair_shape, shape(coef_shape)),
+        [VMEM] * 4,
+        1_200_000_000,
         3_000_000,
-        [pltpu.VMEM((2 * WIDTH, COLS), BF16)] + work + [DMA((2,))],
-        limit=44,
-    )(gammas, table, got, placer, sorted_basis)
-    other_b, slab = middle(slab, (2, 0))
-    chip_a, slab = middle(slab, (2, 1), between(1, other_a))
+        work,
+    )(table, got, placer, slab_3)
+    part_2 = kernel_call(second_kernel, wide_shape, [VMEM] * 3, 1_100_000_000, 3_000_000, work)(table, coef, slab_2)
+    chip_a, chip_b = kernel_call(pair_kernel, (part_shape, part_shape), [VMEM] * 2, 200_000, 900_000)(
+        part_2, between(1, part_3)
+    )
     far_a = between(2, chip_a)
-    chip_b, slab = middle(slab, (1, 0), between(1, other_b))
     far_b = between(2, chip_b)
     part_a, part_b, own = kernel_call(
-        functools.partial(last_kernel, ((1, 0), (1, 1), (0, 0), (0, 1))),
-        (part_shape, part_shape, shape((2, ROWS, 256), F32)),
-        [SMEM, VMEM, VMEM, VMEM, VMEM, HBM, VMEM],
+        last_kernel,
+        (part_shape, part_shape, wide_shape),
+        [VMEM] * 6,
         2_200_000_000,
         6_000_000,
-        [
-            pltpu.VMEM((2 * ROWS, 2 * WIDTH), BF16),
-            pltpu.VMEM((2, 2 * WIDTH, COLS), BF16),
-            pltpu.VMEM((2, *vec_shape), BF16),
-            pltpu.VMEM((2, *weight_shape), BF16),
-            DMA((2,)),
-        ],
-        limit=44,
-    )(gammas, table, got, placer, slab, sorted_basis, chip_b)
+        [pltpu.VMEM(coef_shape, BF16)] + work,
+    )(table, got, placer, slab_1, slab_0, chip_b)
     part_a, part_b, far_a = lax.optimization_barrier((part_a, part_b, far_a))
     near_a = between(1, part_a)
     near_b = between(1, part_b)

time: 70.3 us -> 57.8 us (0.82)
  blocking collectives: 17.1 us -> 0 us
  Pallas kernels: 31.7 us -> 21.6 us
  waiting for transfers between devices: 1.23 us -> 10.3 us
  starting transfers between devices: 16.5 us -> 23 us
    all_to_all x1 -> x0, blocking collectives: 17.1 us -> none  [per_device(): lax.all_to_all(onward, 'mode', 0, 0, tiled=True, axis_index_groups=P_GROUPS)]
    pallas_call x6, Pallas kernels: 26.2 us -> 16.3 us  [the longest x2 7.8 us: sort(): kernel_call(functools.partial(sort_kernel, mask), (slab_shape, slab_shape...]
    all_to_all x0 -> x1, waiting for transfers between devices: none -> 5.4 us  [per_device(): lax.all_to_all(onward, 'mode', 0, 0, tiled=True, axis_index_groups=P_GROUPS)]
    all_to_all x0 -> x1, starting transfers between devices: none -> 5.13 us  [per_device(): lax.all_to_all(onward, 'mode', 0, 0, tiled=True, axis_index_groups=P_GROUPS)]
    all_to_all x1, waiting for transfers between devices: 0.01 us -> 3.71 us  [per_device(): lax.all_to_all(packed.reshape(PLANES, 32, 2 * WIDTH), 'mode', 0, 0, tiled...]
    ppermute x6 -> x5, starting transfers between devices: 7.53 us -> 8.87 us  [between(): return lax.ppermute(part, 'space', [(i, i ^ pair) for i in range(4)])]
    unnamed x8 -> x10, local copies, waits for them, and re-layouts: 2.02 us -> 1.36 us
  transfers between devices with their start and end apart: 7 -> 7, of which waited for: 2 -> 5; matrix products, arithmetic and copies ran while one was open for 1% -> 2% of each run, Pallas kernels for 30% -> 26%
where the time goes in v3:
time: 57.8 us; the launch traced here: 57.4 us
  starting transfers between devices  23 us (40%)
  Pallas kernels  21.6 us (37%)
  waiting for transfers between devices  10.3 us (18%)
  local copies, waits for them, and re-layouts  2.25 us (4%)
    all_to_all x1, starting transfers between devices, per_device(): lax.all_to_all(packed.reshape(PLANES, 32, 2 * WIDTH), 'mode', 0, 0, tiled...  9.01 us
    ppermute x5, starting transfers between devices, between(): return lax.ppermute(part, 'space', [(i, i ^ pair) for i in range(4)])  8.87 us
    pallas_call x2, Pallas kernels, sort(): kernel_call(functools.partial(sort_kernel, mask), (slab_shape, slab_shape...  7.8 us
    all_to_all x1, waiting for transfers between devices, per_device(): lax.all_to_all(onward, 'mode', 0, 0, tiled=True, axis_index_groups=P_GROUPS)  5.4 us
    all_to_all x1, starting transfers between devices, per_device(): lax.all_to_all(onward, 'mode', 0, 0, tiled=True, axis_index_groups=P_GROUPS)  5.13 us
    pallas_call x1, Pallas kernels, per_device(): kernel_call(last_kernel, (part_shape, part_shape, wide_shape), [VMEM] * 6...  3.93 us
    all_to_all x1, waiting for transfers between devices, per_device(): lax.all_to_all(packed.reshape(PLANES, 32, 2 * WIDTH), 'mode', 0, 0, tiled...  3.71 us
    pallas_call x1, Pallas kernels, per_device(): kernel_call(functools.partial(first_kernel, 3), (pair_shape, shape(coef_s...  2.34 us
  transfers between devices with their start and end apart: 7, of which 5 were waited for; matrix products, arithmetic and copies ran while one was open for 2% of the time, Pallas kernels for 26%

profile of v3, /device:TPU:1, one launch (start us, length us, event | category | flops | bytes accessed | tf_op | source)
XLA Modules:
  0.0 57.4 jit_solution(1484305522688764585)
XLA Ops:
  0.0 1.9 %shard_map.65 = bf16[256,512]{1,0:T(8,128)(2,1)} custom-call(s32[32,128]{1,0:T(8,128)} %bitcast.19, bf16[64,2,256]{2,1,0:T(2,128)(2,1)} %bitcast.18, s32[1,64]{1,0:T(1,128)} %bitcast.20), custom_call_target="tpu_custom_call" | custom-call | flops 20000000 | bytes 400000 | tf_op jit(solution)/shard_map/pallas_call | solution.py:272
  1.9 9.0 %all-to-all-start = ((bf16[8,32,512]{2,1,0:T(8,128)(2,1)}), bf16[8,32,512]{2,1,0:T(8,128)(2,1)S(1)}, u32[]{:S(2)}, u32[]{:S(2)}) async-start(bf16[8,32,512]{2,1,0:T(8,128)(2,1)} %bitcast.14), calls=%async_computation | async-start | bytes 524288 | tf_op jit(solution)/shard_map/all_to_all | solution.py:275
  10.9 0.8 %reshape.28 = s32[8,8,64]{2,1,0:T(8,128)S(1)} reshape(s32[4096]{0:T(1024)} %param.8) | data formatting | bytes 32768 | tf_op jit(solution)/shard_map/reshape | solution.py:278
  11.8 0.1 copy.8.route_ref
  11.8 0.0 copy-start
  11.8 0.7 %copy-done = s32[4,3]{1,0:T(4,128)S(1)} copy-done((s32[4,3]{1,0:T(4,128)S(1)}, s32[4,3]{1,0:T(4,128)}, u32[]{:S(2)}) %copy-start) | copy-done | bytes 72
  12.5 0.0 copy-start.1
  12.5 0.7 %copy-done.1 = s32[4]{0:T(128)S(1)} copy-done((s32[4]{0:T(128)S(1)}, s32[4]{0:T(128)}, u32[]{:S(2)}) %copy-start.1) | copy-done | bytes 40
  13.2 0.8 %shard_map.64 = (bf16[2,7,32,128]{3,2,1,0:T(8,128)(2,1)S(1)}, f32[56,128]{1,0:T(8,128)S(1)}) custom-call(s32[4,3]{1,0:T(4,128)S(1)} %copy-done, s32[4]{0:T(128)S(1)} %copy-done.1, s32[64,128]{1,0:T(8,128)S(1)} %copy.8.route_ref), custom_call_target="tpu_custom_call" | custom-call | flops 2000000 | bytes 200000 | tf_op jit(solution)/shard_map/pallas_call | solution.py:280
  14.0 3.6 %shard_map.66 = (bf16[2,512,768]{2,1,0:T(8,128)(2,1)S(1)}, bf16[2,512,768]{2,1,0:T(8,128)(2,1)}, bf16[16,128]{1,0:T(8,128)(2,1)S(1)}) custom-call(bf16[2,512,3072]{2,1,0:T(8,128)(2,1)} %bitcast.12, f32[56,128]{1,0:T(8,128)S(1)} %get-tuple-element.25.after_ref.table_ref), custom_call_target="tpu_custom_call" | custom-call | flops 5000000 | bytes 6000000 | tf_op jit(solution)/shard_map/pallas_call | solution.py:291
  17.6 3.7 %all-to-all-done = bf16[8,32,512]{2,1,0:T(8,128)(2,1)S(1)} async-done(((bf16[8,32,512]{2,1,0:T(8,128)(2,1)}), bf16[8,32,512]{2,1,0:T(8,128)(2,1)S(1)}, u32[]{:S(2)}, u32[]{:S(2)}) %all-to-all-start) | async-done | bytes 262176 | tf_op jit(solution)/shard_map/all_to_all | solution.py:275
  21.3 1.3 %shard_map.67.after_ref = bf16[8,112,512]{2,1,0:T(8,128)(2,1)} custom-call(bf16[256,512]{1,0:T(8,128)(2,1)S(1)} %bitcast.11, bf16[16,128]{1,0:T(8,128)(2,1)S(1)} %get-tuple-element.26.done_ref, f32[56,128]{1,0:T(8,128)S(1)} %get-tuple-element.25.after_ref.table_ref), custom_call_target="tpu_custom_call" | custom-call | flops 70000000 | bytes 1200000 | tf_op jit(solution)/shard_map/pallas_call | solution.py:303
  22.6 5.1 %all-to-all-start.1 = ((bf16[8,112,512]{2,1,0:T(8,128)(2,1)}), bf16[8,112,512]{2,1,0:T(8,128)(2,1)S(1)}, u32[]{:S(2)}, u32[]{:S(2)}) async-start(bf16[8,112,512]{2,1,0:T(8,128)(2,1)} %shard_map.67.after_ref), calls=%async_computation.1 | async-start | bytes 1835008 | tf_op jit(solution)/shard_map/all_to_all | solution.py:312
  27.7 4.2 %shard_map.68 = (bf16[2,512,768]{2,1,0:T(8,128)(2,1)}, bf16[2,512,768]{2,1,0:T(8,128)(2,1)}, bf16[16,128]{1,0:T(8,128)(2,1)}) custom-call(bf16[2,512,3072]{2,1,0:T(8,128)(2,1)} %bitcast.13, bf16[8,112,512]{2,1,0:T(8,128)(2,1)} %shard_map.67.after_ref), custom_call_target="tpu_custom_call" | custom-call | flops 5000000 | bytes 6000000 | tf_op jit(solution)/shard_map/pallas_call | solution.py:291
  31.9 5.4 %all-to-all-done.1.got_ref = bf16[8,112,512]{2,1,0:T(8,128)(2,1)S(1)} async-done(((bf16[8,112,512]{2,1,0:T(8,128)(2,1)}), bf16[8,112,512]{2,1,0:T(8,128)(2,1)S(1)}, u32[]{:S(2)}, u32[]{:S(2)}) %all-to-all-start.1) | async-done | bytes 917536 | tf_op jit(solution)/shard_map/all_to_all | solution.py:312
  37.3 0.0 copy-start.4
  37.3 2.3 %shard_map.69 = (bf16[2,224,256]{2,1,0:T(8,128)(2,1)S(1)}, bf16[448,512]{1,0:T(8,128)(2,1)S(1)}) custom-call(f32[56,128]{1,0:T(8,128)S(1)} %get-tuple-element.25.after_ref.table_ref, bf16[8,112,512]{2,1,0:T(8,128)(2,1)S(1)} %all-to-all-done.1.got_ref, bf16[2,7,32,128]{3,2,1,0:T(8,128)(2,1)S(1)} %get-tuple-element.30.placer_ref, ...), custom_call_target="tpu_custom_call" | custom-call | flops 1200000000 | bytes 3000000 | tf_op jit(solution)/shard_map/pallas_call | solution.py:324
  39.6 5.0 %collective-permute-start = (bf16[2,224,256]{2,1,0:T(8,128)(2,1)S(1)}, bf16[2,224,256]{2,1,0:T(8,128)(2,1)S(1)}, u32[]{:S(2)}, u32[]{:S(2)}) collective-permute-start(bf16[2,224,256]{2,1,0:T(8,128)(2,1)S(1)} %get-tuple-element.36), channel_id=1, source_target_pairs={{0,1},{1,0},{2,3},{3,2},{4,5},{5,4},{6,7},{7,6},{8,9},{9,8},{10,11... | collective-permute-start | bytes 688136 | tf_op jit(solution)/shard_map/ppermute | solution.py:322
  44.6 0.0 copy-done.4
  44.7 0.0 copy-start.2
  44.7 0.0 copy-start.3
  44.7 2.2 %shard_map.70.own_ref = f32[2,224,256]{2,1,0:T(8,128)S(1)} custom-call(f32[56,128]{1,0:T(8,128)S(1)} %get-tuple-element.25.after_ref.table_ref, bf16[448,512]{1,0:T(8,128)(2,1)S(1)} %get-tuple-element.34.coef_ref, bf16[2,512,768]{2,1,0:T(8,128)(2,1)S(1)} %copy-done.4), custom_call_target="tpu_custom_call" | custom-call | flops 1100000000 | bytes 3000000 | tf_op jit(solution)/shard_map/pallas_call | solution.py:332
  46.8 0.0 collective-permute-done.other_ref
  46.9 2.5 %collective-permute-start.1 = (bf16[224,256]{1,0:T(8,128)(2,1)S(1)}, bf16[224,256]{1,0:T(8,128)(2,1)S(1)}, u32[]{:S(2)}, u32[]{:S(2)}) collective-permute-start(bf16[224,256]{1,0:T(8,128)(2,1)S(1)} %get-tuple-element.41), channel_id=1, source_target_pairs={{0,2},{1,3},{2,0},{3,1},{4,6},{5,7},{6,4},{7,5},{8,10},{9,11},{10,... | collective-permute-start | bytes 344072 | tf_op jit(solution)/shard_map/ppermute | solution.py:322
  49.4 0.5 collective-permute-start.4
  49.9 0.0 copy-done.2
  50.0 0.0 copy-done.3
  50.0 3.9 %shard_map.72 = (bf16[224,256]{1,0:T(8,128)(2,1)S(1)}, bf16[224,256]{1,0:T(8,128)(2,1)S(1)}, f32[2,224,256]{2,1,0:T(8,128)S(1)}) custom-call(f32[56,128]{1,0:T(8,128)S(1)} %get-tuple-element.25.after_ref.table_ref, bf16[8,112,512]{2,1,0:T(8,128)(2,1)S(1)} %all-to-all-done.1.got_ref, bf16[2,7,32,128]{3,2,1,0:T(8,128)(2,1)S(1)} %get-tuple-element.30.placer_ref, ...), custom_call_target="tpu_custom_call" | custom-call | flops 2200000000 | bytes 6000000 | tf_op jit(solution)/shard_map/pallas_call | solution.py:338
  53.9 0.0 collective-permute-done.1.far_a_ref
  53.9 0.7 %collective-permute-start.2 = (bf16[224,256]{1,0:T(8,128)(2,1)S(1)}, bf16[224,256]{1,0:T(8,128)(2,1)S(1)}, u32[]{:S(2)}, u32[]{:S(2)}) collective-permute-start(bf16[224,256]{1,0:T(8,128)(2,1)S(1)} %get-tuple-element.42), channel_id=1, source_target_pairs={{0,1},{1,0},{2,3},{3,2},{4,5},{5,4},{6,7},{7,6},{8,9},{9,8},{10,11... | collective-permute-start | bytes 344072 | tf_op jit(solution)/shard_map/ppermute | solution.py:322
  54.6 0.1 collective-permute-start.3
  54.7 0.7 %collective-permute-done.4.far_b_ref = bf16[224,256]{1,0:T(8,128)(2,1)S(1)} collective-permute-done((bf16[224,256]{1,0:T(8,128)(2,1)S(1)}, bf16[224,256]{1,0:T(8,128)(2,1)S(1)}, u32[]{:S(2)}, u32[]{:S(2)}) %collective-permute-start.4) | collective-permute-done | bytes 114720 | tf_op jit(solution)/shard_map/ppermute | solution.py:322
  55.4 0.2 collective-permute-done.2.near_a_ref
  55.6 0.4 collective-permute-done.3.near_b_ref
  55.9 1.3 %shard_map.73 = f32[2,4,2,7,32,32]{5,4,3,2,1,0:T(8,128)} custom-call(f32[2,224,256]{2,1,0:T(8,128)S(1)} %get-tuple-element.38.own_ref, bf16[224,256]{1,0:T(8,128)(2,1)S(1)} %collective-permute-done.2.near_a_ref, bf16[224,256]{1,0:T(8,128)(2,1)S(1)} %collective-permute-done.3.near_b_ref, bf16[224,256]{1,0:T(8,128)(2,1)S(1)} %collective-permute-done.1.far_a_ref, ...), custom_call_target="tpu_custom_call" | custom-call | flops 1000000 | bytes 3000000 | tf_op jit(solution)/shard_map/pallas_call | solution.py:349
  (3 shorter events, 0.1 us)
Async XLA Ops:
  1.9 19.4 %all-to-all-start = ((bf16[8,32,512]{2,1,0:T(8,128)(2,1)}), bf16[8,32,512]{2,1,0:T(8,128)(2,1)S(1)}, u32[]{:S(2)}, u32[]{:S(2)}) async-start(bf16[8,32,512]{2,1,0:T(8,128)(2,1)} %bitcast.14), calls=%async_computation | async-start | bytes 524288 | tf_op jit(solution)/shard_map/all_to_all | solution.py:275
  11.8 0.7 %copy-start = (s32[4,3]{1,0:T(4,128)S(1)}, s32[4,3]{1,0:T(4,128)}, u32[]{:S(2)}) copy-start(s32[4,3]{1,0:T(4,128)} %momenta_ref.1) | copy-start | bytes 148
  12.5 0.7 %copy-start.1 = (s32[4]{0:T(128)S(1)}, s32[4]{0:T(128)}, u32[]{:S(2)}) copy-start(s32[4]{0:T(128)} %gammas_ref.1) | copy-start | bytes 52
  22.6 14.7 %all-to-all-start.1 = ((bf16[8,112,512]{2,1,0:T(8,128)(2,1)}), bf16[8,112,512]{2,1,0:T(8,128)(2,1)S(1)}, u32[]{:S(2)}, u32[]{:S(2)}) async-start(bf16[8,112,512]{2,1,0:T(8,128)(2,1)} %shard_map.67.after_ref), calls=%async_computation.1 | async-start | bytes 1835008 | tf_op jit(solution)/shard_map/all_to_all | solution.py:312
  37.3 7.4 %copy-start.4 = (bf16[2,512,768]{2,1,0:T(8,128)(2,1)S(1)}, bf16[2,512,768]{2,1,0:T(8,128)(2,1)}, u32[]{:S(2)}) copy-start(bf16[2,512,768]{2,1,0:T(8,128)(2,1)} %get-tuple-element.35.slab_ref) | copy-start | bytes 4718596
  39.6 7.2 %collective-permute-start = (bf16[2,224,256]{2,1,0:T(8,128)(2,1)S(1)}, bf16[2,224,256]{2,1,0:T(8,128)(2,1)S(1)}, u32[]{:S(2)}, u32[]{:S(2)}) collective-permute-start(bf16[2,224,256]{2,1,0:T(8,128)(2,1)S(1)} %get-tuple-element.36), channel_id=1, source_target_pairs={{0,1},{1,0},{2,3},{3,2},{4,5},{5,4},{6,7},{7,6},{8,9},{9,8},{10,11... | collective-permute-start | bytes 688136 | tf_op jit(solution)/shard_map/ppermute | solution.py:322
  44.7 5.3 %copy-start.2 = (bf16[2,512,768]{2,1,0:T(8,128)(2,1)S(1)}, bf16[2,512,768]{2,1,0:T(8,128)(2,1)}, u32[]{:S(2)}) copy-start(bf16[2,512,768]{2,1,0:T(8,128)(2,1)} %get-tuple-element.31.far_ref) | copy-start | bytes 4718596
  44.7 5.3 %copy-start.3 = (bf16[2,512,768]{2,1,0:T(8,128)(2,1)S(1)}, bf16[2,512,768]{2,1,0:T(8,128)(2,1)}, u32[]{:S(2)}) copy-start(bf16[2,512,768]{2,1,0:T(8,128)(2,1)} %get-tuple-element.32.near_ref) | copy-start | bytes 4718596
  46.9 7.0 %collective-permute-start.1 = (bf16[224,256]{1,0:T(8,128)(2,1)S(1)}, bf16[224,256]{1,0:T(8,128)(2,1)S(1)}, u32[]{:S(2)}, u32[]{:S(2)}) collective-permute-start(bf16[224,256]{1,0:T(8,128)(2,1)S(1)} %get-tuple-element.41), channel_id=1, source_target_pairs={{0,2},{1,3},{2,0},{3,1},{4,6},{5,7},{6,4},{7,5},{8,10},{9,11},{10,... | collective-permute-start | bytes 344072 | tf_op jit(solution)/shard_map/ppermute | solution.py:322
  49.4 5.9 %collective-permute-start.4 = (bf16[224,256]{1,0:T(8,128)(2,1)S(1)}, bf16[224,256]{1,0:T(8,128)(2,1)S(1)}, u32[]{:S(2)}, u32[]{:S(2)}) collective-permute-start(bf16[224,256]{1,0:T(8,128)(2,1)S(1)} %get-tuple-element.37.before_ref), channel_id=1, source_target_pairs={{0,2},{1,3},{2,0},{3,1},{4,6},{5,7},{6,4},{7,5},{8,10},{9,11},{10,... | collective-permute-start | bytes 344072 | tf_op jit(solution)/shard_map/ppermute | solution.py:322
  53.9 1.7 %collective-permute-start.2 = (bf16[224,256]{1,0:T(8,128)(2,1)S(1)}, bf16[224,256]{1,0:T(8,128)(2,1)S(1)}, u32[]{:S(2)}, u32[]{:S(2)}) collective-permute-start(bf16[224,256]{1,0:T(8,128)(2,1)S(1)} %get-tuple-element.42), channel_id=1, source_target_pairs={{0,1},{1,0},{2,3},{3,2},{4,5},{5,4},{6,7},{7,6},{8,9},{9,8},{10,11... | collective-permute-start | bytes 344072 | tf_op jit(solution)/shard_map/ppermute | solution.py:322
  54.6 1.3 %collective-permute-start.3 = (bf16[224,256]{1,0:T(8,128)(2,1)S(1)}, bf16[224,256]{1,0:T(8,128)(2,1)S(1)}, u32[]{:S(2)}, u32[]{:S(2)}) collective-permute-start(bf16[224,256]{1,0:T(8,128)(2,1)S(1)} %get-tuple-element.43), channel_id=1, source_target_pairs={{0,1},{1,0},{2,3},{3,2},{4,5},{5,4},{6,7},{7,6},{8,9},{9,8},{10,11... | collective-permute-start | bytes 344072 | tf_op jit(solution)/shard_map/ppermute | solution.py:322

commit v4 on v3

--- a/solution.py
+++ b/solution.py
@@ -55,7 +55,7 @@
         out_ref[:, part * WIDTH : (part + 1) * WIDTH] = packed.astype(BF16)
 
 
-def forward_kernel(got_ref, done_ref, table_ref, out_ref, sorted_ref, sems):
+def forward_kernel(got_ref, done_ref, out_ref, sorted_ref, sems):
     n = (SPOTS + STOPW - 1) * 16
     row = iota((n, PLANES * 32), 0)
     col = iota((n, PLANES * 32), 1)
@@ -73,7 +73,7 @@
         copy.wait()
 
 
-def tables_kernel(momenta_ref, gammas_ref, route_ref, placer_ref, table_ref):
+def tables_kernel(momenta_ref, gammas_ref, route_ref, after_ref, placer_ref, table_ref):
     me = lax.axis_index("mode")
     route = route_ref[...]
     owner = lax.shift_right_logical(route, 6)
@@ -120,7 +120,8 @@
     return lax.shift_right_logical(lax.axis_index("space") ^ mask, 1)
 
 
-def sort_kernel(mask, basis_ref, after_ref, far_ref, near_ref, done_ref, reads_ref, in_sems, done_sem):
+def sort_kernel(mask, basis_ref, *rest):
+    far_ref, near_ref, done_ref, reads_ref, in_sems, done_sem = rest[-6:]
     step = 128
     chunks = 2 * WIDTH // step
     low = iota((step, 128), 1) < 64
@@ -163,58 +164,85 @@
         coef_ref[bottom, WIDTH:] = re.astype(BF16)
 
 
-def entries(table_ref, coef_ref, slab, vec_ref, weight_ref):
-    vec = jnp.dot(coef_ref[...], slab, preferred_element_type=F32).astype(BF16)
-    vec_ref[:, :COLS] = vec[:ROWS]
-    vec_ref[:, COLS:] = vec[ROWS:]
-    own = []
+def expand(coef_ref, slab, vec_ref, chunk):
+    lanes = slice(chunk * 256, (chunk + 1) * 256)
+    vec = jnp.dot(coef_ref[...], slab[:, lanes], preferred_element_type=F32).astype(BF16)
+    vec_ref[:, lanes] = vec[:ROWS]
+    vec_ref[:, COLS + chunk * 256 : COLS + (chunk + 1) * 256] = vec[ROWS:]
+
+
+def weigh(op, table_ref, vec_ref, weight_ref):
+    at = OPS * 12 + op * 2
+    swap = jnp.broadcast_to(table_ref[at : at + 1, :], (MODES, 128)) > 0.5
+    cross = jnp.broadcast_to(table_ref[at + 1 : at + 2, :], (MODES, 128)) > 0.5
+    spun = []
     for part in range(2):
         lanes = [slice(part * COLS + group * 128, part * COLS + (group + 1) * 128) for group in range(6)]
-        own.append([vec_ref[0:MODES, at].astype(F32) for at in lanes])
-    rolled = [[pltpu.roll(own[part][4 + half], 64, 1) for half in range(2)] for part in range(2)]
+        v = [vec_ref[0:MODES, at].astype(F32) for at in lanes]
+        r = [pltpu.roll(v[4 + half], 64, 1) for half in range(2)]
+        crossed = [jnp.where(cross, v[spin ^ 2], v[spin]) for spin in range(4)]
+        whole = [jnp.where(cross, v[4 + (half ^ 1)], v[4 + half]) for half in range(2)]
+        turned = [jnp.where(cross, r[half ^ 1], r[half]) for half in range(2)]
+        spun.append(
+            [jnp.where(swap, crossed[spin ^ 1], crossed[spin]) for spin in range(4)]
+            + [jnp.where(swap, turned[half], whole[half]) for half in range(2)]
+        )
+    for group in range(6):
+        re = spun[0][group]
+        im = spun[1][group]
+        at = (op * 6 + group) * 2
+        cosine = table_ref[at : at + 1, :]
+        sine = table_ref[at + 1 : at + 2, :]
+        w_re = cosine * re - sine * im
+        w_im = sine * re + cosine * im
+        real = slice(op * MODES, (op + 1) * MODES)
+        imag = slice(128 + op * MODES, 128 + (op + 1) * MODES)
+        left = slice(group * 128, (group + 1) * 128)
+        right = slice(COLS + group * 128, COLS + (group + 1) * 128)
+        weight_ref[real, left] = w_re.astype(BF16)
+        weight_ref[real, right] = w_im.astype(BF16)
+        weight_ref[imag, left] = (-w_im).astype(BF16)
+        weight_ref[imag, right] = w_re.astype(BF16)
+
+
+def contract(vec_ref, weight_ref, third):
+    lanes = slice(third * 512, (third + 1) * 512)
+    return lax.dot_general(
+        vec_ref[:, lanes], weight_ref[:, lanes], (((1,), (1,)), ((), ())), preferred_element_type=F32
+    )
+
+
+def entries(table_ref, coef_ref, slab_ref, store, vec_0, weight_0, vec_1, weight_1):
+    for chunk in range(3):
+        expand(coef_ref, slab_ref[0], vec_0, chunk)
     for op in range(OPS):
-        at = OPS * 12 + op * 2
-        swap = jnp.broadcast_to(table_ref[at : at + 1, :], (MODES, 128)) > 0.5
-        cross = jnp.broadcast_to(table_ref[at + 1 : at + 2, :], (MODES, 128)) > 0.5
-        spun = []
-        for part in range(2):
-            v = own[part]
-            r = rolled[part]
-            crossed = [jnp.where(cross, v[spin ^ 2], v[spin]) for spin in range(4)]
-            whole = [jnp.where(cross, v[4 + (half ^ 1)], v[4 + half]) for half in range(2)]
-            turned = [jnp.where(cross, r[half ^ 1], r[half]) for half in range(2)]
-            spun.append(
-                [jnp.where(swap, crossed[spin ^ 1], crossed[spin]) for spin in range(4)]
-                + [jnp.where(swap, turned[half], whole[half]) for half in range(2)]
-            )
-        for group in range(6):
-            re = spun[0][group]
-            im = spun[1][group]
-            at = (op * 6 + group) * 2
-            cosine = table_ref[at : at + 1, :]
-            sine = table_ref[at + 1 : at + 2, :]
-            w_re = cosine * re - sine * im
-            w_im = sine * re + cosine * im
-            real = slice(op * MODES, (op + 1) * MODES)
-            imag = slice(128 + op * MODES, 128 + (op + 1) * MODES)
-            left = slice(group * 128, (group + 1) * 128)
-            right = slice(COLS + group * 128, COLS + (group + 1) * 128)
-            weight_ref[real, left] = w_re.astype(BF16)
-            weight_ref[real, right] = w_im.astype(BF16)
-            weight_ref[imag, left] = (-w_im).astype(BF16)
-            weight_ref[imag, right] = w_re.astype(BF16)
-    return lax.dot_general(vec_ref[...], weight_ref[...], (((1,), (1,)), ((), ())), preferred_element_type=F32)
+        weigh(op, table_ref, vec_0, weight_0)
+        if op < 3:
+            expand(coef_ref, slab_ref[1], vec_1, op)
+    total = None
+    for op in range(OPS):
+        if op < 3:
+            part = contract(vec_0, weight_0, op)
+            total = part if total is None else total + part
+        weigh(op, table_ref, vec_1, weight_1)
+    store(0, total)
+    store(1, sum(contract(vec_1, weight_1, third) for third in range(3)))
+
+
+def put(*refs):
+    def store(t, total):
+        refs[t][...] = total.astype(refs[t].dtype)
+
+    return store
 
 
 def first_kernel(mask, table_ref, got_ref, placer_ref, slab_ref, out_ref, coef_ref, *work):
     place(block_of(mask), got_ref, placer_ref, coef_ref)
-    for t in range(2):
-        out_ref[t] = entries(table_ref, coef_ref, slab_ref[t], *work[2 * t : 2 * t + 2]).astype(BF16)
+    entries(table_ref, coef_ref, slab_ref, put(out_ref.at[0], out_ref.at[1]), *work)
 
 
 def second_kernel(table_ref, coef_ref, slab_ref, out_ref, *work):
-    for t in range(2):
-        out_ref[t] = entries(table_ref, coef_ref, slab_ref[t], *work[2 * t : 2 * t + 2])
+    entries(table_ref, coef_ref, slab_ref, put(out_ref.at[0], out_ref.at[1]), *work)
 
 
 def pair_kernel(own_ref, other_ref, out_a_ref, out_b_ref):
@@ -224,10 +252,8 @@
 
 def last_kernel(table_ref, got_ref, placer_ref, far_ref, near_ref, before_ref, part_a_ref, part_b_ref, own_ref, coef_ref, *work):
     place(block_of(0), got_ref, placer_ref, coef_ref)
-    for t, part_ref in enumerate((part_a_ref, part_b_ref)):
-        part_ref[...] = entries(table_ref, coef_ref, far_ref[t], *work[2 * t : 2 * t + 2]).astype(BF16)
-    for t in range(2):
-        own_ref[t] = entries(table_ref, coef_ref, near_ref[t], *work[2 * t : 2 * t + 2])
+    entries(table_ref, coef_ref, far_ref, put(part_a_ref, part_b_ref), *work)
+    entries(table_ref, coef_ref, near_ref, put(own_ref.at[0], own_ref.at[1]), *work)
 
 
 def total_kernel(own_ref, near_a_ref, near_b_ref, far_a_ref, far_b_ref, out_ref, total_ref, sems):
@@ -275,42 +301,42 @@
     first = lax.all_to_all(
         packed.reshape(PLANES, 32, 2 * WIDTH), "mode", 0, 0, tiled=True, axis_index_groups=Z_GROUPS
     )
+    slab_shape = shape((2, 2 * WIDTH, COLS))
+    token = shape((16, 128))
+
+    def sort(mask, limit, *after):
+        return kernel_call(
+            functools.partial(sort_kernel, mask),
+            (slab_shape, slab_shape, token),
+            [HBM] * (1 + len(after)),
+            5_000_000,
+            6_000_000,
+            [pltpu.VMEM((2 * WIDTH, 4 * COLS), BF16), DMA((4,)), DMA],
+            limit=limit,
+            out_specs=(VMEM, VMEM, HBM),
+        )(basis.reshape(2, 2 * WIDTH, 4 * COLS), *after)
+
+    slab_3, slab_2, done = sort(2, 52)
+    onward = kernel_call(
+        forward_kernel,
+        shape((SPOTS, STOPW * 16, 2 * WIDTH)),
+        [VMEM, HBM],
+        70_000_000,
+        1_200_000,
+        [pltpu.VMEM(((SPOTS + STOPW - 1) * 16, 2 * WIDTH), BF16), DMA((SPOTS,))],
+        out_specs=HBM,
+    )(first.reshape(PLANES * 32, 2 * WIDTH), done)
     by_reader = route.reshape(PLANES, SPOTS, ITEMS).transpose(2, 1, 0).reshape(ITEMS, 64)
     by_reader = jnp.repeat(by_reader, 2, axis=1)
     placer, table = kernel_call(
         tables_kernel,
         (shape((2, STOPW, MODES, CAND)), shape((OPS * 14, 128), F32)),
-        [SMEM, SMEM, VMEM],
+        [SMEM, SMEM, VMEM, HBM],
         2_000_000,
         200_000,
-    )(momenta, gammas, by_reader)
-    slab_shape = shape((2, 2 * WIDTH, COLS))
-    token = shape((16, 128))
-
-    def sort(mask, after, limit):
-        return kernel_call(
-            functools.partial(sort_kernel, mask),
-            (slab_shape, slab_shape, token),
-            [HBM, HBM],
-            5_000_000,
-            6_000_000,
-            [pltpu.VMEM((2 * WIDTH, 4 * COLS), BF16), DMA((4,)), DMA],
-            limit=limit,
-            out_specs=(VMEM, VMEM, HBM),
-        )(basis.reshape(2, 2 * WIDTH, 4 * COLS), after)
-
-    slab_3, slab_2, done = sort(2, table, 52)
-    onward = kernel_call(
-        forward_kernel,
-        shape((SPOTS, STOPW * 16, 2 * WIDTH)),
-        [VMEM, HBM, VMEM],
-        70_000_000,
-        1_200_000,
-        [pltpu.VMEM(((SPOTS + STOPW - 1) * 16, 2 * WIDTH), BF16), DMA((SPOTS,))],
-        out_specs=HBM,
-    )(first.reshape(PLANES * 32, 2 * WIDTH), done, table)
+    )(momenta, gammas, by_reader, onward)
     got = lax.all_to_all(onward, "mode", 0, 0, tiled=True, axis_index_groups=P_GROUPS)
-    slab_1, slab_0, _ = sort(0, onward, 59)
+    slab_1, slab_0, _ = sort(0, 59, onward)
     got, slab_1, slab_0 = lax.optimization_barrier((got, slab_1, slab_0))
     part_shape = shape((ROWS, 256))
     pair_shape = shape((2, ROWS, 256))

time: 57.8 us -> 56.2 us (0.972)
  waiting for transfers between devices: 10.3 us -> 12.4 us
  local copies, waits for them, and re-layouts: 2.25 us -> 0.2 us
  Pallas kernels: 21.6 us -> 20.2 us
    all_to_all x1, waiting for transfers between devices: 3.71 us -> 6.73 us  [per_device(): lax.all_to_all(packed.reshape(PLANES, 32, 2 * WIDTH), 'mode', 0, 0, tiled...]
    unnamed x10 -> x12, local copies, waits for them, and re-layouts: 1.36 us -> 0.04 us
    all_to_all x1, waiting for transfers between devices: 5.4 us -> 4.38 us  [per_device(): lax.all_to_all(onward, 'mode', 0, 0, tiled=True, axis_index_groups=P_GROUPS)]
    reshape x1, local copies, waits for them, and re-layouts: 0.79 us -> 0.07 us  [per_device(): route.reshape(PLANES, SPOTS, ITEMS).transpose(2, 1, 0).reshape(ITEMS, 64)]
  transfers between devices with their start and end apart: 7 -> 7, of which waited for: 5 -> 3; matrix products, arithmetic and copies ran while one was open for 2% -> 0% of each run, Pallas kernels for 26% -> 24%
where the time goes in v4:
time: 56.2 us; the launch traced here: 55.9 us
  starting transfers between devices  23 us (41%)
  Pallas kernels  20.2 us (36%)
  waiting for transfers between devices  12.4 us (22%)
    all_to_all x1, starting transfers between devices, per_device(): lax.all_to_all(packed.reshape(PLANES, 32, 2 * WIDTH), 'mode', 0, 0, tiled...  9.01 us
    ppermute x5, starting transfers between devices, between(): return lax.ppermute(part, 'space', [(i, i ^ pair) for i in range(4)])  8.9 us
    pallas_call x2, Pallas kernels, sort(): kernel_call(functools.partial(sort_kernel, mask), (slab_shape, slab_shape...  7.81 us
    all_to_all x1, waiting for transfers between devices, per_device(): lax.all_to_all(packed.reshape(PLANES, 32, 2 * WIDTH), 'mode', 0, 0, tiled...  6.73 us
    all_to_all x1, starting transfers between devices, per_device(): lax.all_to_all(onward, 'mode', 0, 0, tiled=True, axis_index_groups=P_GROUPS)  5.13 us
    all_to_all x1, waiting for transfers between devices, per_device(): lax.all_to_all(onward, 'mode', 0, 0, tiled=True, axis_index_groups=P_GROUPS)  4.38 us
    pallas_call x1, Pallas kernels, per_device(): kernel_call(last_kernel, (part_shape, part_shape, wide_shape), [VMEM] * 6...  3.36 us
    pallas_call x1, Pallas kernels, per_device(): kernel_call(pack_kernel, shape((PLANES * 32, 2 * WIDTH)), [VMEM] * 3, 200...  1.93 us
  transfers between devices with their start and end apart: 7, of which 3 were waited for; matrix products, arithmetic and copies ran while one was open for 0% of the time, Pallas kernels for 24%

profile of v4, /device:TPU:1, one launch (start us, length us, event | category | flops | bytes accessed | tf_op | source)
XLA Modules:
  0.0 55.9 jit_solution(13717857513448652093)
XLA Ops:
  0.0 1.9 %shard_map.64 = bf16[256,512]{1,0:T(8,128)(2,1)} custom-call(s32[32,128]{1,0:T(8,128)} %bitcast.19, bf16[64,2,256]{2,1,0:T(2,128)(2,1)} %bitcast.18, s32[1,64]{1,0:T(1,128)} %bitcast.20), custom_call_target="tpu_custom_call" | custom-call | flops 20000000 | bytes 400000 | tf_op jit(solution)/shard_map/pallas_call | solution.py:298
  1.9 9.0 %all-to-all-start = ((bf16[8,32,512]{2,1,0:T(8,128)(2,1)}), bf16[8,32,512]{2,1,0:T(8,128)(2,1)S(1)}, u32[]{:S(2)}, u32[]{:S(2)}) async-start(bf16[8,32,512]{2,1,0:T(8,128)(2,1)} %bitcast.14), calls=%async_computation | async-start | bytes 524288 | tf_op jit(solution)/shard_map/all_to_all | solution.py:301
  10.9 3.6 %shard_map.65 = (bf16[2,512,768]{2,1,0:T(8,128)(2,1)S(1)}, bf16[2,512,768]{2,1,0:T(8,128)(2,1)}, bf16[16,128]{1,0:T(8,128)(2,1)S(1)}) custom-call(bf16[2,512,3072]{2,1,0:T(8,128)(2,1)} %bitcast.12), custom_call_target="tpu_custom_call" | custom-call | flops 5000000 | bytes 6000000 | tf_op jit(solution)/shard_map/pallas_call | solution.py:308
  14.6 0.0 copy-start.5
  14.6 6.7 %all-to-all-done = bf16[8,32,512]{2,1,0:T(8,128)(2,1)S(1)} async-done(((bf16[8,32,512]{2,1,0:T(8,128)(2,1)}), bf16[8,32,512]{2,1,0:T(8,128)(2,1)S(1)}, u32[]{:S(2)}, u32[]{:S(2)}) %all-to-all-start) | async-done | bytes 262176 | tf_op jit(solution)/shard_map/all_to_all | solution.py:301
  21.3 0.0 copy-start
  21.3 0.0 copy-start.1
  21.3 1.2 %shard_map.66.after_ref.rest_0_ = bf16[8,112,512]{2,1,0:T(8,128)(2,1)} custom-call(bf16[256,512]{1,0:T(8,128)(2,1)S(1)} %bitcast.11, bf16[16,128]{1,0:T(8,128)(2,1)S(1)} %get-tuple-element.25.done_ref), custom_call_target="tpu_custom_call" | custom-call | flops 70000000 | bytes 1200000 | tf_op jit(solution)/shard_map/pallas_call | solution.py:320
  22.6 5.1 %all-to-all-start.1 = ((bf16[8,112,512]{2,1,0:T(8,128)(2,1)}), bf16[8,112,512]{2,1,0:T(8,128)(2,1)S(1)}, u32[]{:S(2)}, u32[]{:S(2)}) async-start(bf16[8,112,512]{2,1,0:T(8,128)(2,1)} %shard_map.66.after_ref.rest_0_), calls=%async_computation.1 | async-start | bytes 1835008 | tf_op jit(solution)/shard_map/all_to_all | solution.py:338
  27.7 0.0 copy-done.5
  27.7 0.1 reshape.28
  27.8 0.1 copy.8.route_ref
  27.9 0.0 copy-done
  27.9 0.0 copy-done.1
  27.9 0.8 %shard_map.67 = (bf16[2,7,32,128]{3,2,1,0:T(8,128)(2,1)S(1)}, f32[56,128]{1,0:T(8,128)S(1)}) custom-call(s32[4,3]{1,0:T(4,128)S(1)} %copy-done, s32[4]{0:T(128)S(1)} %copy-done.1, s32[64,128]{1,0:T(8,128)S(1)} %copy.8.route_ref, bf16[8,112,512]{2,1,0:T(8,128)(2,1)} %shard_map.66.after_ref.rest_0_), custom_call_target="tpu_custom_call" | custom-call | flops 2000000 | bytes 200000 | tf_op jit(solution)/shard_map/pallas_call | solution.py:331
  28.7 4.2 %shard_map.68 = (bf16[2,512,768]{2,1,0:T(8,128)(2,1)}, bf16[2,512,768]{2,1,0:T(8,128)(2,1)}, bf16[16,128]{1,0:T(8,128)(2,1)}) custom-call(bf16[2,512,3072]{2,1,0:T(8,128)(2,1)} %bitcast.13, bf16[8,112,512]{2,1,0:T(8,128)(2,1)} %shard_map.66.after_ref.rest_0_), custom_call_target="tpu_custom_call" | custom-call | flops 5000000 | bytes 6000000 | tf_op jit(solution)/shard_map/pallas_call | solution.py:308
  32.9 4.4 %all-to-all-done.1.got_ref = bf16[8,112,512]{2,1,0:T(8,128)(2,1)S(1)} async-done(((bf16[8,112,512]{2,1,0:T(8,128)(2,1)}), bf16[8,112,512]{2,1,0:T(8,128)(2,1)S(1)}, u32[]{:S(2)}, u32[]{:S(2)}) %all-to-all-start.1) | async-done | bytes 917536 | tf_op jit(solution)/shard_map/all_to_all | solution.py:338
  37.3 0.0 copy-start.2
  37.3 1.9 %shard_map.69 = (bf16[2,224,256]{2,1,0:T(8,128)(2,1)S(1)}, bf16[448,512]{1,0:T(8,128)(2,1)S(1)}) custom-call(f32[56,128]{1,0:T(8,128)S(1)} %get-tuple-element.26.table_ref, bf16[8,112,512]{2,1,0:T(8,128)(2,1)S(1)} %all-to-all-done.1.got_ref, bf16[2,7,32,128]{3,2,1,0:T(8,128)(2,1)S(1)} %get-tuple-element.30.placer_ref, ...), custom_call_target="tpu_custom_call" | custom-call | flops 1200000000 | bytes 3000000 | tf_op jit(solution)/shard_map/pallas_call | solution.py:350
  39.2 5.0 %collective-permute-start = (bf16[2,224,256]{2,1,0:T(8,128)(2,1)S(1)}, bf16[2,224,256]{2,1,0:T(8,128)(2,1)S(1)}, u32[]{:S(2)}, u32[]{:S(2)}) collective-permute-start(bf16[2,224,256]{2,1,0:T(8,128)(2,1)S(1)} %get-tuple-element.36), channel_id=1, source_target_pairs={{0,1},{1,0},{2,3},{3,2},{4,5},{5,4},{6,7},{7,6},{8,9},{9,8},{10,11... | collective-permute-start | bytes 688136 | tf_op jit(solution)/shard_map/ppermute | solution.py:348
  44.2 0.0 copy-done.2
  44.2 0.0 copy-start.3
  44.2 0.0 copy-start.4
  44.2 1.8 %shard_map.70.own_ref = f32[2,224,256]{2,1,0:T(8,128)S(1)} custom-call(f32[56,128]{1,0:T(8,128)S(1)} %get-tuple-element.26.table_ref, bf16[448,512]{1,0:T(8,128)(2,1)S(1)} %get-tuple-element.34.coef_ref, bf16[2,512,768]{2,1,0:T(8,128)(2,1)S(1)} %copy-done.2), custom_call_target="tpu_custom_call" | custom-call | flops 1100000000 | bytes 3000000 | tf_op jit(solution)/shard_map/pallas_call | solution.py:358
  46.0 0.0 collective-permute-done.other_ref
  46.1 2.5 %collective-permute-start.1 = (bf16[224,256]{1,0:T(8,128)(2,1)S(1)}, bf16[224,256]{1,0:T(8,128)(2,1)S(1)}, u32[]{:S(2)}, u32[]{:S(2)}) collective-permute-start(bf16[224,256]{1,0:T(8,128)(2,1)S(1)} %get-tuple-element.41), channel_id=1, source_target_pairs={{0,2},{1,3},{2,0},{3,1},{4,6},{5,7},{6,4},{7,5},{8,10},{9,11},{10,... | collective-permute-start | bytes 344072 | tf_op jit(solution)/shard_map/ppermute | solution.py:348
  48.6 0.5 collective-permute-start.4
  49.1 0.0 copy-done.3
  49.1 0.0 copy-done.4
  49.1 3.4 %shard_map.72 = (bf16[224,256]{1,0:T(8,128)(2,1)S(1)}, bf16[224,256]{1,0:T(8,128)(2,1)S(1)}, f32[2,224,256]{2,1,0:T(8,128)S(1)}) custom-call(f32[56,128]{1,0:T(8,128)S(1)} %get-tuple-element.26.table_ref, bf16[8,112,512]{2,1,0:T(8,128)(2,1)S(1)} %all-to-all-done.1.got_ref, bf16[2,7,32,128]{3,2,1,0:T(8,128)(2,1)S(1)} %get-tuple-element.30.placer_ref, ...), custom_call_target="tpu_custom_call" | custom-call | flops 2200000000 | bytes 6000000 | tf_op jit(solution)/shard_map/pallas_call | solution.py:364
  52.5 0.0 collective-permute-done.1.far_a_ref
  52.5 0.7 %collective-permute-start.2 = (bf16[224,256]{1,0:T(8,128)(2,1)S(1)}, bf16[224,256]{1,0:T(8,128)(2,1)S(1)}, u32[]{:S(2)}, u32[]{:S(2)}) collective-permute-start(bf16[224,256]{1,0:T(8,128)(2,1)S(1)} %get-tuple-element.42), channel_id=1, source_target_pairs={{0,1},{1,0},{2,3},{3,2},{4,5},{5,4},{6,7},{7,6},{8,9},{9,8},{10,11... | collective-permute-start | bytes 344072 | tf_op jit(solution)/shard_map/ppermute | solution.py:348
  53.2 0.1 collective-permute-start.3
  53.3 1.2 %collective-permute-done.4.far_b_ref = bf16[224,256]{1,0:T(8,128)(2,1)S(1)} collective-permute-done((bf16[224,256]{1,0:T(8,128)(2,1)S(1)}, bf16[224,256]{1,0:T(8,128)(2,1)S(1)}, u32[]{:S(2)}, u32[]{:S(2)}) %collective-permute-start.4) | collective-permute-done | bytes 114720 | tf_op jit(solution)/shard_map/ppermute | solution.py:348
  54.6 0.0 collective-permute-done.2.near_a_ref
  54.6 0.0 collective-permute-done.3.near_b_ref
  54.6 1.3 %shard_map.73 = f32[2,4,2,7,32,32]{5,4,3,2,1,0:T(8,128)} custom-call(f32[2,224,256]{2,1,0:T(8,128)S(1)} %get-tuple-element.38.own_ref, bf16[224,256]{1,0:T(8,128)(2,1)S(1)} %collective-permute-done.2.near_a_ref, bf16[224,256]{1,0:T(8,128)(2,1)S(1)} %collective-permute-done.3.near_b_ref, bf16[224,256]{1,0:T(8,128)(2,1)S(1)} %collective-permute-done.1.far_a_ref, ...), custom_call_target="tpu_custom_call" | custom-call | flops 1000000 | bytes 3000000 | tf_op jit(solution)/shard_map/pallas_call | solution.py:375
  (3 shorter events, 0.1 us)
Async XLA Ops:
  1.9 19.4 %all-to-all-start = ((bf16[8,32,512]{2,1,0:T(8,128)(2,1)}), bf16[8,32,512]{2,1,0:T(8,128)(2,1)S(1)}, u32[]{:S(2)}, u32[]{:S(2)}) async-start(bf16[8,32,512]{2,1,0:T(8,128)(2,1)} %bitcast.14), calls=%async_computation | async-start | bytes 524288 | tf_op jit(solution)/shard_map/all_to_all | solution.py:301
  14.6 13.1 %copy-start.5 = (s32[4096]{0:T(1024)S(1)}, s32[4096]{0:T(1024)}, u32[]{:S(2)}) copy-start(s32[4096]{0:T(1024)} %param.8) | copy-start | bytes 49156
  21.3 6.6 %copy-start = (s32[4,3]{1,0:T(4,128)S(1)}, s32[4,3]{1,0:T(4,128)}, u32[]{:S(2)}) copy-start(s32[4,3]{1,0:T(4,128)} %momenta_ref.1) | copy-start | bytes 148
  21.3 6.6 %copy-start.1 = (s32[4]{0:T(128)S(1)}, s32[4]{0:T(128)}, u32[]{:S(2)}) copy-start(s32[4]{0:T(128)} %gammas_ref.1) | copy-start | bytes 52
  22.6 14.7 %all-to-all-start.1 = ((bf16[8,112,512]{2,1,0:T(8,128)(2,1)}), bf16[8,112,512]{2,1,0:T(8,128)(2,1)S(1)}, u32[]{:S(2)}, u32[]{:S(2)}) async-start(bf16[8,112,512]{2,1,0:T(8,128)(2,1)} %shard_map.66.after_ref.rest_0_), calls=%async_computation.1 | async-start | bytes 1835008 | tf_op jit(solution)/shard_map/all_to_all | solution.py:338
  37.3 7.0 %copy-start.2 = (bf16[2,512,768]{2,1,0:T(8,128)(2,1)S(1)}, bf16[2,512,768]{2,1,0:T(8,128)(2,1)}, u32[]{:S(2)}) copy-start(bf16[2,512,768]{2,1,0:T(8,128)(2,1)} %get-tuple-element.35.slab_ref) | copy-start | bytes 4718596
  39.2 6.8 %collective-permute-start = (bf16[2,224,256]{2,1,0:T(8,128)(2,1)S(1)}, bf16[2,224,256]{2,1,0:T(8,128)(2,1)S(1)}, u32[]{:S(2)}, u32[]{:S(2)}) collective-permute-start(bf16[2,224,256]{2,1,0:T(8,128)(2,1)S(1)} %get-tuple-element.36), channel_id=1, source_target_pairs={{0,1},{1,0},{2,3},{3,2},{4,5},{5,4},{6,7},{7,6},{8,9},{9,8},{10,11... | collective-permute-start | bytes 688136 | tf_op jit(solution)/shard_map/ppermute | solution.py:348
  44.2 4.9 %copy-start.3 = (bf16[2,512,768]{2,1,0:T(8,128)(2,1)S(1)}, bf16[2,512,768]{2,1,0:T(8,128)(2,1)}, u32[]{:S(2)}) copy-start(bf16[2,512,768]{2,1,0:T(8,128)(2,1)} %get-tuple-element.31.far_ref) | copy-start | bytes 4718596
  44.2 4.9 %copy-start.4 = (bf16[2,512,768]{2,1,0:T(8,128)(2,1)S(1)}, bf16[2,512,768]{2,1,0:T(8,128)(2,1)}, u32[]{:S(2)}) copy-start(bf16[2,512,768]{2,1,0:T(8,128)(2,1)} %get-tuple-element.32.near_ref) | copy-start | bytes 4718596
  46.1 6.4 %collective-permute-start.1 = (bf16[224,256]{1,0:T(8,128)(2,1)S(1)}, bf16[224,256]{1,0:T(8,128)(2,1)S(1)}, u32[]{:S(2)}, u32[]{:S(2)}) collective-permute-start(bf16[224,256]{1,0:T(8,128)(2,1)S(1)} %get-tuple-element.41), channel_id=1, source_target_pairs={{0,2},{1,3},{2,0},{3,1},{4,6},{5,7},{6,4},{7,5},{8,10},{9,11},{10,... | collective-permute-start | bytes 344072 | tf_op jit(solution)/shard_map/ppermute | solution.py:348
  48.6 6.0 %collective-permute-start.4 = (bf16[224,256]{1,0:T(8,128)(2,1)S(1)}, bf16[224,256]{1,0:T(8,128)(2,1)S(1)}, u32[]{:S(2)}, u32[]{:S(2)}) collective-permute-start(bf16[224,256]{1,0:T(8,128)(2,1)S(1)} %get-tuple-element.37.before_ref), channel_id=1, source_target_pairs={{0,2},{1,3},{2,0},{3,1},{4,6},{5,7},{6,4},{7,5},{8,10},{9,11},{10,... | collective-permute-start | bytes 344072 | tf_op jit(solution)/shard_map/ppermute | solution.py:348
  52.5 2.0 %collective-permute-start.2 = (bf16[224,256]{1,0:T(8,128)(2,1)S(1)}, bf16[224,256]{1,0:T(8,128)(2,1)S(1)}, u32[]{:S(2)}, u32[]{:S(2)}) collective-permute-start(bf16[224,256]{1,0:T(8,128)(2,1)S(1)} %get-tuple-element.42), channel_id=1, source_target_pairs={{0,1},{1,0},{2,3},{3,2},{4,5},{5,4},{6,7},{7,6},{8,9},{9,8},{10,11... | collective-permute-start | bytes 344072 | tf_op jit(solution)/shard_map/ppermute | solution.py:348
  53.2 1.3 %collective-permute-start.3 = (bf16[224,256]{1,0:T(8,128)(2,1)S(1)}, bf16[224,256]{1,0:T(8,128)(2,1)S(1)}, u32[]{:S(2)}, u32[]{:S(2)}) collective-permute-start(bf16[224,256]{1,0:T(8,128)(2,1)S(1)} %get-tuple-element.43), channel_id=1, source_target_pairs={{0,1},{1,0},{2,3},{3,2},{4,5},{5,4},{6,7},{7,6},{8,9},{9,8},{10,11... | collective-permute-start | bytes 344072 | tf_op jit(solution)/shard_map/ppermute | solution.py:348

commit v5 on v4

--- a/solution.py
+++ b/solution.py
@@ -30,7 +30,16 @@
     return lax.broadcasted_iota(jnp.int32, shape, axis)
 
 
-def pack_kernel(route_ref, coefs_ref, counts_ref, out_ref):
+def pack_kernel(route_in, coefs_in, counts_in, out_hbm, route_ref, coefs_ref, counts_ref, out_ref, sems, out_sems):
+    reads = [
+        pltpu.make_async_copy(source, target, sems.at[n])
+        for n, (source, target) in enumerate(
+            ((route_in, route_ref), (counts_in, counts_ref), (coefs_in, coefs_ref))
+        )
+    ]
+    for read in reads:
+        read.start()
+    reads[0].wait()
     me = lax.axis_index("mode")
     row = route_ref[pl.ds(me // 2, 1), :]
     row = jnp.where(me % 2 == 1, pltpu.roll(row, 64, 1), row)[:, :ITEMS]
@@ -46,13 +55,23 @@
     plane = (lax.shift_right_logical(q, 5) - (lax.shift_right_logical(q, 4) & 1)) & 7
     want = plane * 16 + (q & 15)
     outgoing = jnp.where(want == target, 1.0, 0.0).astype(BF16)
+    reads[1].wait()
     counts = jnp.broadcast_to(counts_ref[...], (ITEMS, ITEMS)).astype(F32)
     limit = jnp.sum(jnp.where(i == j, counts, 0.0), axis=1, keepdims=True).astype(jnp.int32)
     keep = iota((ITEMS, WIDTH), 1) < limit
-    for part in range(2):
-        block = jnp.where(keep, coefs_ref[:, part, :].astype(F32), 0.0).astype(BF16)
-        packed = jnp.dot(outgoing, block, preferred_element_type=F32)
-        out_ref[:, part * WIDTH : (part + 1) * WIDTH] = packed.astype(BF16)
+    reads[2].wait()
+    blocks = [jnp.where(keep, coefs_ref[:, part, :].astype(F32), 0.0).astype(BF16) for part in range(2)]
+    writes = []
+    for half in range(2):
+        rows = slice(half * 128, (half + 1) * 128)
+        for part in range(2):
+            packed = jnp.dot(outgoing[rows], blocks[part], preferred_element_type=F32)
+            out_ref[rows, part * WIDTH : (part + 1) * WIDTH] = packed.astype(BF16)
+        write = pltpu.make_async_copy(out_ref.at[rows], out_hbm.at[rows], out_sems.at[half])
+        write.start()
+        writes.append(write)
+    for write in writes:
+        write.wait()
 
 
 def forward_kernel(got_ref, done_ref, out_ref, sorted_ref, sems):
@@ -122,6 +141,7 @@
 
 def sort_kernel(mask, basis_ref, *rest):
     far_ref, near_ref, done_ref, reads_ref, in_sems, done_sem = rest[-6:]
+    odd_far_ref, odd_near_ref = (near_ref, far_ref) if mask == 2 else (far_ref, near_ref)
     step = 128
     chunks = 2 * WIDTH // step
     low = iota((step, 128), 1) < 64
@@ -139,14 +159,14 @@
             done = pltpu.make_async_copy(reads_ref.at[:16, :128], done_ref, done_sem)
             done.start()
         rows = slice(chunk * step, (chunk + 1) * step)
-        for out_ref, half in ((far_ref, 1 - core), (near_ref, core)):
+        for even_ref, odd_ref, half in ((far_ref, odd_far_ref, 1 - core), (near_ref, odd_near_ref, core)):
             for group, (first, second) in enumerate(PAIRS):
                 lanes = slice(group * 128, (group + 1) * 128)
                 at = pl.multiple_of(half * 128, 128)
                 a = reads_ref[rows, pl.ds(first * 256 + at, 128)]
                 b = reads_ref[rows, pl.ds(second * 256 + at, 128)]
-                out_ref[0, rows, lanes] = jnp.where(low, a, pltpu.roll(b, 64, 1))
-                out_ref[1, rows, lanes] = jnp.where(low, pltpu.roll(a, 64, 1), b)
+                even_ref[0, rows, lanes] = jnp.where(low, a, pltpu.roll(b, 64, 1))
+                odd_ref[1, rows, lanes] = jnp.where(low, pltpu.roll(a, 64, 1), b)
     done.wait()
 
 
@@ -296,7 +316,21 @@
 
 def per_device(coefs, counts, route, basis, momenta, gammas):
     packed = kernel_call(
-        pack_kernel, shape((PLANES * 32, 2 * WIDTH)), [VMEM] * 3, 20_000_000, 400_000, limit=60
+        pack_kernel,
+        shape((PLANES * 32, 2 * WIDTH)),
+        [HBM] * 3,
+        20_000_000,
+        400_000,
+        [
+            pltpu.VMEM((32, 128), jnp.int32),
+            pltpu.VMEM((ITEMS, 2, WIDTH), BF16),
+            pltpu.VMEM((1, ITEMS), jnp.int32),
+            pltpu.VMEM((PLANES * 32, 2 * WIDTH), BF16),
+            DMA((3,)),
+            DMA((2,)),
+        ],
+        limit=60,
+        out_specs=HBM,
     )(route.reshape(32, 128), coefs.reshape(ITEMS, 2, WIDTH), counts.reshape(1, ITEMS))
     first = lax.all_to_all(
         packed.reshape(PLANES, 32, 2 * WIDTH), "mode", 0, 0, tiled=True, axis_index_groups=Z_GROUPS
@@ -360,7 +394,7 @@
         part_2, between(1, part_3)
     )
     far_a = between(2, chip_a)
-    far_b = between(2, chip_b)
+    far_b = between(3, chip_b)
     part_a, part_b, own = kernel_call(
         last_kernel,
         (part_shape, part_shape, wide_shape),

time: 56.2 us -> 56.9 us (1.012)
  waiting for transfers between devices: 12.4 us -> 13 us
    ppermute x5, waiting for transfers between devices: 1.25 us -> 1.88 us  [between(): return lax.ppermute(part, 'space', [(i, i ^ pair) for i in range(4)])]
where the time goes in v5:
time: 56.9 us; the launch traced here: 56.6 us
  starting transfers between devices  23.1 us (41%)
  Pallas kernels  20.2 us (36%)
  waiting for transfers between devices  13 us (23%)
    all_to_all x1, starting transfers between devices, per_device(): lax.all_to_all(packed.reshape(PLANES, 32, 2 * WIDTH), 'mode', 0, 0, tiled...  9.03 us
    ppermute x5, starting transfers between devices, between(): return lax.ppermute(part, 'space', [(i, i ^ pair) for i in range(4)])  8.9 us
    pallas_call x2, Pallas kernels, sort(): kernel_call(functools.partial(sort_kernel, mask), (slab_shape, slab_shape...  7.81 us
    all_to_all x1, waiting for transfers between devices, per_device(): lax.all_to_all(packed.reshape(PLANES, 32, 2 * WIDTH), 'mode', 0, 0, tiled...  6.73 us
    all_to_all x1, starting transfers between devices, per_device(): lax.all_to_all(onward, 'mode', 0, 0, tiled=True, axis_index_groups=P_GROUPS)  5.13 us
    all_to_all x1, waiting for transfers between devices, per_device(): lax.all_to_all(onward, 'mode', 0, 0, tiled=True, axis_index_groups=P_GROUPS)  4.4 us
    pallas_call x1, Pallas kernels, per_device(): kernel_call(last_kernel, (part_shape, part_shape, wide_shape), [VMEM] * 6...  3.37 us
    pallas_call x1, Pallas kernels, per_device(): kernel_call(pack_kernel, shape((PLANES * 32, 2 * WIDTH)), [HBM] * 3, 2000...  1.98 us
  transfers between devices with their start and end apart: 7, of which 3 were waited for; matrix products, arithmetic and copies ran while one was open for 0% of the time, Pallas kernels for 24%

profile of v5, /device:TPU:1, one launch (start us, length us, event | category | flops | bytes accessed | tf_op | source)
XLA Modules:
  0.0 56.6 jit_solution(8078831787937233759)
XLA Ops:
  0.0 2.0 %shard_map.64 = bf16[256,512]{1,0:T(8,128)(2,1)} custom-call(s32[32,128]{1,0:T(8,128)} %bitcast.19, bf16[64,2,256]{2,1,0:T(2,128)(2,1)} %bitcast.18, s32[1,64]{1,0:T(1,128)} %bitcast.20), custom_call_target="tpu_custom_call" | custom-call | flops 20000000 | bytes 400000 | tf_op jit(solution)/shard_map/pallas_call | solution.py:318
  2.0 9.0 %all-to-all-start = ((bf16[8,32,512]{2,1,0:T(8,128)(2,1)}), bf16[8,32,512]{2,1,0:T(8,128)(2,1)S(1)}, u32[]{:S(2)}, u32[]{:S(2)}) async-start(bf16[8,32,512]{2,1,0:T(8,128)(2,1)} %bitcast.14), calls=%async_computation | async-start | bytes 524288 | tf_op jit(solution)/shard_map/all_to_all | solution.py:335
  11.0 3.6 %shard_map.65 = (bf16[2,512,768]{2,1,0:T(8,128)(2,1)S(1)}, bf16[2,512,768]{2,1,0:T(8,128)(2,1)}, bf16[16,128]{1,0:T(8,128)(2,1)S(1)}) custom-call(bf16[2,512,3072]{2,1,0:T(8,128)(2,1)} %bitcast.12), custom_call_target="tpu_custom_call" | custom-call | flops 5000000 | bytes 6000000 | tf_op jit(solution)/shard_map/pallas_call | solution.py:342
  14.7 0.0 copy-start.5
  14.7 6.7 %all-to-all-done = bf16[8,32,512]{2,1,0:T(8,128)(2,1)S(1)} async-done(((bf16[8,32,512]{2,1,0:T(8,128)(2,1)}), bf16[8,32,512]{2,1,0:T(8,128)(2,1)S(1)}, u32[]{:S(2)}, u32[]{:S(2)}) %all-to-all-start) | async-done | bytes 262176 | tf_op jit(solution)/shard_map/all_to_all | solution.py:335
  21.4 0.0 copy-start
  21.4 0.0 copy-start.1
  21.4 1.2 %shard_map.66.after_ref.rest_0_ = bf16[8,112,512]{2,1,0:T(8,128)(2,1)} custom-call(bf16[256,512]{1,0:T(8,128)(2,1)S(1)} %bitcast.11, bf16[16,128]{1,0:T(8,128)(2,1)S(1)} %get-tuple-element.25.done_ref), custom_call_target="tpu_custom_call" | custom-call | flops 70000000 | bytes 1200000 | tf_op jit(solution)/shard_map/pallas_call | solution.py:354
  22.7 5.1 %all-to-all-start.1 = ((bf16[8,112,512]{2,1,0:T(8,128)(2,1)}), bf16[8,112,512]{2,1,0:T(8,128)(2,1)S(1)}, u32[]{:S(2)}, u32[]{:S(2)}) async-start(bf16[8,112,512]{2,1,0:T(8,128)(2,1)} %shard_map.66.after_ref.rest_0_), calls=%async_computation.1 | async-start | bytes 1835008 | tf_op jit(solution)/shard_map/all_to_all | solution.py:372
  27.8 0.0 copy-done.5
  27.8 0.1 reshape.28
  27.9 0.1 copy.8.route_ref
  28.0 0.0 copy-done
  28.0 0.0 copy-done.1
  28.0 0.8 %shard_map.67 = (bf16[2,7,32,128]{3,2,1,0:T(8,128)(2,1)S(1)}, f32[56,128]{1,0:T(8,128)S(1)}) custom-call(s32[4,3]{1,0:T(4,128)S(1)} %copy-done, s32[4]{0:T(128)S(1)} %copy-done.1, s32[64,128]{1,0:T(8,128)S(1)} %copy.8.route_ref, bf16[8,112,512]{2,1,0:T(8,128)(2,1)} %shard_map.66.after_ref.rest_0_), custom_call_target="tpu_custom_call" | custom-call | flops 2000000 | bytes 200000 | tf_op jit(solution)/shard_map/pallas_call | solution.py:365
  28.8 4.2 %shard_map.68 = (bf16[2,512,768]{2,1,0:T(8,128)(2,1)}, bf16[2,512,768]{2,1,0:T(8,128)(2,1)}, bf16[16,128]{1,0:T(8,128)(2,1)}) custom-call(bf16[2,512,3072]{2,1,0:T(8,128)(2,1)} %bitcast.13, bf16[8,112,512]{2,1,0:T(8,128)(2,1)} %shard_map.66.after_ref.rest_0_), custom_call_target="tpu_custom_call" | custom-call | flops 5000000 | bytes 6000000 | tf_op jit(solution)/shard_map/pallas_call | solution.py:342
  33.0 4.4 %all-to-all-done.1.got_ref = bf16[8,112,512]{2,1,0:T(8,128)(2,1)S(1)} async-done(((bf16[8,112,512]{2,1,0:T(8,128)(2,1)}), bf16[8,112,512]{2,1,0:T(8,128)(2,1)S(1)}, u32[]{:S(2)}, u32[]{:S(2)}) %all-to-all-start.1) | async-done | bytes 917536 | tf_op jit(solution)/shard_map/all_to_all | solution.py:372
  37.4 0.0 copy-start.2
  37.4 1.9 %shard_map.69 = (bf16[2,224,256]{2,1,0:T(8,128)(2,1)S(1)}, bf16[448,512]{1,0:T(8,128)(2,1)S(1)}) custom-call(f32[56,128]{1,0:T(8,128)S(1)} %get-tuple-element.26.table_ref, bf16[8,112,512]{2,1,0:T(8,128)(2,1)S(1)} %all-to-all-done.1.got_ref, bf16[2,7,32,128]{3,2,1,0:T(8,128)(2,1)S(1)} %get-tuple-element.30.placer_ref, ...), custom_call_target="tpu_custom_call" | custom-call | flops 1200000000 | bytes 3000000 | tf_op jit(solution)/shard_map/pallas_call | solution.py:384
  39.3 5.0 %collective-permute-start = (bf16[2,224,256]{2,1,0:T(8,128)(2,1)S(1)}, bf16[2,224,256]{2,1,0:T(8,128)(2,1)S(1)}, u32[]{:S(2)}, u32[]{:S(2)}) collective-permute-start(bf16[2,224,256]{2,1,0:T(8,128)(2,1)S(1)} %get-tuple-element.36), channel_id=1, source_target_pairs={{0,1},{1,0},{2,3},{3,2},{4,5},{5,4},{6,7},{7,6},{8,9},{9,8},{10,11... | collective-permute-start | bytes 688136 | tf_op jit(solution)/shard_map/ppermute | solution.py:382
  44.3 0.0 copy-done.2
  44.3 0.0 copy-start.3
  44.3 0.0 copy-start.4
  44.3 1.8 %shard_map.70.own_ref = f32[2,224,256]{2,1,0:T(8,128)S(1)} custom-call(f32[56,128]{1,0:T(8,128)S(1)} %get-tuple-element.26.table_ref, bf16[448,512]{1,0:T(8,128)(2,1)S(1)} %get-tuple-element.34.coef_ref, bf16[2,512,768]{2,1,0:T(8,128)(2,1)S(1)} %copy-done.2), custom_call_target="tpu_custom_call" | custom-call | flops 1100000000 | bytes 3000000 | tf_op jit(solution)/shard_map/pallas_call | solution.py:392
  46.1 0.0 collective-permute-done.other_ref
  46.1 2.5 %collective-permute-start.1 = (bf16[224,256]{1,0:T(8,128)(2,1)S(1)}, bf16[224,256]{1,0:T(8,128)(2,1)S(1)}, u32[]{:S(2)}, u32[]{:S(2)}) collective-permute-start(bf16[224,256]{1,0:T(8,128)(2,1)S(1)} %get-tuple-element.41), channel_id=1, source_target_pairs={{0,2},{1,3},{2,0},{3,1},{4,6},{5,7},{6,4},{7,5},{8,10},{9,11},{10,... | collective-permute-start | bytes 344072 | tf_op jit(solution)/shard_map/ppermute | solution.py:382
  48.7 0.8 %collective-permute-start.4 = (bf16[224,256]{1,0:T(8,128)(2,1)S(1)}, bf16[224,256]{1,0:T(8,128)(2,1)S(1)}, u32[]{:S(2)}, u32[]{:S(2)}) collective-permute-start(bf16[224,256]{1,0:T(8,128)(2,1)S(1)} %get-tuple-element.37.before_ref), channel_id=1, source_target_pairs={{0,3},{1,2},{2,1},{3,0},{4,7},{5,6},{6,5},{7,4},{8,11},{9,10},{10,... | collective-permute-start | bytes 344072 | tf_op jit(solution)/shard_map/ppermute | solution.py:382
  49.4 0.0 copy-done.3
  49.4 0.0 copy-done.4
  49.4 3.4 %shard_map.72 = (bf16[224,256]{1,0:T(8,128)(2,1)S(1)}, bf16[224,256]{1,0:T(8,128)(2,1)S(1)}, f32[2,224,256]{2,1,0:T(8,128)S(1)}) custom-call(f32[56,128]{1,0:T(8,128)S(1)} %get-tuple-element.26.table_ref, bf16[8,112,512]{2,1,0:T(8,128)(2,1)S(1)} %all-to-all-done.1.got_ref, bf16[2,7,32,128]{3,2,1,0:T(8,128)(2,1)S(1)} %get-tuple-element.30.placer_ref, ...), custom_call_target="tpu_custom_call" | custom-call | flops 2200000000 | bytes 6000000 | tf_op jit(solution)/shard_map/pallas_call | solution.py:398
  52.8 0.0 collective-permute-done.1.far_a_ref
  52.8 0.5 collective-permute-start.2
  53.3 0.1 collective-permute-start.3
  53.4 1.9 %collective-permute-done.4.far_b_ref = bf16[224,256]{1,0:T(8,128)(2,1)S(1)} collective-permute-done((bf16[224,256]{1,0:T(8,128)(2,1)S(1)}, bf16[224,256]{1,0:T(8,128)(2,1)S(1)}, u32[]{:S(2)}, u32[]{:S(2)}) %collective-permute-start.4) | collective-permute-done | bytes 114720 | tf_op jit(solution)/shard_map/ppermute | solution.py:382
  55.3 0.0 collective-permute-done.2.near_a_ref
  55.3 0.0 collective-permute-done.3.near_b_ref
  55.3 1.3 %shard_map.73 = f32[2,4,2,7,32,32]{5,4,3,2,1,0:T(8,128)} custom-call(f32[2,224,256]{2,1,0:T(8,128)S(1)} %get-tuple-element.38.own_ref, bf16[224,256]{1,0:T(8,128)(2,1)S(1)} %collective-permute-done.2.near_a_ref, bf16[224,256]{1,0:T(8,128)(2,1)S(1)} %collective-permute-done.3.near_b_ref, bf16[224,256]{1,0:T(8,128)(2,1)S(1)} %collective-permute-done.1.far_a_ref, ...), custom_call_target="tpu_custom_call" | custom-call | flops 1000000 | bytes 3000000 | tf_op jit(solution)/shard_map/pallas_call | solution.py:409
  (3 shorter events, 0.1 us)
Async XLA Ops:
  2.0 19.4 %all-to-all-start = ((bf16[8,32,512]{2,1,0:T(8,128)(2,1)}), bf16[8,32,512]{2,1,0:T(8,128)(2,1)S(1)}, u32[]{:S(2)}, u32[]{:S(2)}) async-start(bf16[8,32,512]{2,1,0:T(8,128)(2,1)} %bitcast.14), calls=%async_computation | async-start | bytes 524288 | tf_op jit(solution)/shard_map/all_to_all | solution.py:335
  14.7 13.1 %copy-start.5 = (s32[4096]{0:T(1024)S(1)}, s32[4096]{0:T(1024)}, u32[]{:S(2)}) copy-start(s32[4096]{0:T(1024)} %param.8) | copy-start | bytes 49156
  21.4 6.6 %copy-start = (s32[4,3]{1,0:T(4,128)S(1)}, s32[4,3]{1,0:T(4,128)}, u32[]{:S(2)}) copy-start(s32[4,3]{1,0:T(4,128)} %momenta_ref.1) | copy-start | bytes 148
  21.4 6.6 %copy-start.1 = (s32[4]{0:T(128)S(1)}, s32[4]{0:T(128)}, u32[]{:S(2)}) copy-start(s32[4]{0:T(128)} %gammas_ref.1) | copy-start | bytes 52
  22.7 14.7 %all-to-all-start.1 = ((bf16[8,112,512]{2,1,0:T(8,128)(2,1)}), bf16[8,112,512]{2,1,0:T(8,128)(2,1)S(1)}, u32[]{:S(2)}, u32[]{:S(2)}) async-start(bf16[8,112,512]{2,1,0:T(8,128)(2,1)} %shard_map.66.after_ref.rest_0_), calls=%async_computation.1 | async-start | bytes 1835008 | tf_op jit(solution)/shard_map/all_to_all | solution.py:372
  37.4 7.0 %copy-start.2 = (bf16[2,512,768]{2,1,0:T(8,128)(2,1)S(1)}, bf16[2,512,768]{2,1,0:T(8,128)(2,1)}, u32[]{:S(2)}) copy-start(bf16[2,512,768]{2,1,0:T(8,128)(2,1)} %get-tuple-element.35.slab_ref) | copy-start | bytes 4718596
  39.3 6.8 %collective-permute-start = (bf16[2,224,256]{2,1,0:T(8,128)(2,1)S(1)}, bf16[2,224,256]{2,1,0:T(8,128)(2,1)S(1)}, u32[]{:S(2)}, u32[]{:S(2)}) collective-permute-start(bf16[2,224,256]{2,1,0:T(8,128)(2,1)S(1)} %get-tuple-element.36), channel_id=1, source_target_pairs={{0,1},{1,0},{2,3},{3,2},{4,5},{5,4},{6,7},{7,6},{8,9},{9,8},{10,11... | collective-permute-start | bytes 688136 | tf_op jit(solution)/shard_map/ppermute | solution.py:382
  44.3 5.1 %copy-start.3 = (bf16[2,512,768]{2,1,0:T(8,128)(2,1)S(1)}, bf16[2,512,768]{2,1,0:T(8,128)(2,1)}, u32[]{:S(2)}) copy-start(bf16[2,512,768]{2,1,0:T(8,128)(2,1)} %get-tuple-element.31.far_ref) | copy-start | bytes 4718596
  44.3 5.1 %copy-start.4 = (bf16[2,512,768]{2,1,0:T(8,128)(2,1)S(1)}, bf16[2,512,768]{2,1,0:T(8,128)(2,1)}, u32[]{:S(2)}) copy-start(bf16[2,512,768]{2,1,0:T(8,128)(2,1)} %get-tuple-element.32.near_ref) | copy-start | bytes 4718596
  46.1 6.7 %collective-permute-start.1 = (bf16[224,256]{1,0:T(8,128)(2,1)S(1)}, bf16[224,256]{1,0:T(8,128)(2,1)S(1)}, u32[]{:S(2)}, u32[]{:S(2)}) collective-permute-start(bf16[224,256]{1,0:T(8,128)(2,1)S(1)} %get-tuple-element.41), channel_id=1, source_target_pairs={{0,2},{1,3},{2,0},{3,1},{4,6},{5,7},{6,4},{7,5},{8,10},{9,11},{10,... | collective-permute-start | bytes 344072 | tf_op jit(solution)/shard_map/ppermute | solution.py:382
  48.7 6.6 %collective-permute-start.4 = (bf16[224,256]{1,0:T(8,128)(2,1)S(1)}, bf16[224,256]{1,0:T(8,128)(2,1)S(1)}, u32[]{:S(2)}, u32[]{:S(2)}) collective-permute-start(bf16[224,256]{1,0:T(8,128)(2,1)S(1)} %get-tuple-element.37.before_ref), channel_id=1, source_target_pairs={{0,3},{1,2},{2,1},{3,0},{4,7},{5,6},{6,5},{7,4},{8,11},{9,10},{10,... | collective-permute-start | bytes 344072 | tf_op jit(solution)/shard_map/ppermute | solution.py:382
  52.8 2.5 %collective-permute-start.2 = (bf16[224,256]{1,0:T(8,128)(2,1)S(1)}, bf16[224,256]{1,0:T(8,128)(2,1)S(1)}, u32[]{:S(2)}, u32[]{:S(2)}) collective-permute-start(bf16[224,256]{1,0:T(8,128)(2,1)S(1)} %get-tuple-element.42), channel_id=1, source_target_pairs={{0,1},{1,0},{2,3},{3,2},{4,5},{5,4},{6,7},{7,6},{8,9},{9,8},{10,11... | collective-permute-start | bytes 344072 | tf_op jit(solution)/shard_map/ppermute | solution.py:382
  53.3 2.0 %collective-permute-start.3 = (bf16[224,256]{1,0:T(8,128)(2,1)S(1)}, bf16[224,256]{1,0:T(8,128)(2,1)S(1)}, u32[]{:S(2)}, u32[]{:S(2)}) collective-permute-start(bf16[224,256]{1,0:T(8,128)(2,1)S(1)} %get-tuple-element.43), channel_id=1, source_target_pairs={{0,1},{1,0},{2,3},{3,2},{4,5},{5,4},{6,7},{7,6},{8,9},{9,8},{10,11... | collective-permute-start | bytes 344072 | tf_op jit(solution)/shard_map/ppermute | solution.py:382

commit v6 on v4

--- a/solution.py
+++ b/solution.py
@@ -56,19 +56,20 @@
 
 
 def forward_kernel(got_ref, done_ref, out_ref, sorted_ref, sems):
-    n = (SPOTS + STOPW - 1) * 16
-    row = iota((n, PLANES * 32), 0)
-    col = iota((n, PLANES * 32), 1)
-    block = (SPOTS - 1 - lax.shift_right_logical(row, 4)) & 15
-    source = (lax.shift_right_logical(row, 1) & 7) * 32 + block * 2 + (row & 1)
-    order = jnp.where(col == source, 1.0, 0.0).astype(BF16)
-    sorted_ref[...] = jnp.dot(order, got_ref[...], preferred_element_type=F32).astype(BF16)
+    got = got_ref[...]
     copies = []
-    for spot in range(SPOTS):
-        at = (SPOTS - 1 - spot) * 16
-        copies.append(pltpu.make_async_copy(sorted_ref.at[at : at + STOPW * 16], out_ref.at[spot], sems.at[spot]))
-    for copy in copies:
-        copy.start()
+    for low, high, spots in ((112, 224, (0,)), (48, 112, (1, 2, 3, 4)), (0, 48, (5, 6, 7))):
+        row = low + iota((high - low, PLANES * 32), 0)
+        col = iota((high - low, PLANES * 32), 1)
+        block = (SPOTS - 1 - lax.shift_right_logical(row, 4)) & 15
+        source = (lax.shift_right_logical(row, 1) & 7) * 32 + block * 2 + (row & 1)
+        order = jnp.where(col == source, 1.0, 0.0).astype(BF16)
+        sorted_ref[low:high] = jnp.dot(order, got, preferred_element_type=F32).astype(BF16)
+        for spot in spots:
+            at = (SPOTS - 1 - spot) * 16
+            copy = pltpu.make_async_copy(sorted_ref.at[at : at + STOPW * 16], out_ref.at[spot], sems.at[spot])
+            copy.start()
+            copies.append(copy)
     for copy in copies:
         copy.wait()
 

time: 56.2 us -> 56.1 us (level)
  no operation moved by 1% of the time
where the time goes in v6:
time: 56.1 us; the launch traced here: 55.9 us
  starting transfers between devices  23 us (41%)
  Pallas kernels  20.1 us (36%)
  waiting for transfers between devices  12.4 us (22%)
    all_to_all x1, starting transfers between devices, per_device(): lax.all_to_all(packed.reshape(PLANES, 32, 2 * WIDTH), 'mode', 0, 0, tiled...  9.01 us
    ppermute x5, starting transfers between devices, between(): return lax.ppermute(part, 'space', [(i, i ^ pair) for i in range(4)])  8.89 us
    pallas_call x2, Pallas kernels, sort(): kernel_call(functools.partial(sort_kernel, mask), (slab_shape, slab_shape...  7.81 us
    all_to_all x1, waiting for transfers between devices, per_device(): lax.all_to_all(packed.reshape(PLANES, 32, 2 * WIDTH), 'mode', 0, 0, tiled...  6.73 us
    all_to_all x1, starting transfers between devices, per_device(): lax.all_to_all(onward, 'mode', 0, 0, tiled=True, axis_index_groups=P_GROUPS)  5.13 us
    all_to_all x1, waiting for transfers between devices, per_device(): lax.all_to_all(onward, 'mode', 0, 0, tiled=True, axis_index_groups=P_GROUPS)  4.39 us
    pallas_call x1, Pallas kernels, per_device(): kernel_call(last_kernel, (part_shape, part_shape, wide_shape), [VMEM] * 6...  3.36 us
    pallas_call x1, Pallas kernels, per_device(): kernel_call(pack_kernel, shape((PLANES * 32, 2 * WIDTH)), [VMEM] * 3, 200...  1.93 us
  transfers between devices with their start and end apart: 7, of which 3 were waited for; matrix products, arithmetic and copies ran while one was open for 0% of the time, Pallas kernels for 24%

profile of v6, /device:TPU:1, one launch (start us, length us, event | category | flops | bytes accessed | tf_op | source)
XLA Modules:
  0.0 55.9 jit_solution(11947408672501392926)
XLA Ops:
  0.0 1.9 %shard_map.64 = bf16[256,512]{1,0:T(8,128)(2,1)} custom-call(s32[32,128]{1,0:T(8,128)} %bitcast.19, bf16[64,2,256]{2,1,0:T(2,128)(2,1)} %bitcast.18, s32[1,64]{1,0:T(1,128)} %bitcast.20), custom_call_target="tpu_custom_call" | custom-call | flops 20000000 | bytes 400000 | tf_op jit(solution)/shard_map/pallas_call | solution.py:299
  1.9 9.0 %all-to-all-start = ((bf16[8,32,512]{2,1,0:T(8,128)(2,1)}), bf16[8,32,512]{2,1,0:T(8,128)(2,1)S(1)}, u32[]{:S(2)}, u32[]{:S(2)}) async-start(bf16[8,32,512]{2,1,0:T(8,128)(2,1)} %bitcast.14), calls=%async_computation | async-start | bytes 524288 | tf_op jit(solution)/shard_map/all_to_all | solution.py:302
  10.9 3.6 %shard_map.65 = (bf16[2,512,768]{2,1,0:T(8,128)(2,1)S(1)}, bf16[2,512,768]{2,1,0:T(8,128)(2,1)}, bf16[16,128]{1,0:T(8,128)(2,1)S(1)}) custom-call(bf16[2,512,3072]{2,1,0:T(8,128)(2,1)} %bitcast.12), custom_call_target="tpu_custom_call" | custom-call | flops 5000000 | bytes 6000000 | tf_op jit(solution)/shard_map/pallas_call | solution.py:309
  14.6 0.0 copy-start.5
  14.6 6.7 %all-to-all-done = bf16[8,32,512]{2,1,0:T(8,128)(2,1)S(1)} async-done(((bf16[8,32,512]{2,1,0:T(8,128)(2,1)}), bf16[8,32,512]{2,1,0:T(8,128)(2,1)S(1)}, u32[]{:S(2)}, u32[]{:S(2)}) %all-to-all-start) | async-done | bytes 262176 | tf_op jit(solution)/shard_map/all_to_all | solution.py:302
  21.3 0.0 copy-start
  21.3 0.0 copy-start.1
  21.3 1.2 %shard_map.66.after_ref.rest_0_ = bf16[8,112,512]{2,1,0:T(8,128)(2,1)} custom-call(bf16[256,512]{1,0:T(8,128)(2,1)S(1)} %bitcast.11, bf16[16,128]{1,0:T(8,128)(2,1)S(1)} %get-tuple-element.25.done_ref), custom_call_target="tpu_custom_call" | custom-call | flops 70000000 | bytes 1200000 | tf_op jit(solution)/shard_map/pallas_call | solution.py:321
  22.5 5.1 %all-to-all-start.1 = ((bf16[8,112,512]{2,1,0:T(8,128)(2,1)}), bf16[8,112,512]{2,1,0:T(8,128)(2,1)S(1)}, u32[]{:S(2)}, u32[]{:S(2)}) async-start(bf16[8,112,512]{2,1,0:T(8,128)(2,1)} %shard_map.66.after_ref.rest_0_), calls=%async_computation.1 | async-start | bytes 1835008 | tf_op jit(solution)/shard_map/all_to_all | solution.py:339
  27.7 0.0 copy-done.5
  27.7 0.1 reshape.28
  27.8 0.1 copy.8.route_ref
  27.9 0.0 copy-done
  27.9 0.0 copy-done.1
  27.9 0.8 %shard_map.67 = (bf16[2,7,32,128]{3,2,1,0:T(8,128)(2,1)S(1)}, f32[56,128]{1,0:T(8,128)S(1)}) custom-call(s32[4,3]{1,0:T(4,128)S(1)} %copy-done, s32[4]{0:T(128)S(1)} %copy-done.1, s32[64,128]{1,0:T(8,128)S(1)} %copy.8.route_ref, bf16[8,112,512]{2,1,0:T(8,128)(2,1)} %shard_map.66.after_ref.rest_0_), custom_call_target="tpu_custom_call" | custom-call | flops 2000000 | bytes 200000 | tf_op jit(solution)/shard_map/pallas_call | solution.py:332
  28.7 4.2 %shard_map.68 = (bf16[2,512,768]{2,1,0:T(8,128)(2,1)}, bf16[2,512,768]{2,1,0:T(8,128)(2,1)}, bf16[16,128]{1,0:T(8,128)(2,1)}) custom-call(bf16[2,512,3072]{2,1,0:T(8,128)(2,1)} %bitcast.13, bf16[8,112,512]{2,1,0:T(8,128)(2,1)} %shard_map.66.after_ref.rest_0_), custom_call_target="tpu_custom_call" | custom-call | flops 5000000 | bytes 6000000 | tf_op jit(solution)/shard_map/pallas_call | solution.py:309
  32.8 4.4 %all-to-all-done.1.got_ref = bf16[8,112,512]{2,1,0:T(8,128)(2,1)S(1)} async-done(((bf16[8,112,512]{2,1,0:T(8,128)(2,1)}), bf16[8,112,512]{2,1,0:T(8,128)(2,1)S(1)}, u32[]{:S(2)}, u32[]{:S(2)}) %all-to-all-start.1) | async-done | bytes 917536 | tf_op jit(solution)/shard_map/all_to_all | solution.py:339
  37.2 0.0 copy-start.2
  37.2 1.9 %shard_map.69 = (bf16[2,224,256]{2,1,0:T(8,128)(2,1)S(1)}, bf16[448,512]{1,0:T(8,128)(2,1)S(1)}) custom-call(f32[56,128]{1,0:T(8,128)S(1)} %get-tuple-element.26.table_ref, bf16[8,112,512]{2,1,0:T(8,128)(2,1)S(1)} %all-to-all-done.1.got_ref, bf16[2,7,32,128]{3,2,1,0:T(8,128)(2,1)S(1)} %get-tuple-element.30.placer_ref, ...), custom_call_target="tpu_custom_call" | custom-call | flops 1200000000 | bytes 3000000 | tf_op jit(solution)/shard_map/pallas_call | solution.py:351
  39.2 5.0 %collective-permute-start = (bf16[2,224,256]{2,1,0:T(8,128)(2,1)S(1)}, bf16[2,224,256]{2,1,0:T(8,128)(2,1)S(1)}, u32[]{:S(2)}, u32[]{:S(2)}) collective-permute-start(bf16[2,224,256]{2,1,0:T(8,128)(2,1)S(1)} %get-tuple-element.36), channel_id=1, source_target_pairs={{0,1},{1,0},{2,3},{3,2},{4,5},{5,4},{6,7},{7,6},{8,9},{9,8},{10,11... | collective-permute-start | bytes 688136 | tf_op jit(solution)/shard_map/ppermute | solution.py:349
  44.2 0.0 copy-done.2
  44.2 0.0 copy-start.3
  44.2 0.0 copy-start.4
  44.2 1.8 %shard_map.70.own_ref = f32[2,224,256]{2,1,0:T(8,128)S(1)} custom-call(f32[56,128]{1,0:T(8,128)S(1)} %get-tuple-element.26.table_ref, bf16[448,512]{1,0:T(8,128)(2,1)S(1)} %get-tuple-element.34.coef_ref, bf16[2,512,768]{2,1,0:T(8,128)(2,1)S(1)} %copy-done.2), custom_call_target="tpu_custom_call" | custom-call | flops 1100000000 | bytes 3000000 | tf_op jit(solution)/shard_map/pallas_call | solution.py:359
  46.0 0.0 collective-permute-done.other_ref
  46.0 2.5 %collective-permute-start.1 = (bf16[224,256]{1,0:T(8,128)(2,1)S(1)}, bf16[224,256]{1,0:T(8,128)(2,1)S(1)}, u32[]{:S(2)}, u32[]{:S(2)}) collective-permute-start(bf16[224,256]{1,0:T(8,128)(2,1)S(1)} %get-tuple-element.41), channel_id=1, source_target_pairs={{0,2},{1,3},{2,0},{3,1},{4,6},{5,7},{6,4},{7,5},{8,10},{9,11},{10,... | collective-permute-start | bytes 344072 | tf_op jit(solution)/shard_map/ppermute | solution.py:349
  48.6 0.5 collective-permute-start.4
  49.1 0.0 copy-done.3
  49.1 0.0 copy-done.4
  49.1 3.4 %shard_map.72 = (bf16[224,256]{1,0:T(8,128)(2,1)S(1)}, bf16[224,256]{1,0:T(8,128)(2,1)S(1)}, f32[2,224,256]{2,1,0:T(8,128)S(1)}) custom-call(f32[56,128]{1,0:T(8,128)S(1)} %get-tuple-element.26.table_ref, bf16[8,112,512]{2,1,0:T(8,128)(2,1)S(1)} %all-to-all-done.1.got_ref, bf16[2,7,32,128]{3,2,1,0:T(8,128)(2,1)S(1)} %get-tuple-element.30.placer_ref, ...), custom_call_target="tpu_custom_call" | custom-call | flops 2200000000 | bytes 6000000 | tf_op jit(solution)/shard_map/pallas_call | solution.py:365
  52.5 0.0 collective-permute-done.1.far_a_ref
  52.5 0.7 %collective-permute-start.2 = (bf16[224,256]{1,0:T(8,128)(2,1)S(1)}, bf16[224,256]{1,0:T(8,128)(2,1)S(1)}, u32[]{:S(2)}, u32[]{:S(2)}) collective-permute-start(bf16[224,256]{1,0:T(8,128)(2,1)S(1)} %get-tuple-element.42), channel_id=1, source_target_pairs={{0,1},{1,0},{2,3},{3,2},{4,5},{5,4},{6,7},{7,6},{8,9},{9,8},{10,11... | collective-permute-start | bytes 344072 | tf_op jit(solution)/shard_map/ppermute | solution.py:349
  53.2 0.1 collective-permute-start.3
  53.3 1.2 %collective-permute-done.4.far_b_ref = bf16[224,256]{1,0:T(8,128)(2,1)S(1)} collective-permute-done((bf16[224,256]{1,0:T(8,128)(2,1)S(1)}, bf16[224,256]{1,0:T(8,128)(2,1)S(1)}, u32[]{:S(2)}, u32[]{:S(2)}) %collective-permute-start.4) | collective-permute-done | bytes 114720 | tf_op jit(solution)/shard_map/ppermute | solution.py:349
  54.5 0.0 collective-permute-done.2.near_a_ref
  54.5 0.0 collective-permute-done.3.near_b_ref
  54.5 1.3 %shard_map.73 = f32[2,4,2,7,32,32]{5,4,3,2,1,0:T(8,128)} custom-call(f32[2,224,256]{2,1,0:T(8,128)S(1)} %get-tuple-element.38.own_ref, bf16[224,256]{1,0:T(8,128)(2,1)S(1)} %collective-permute-done.2.near_a_ref, bf16[224,256]{1,0:T(8,128)(2,1)S(1)} %collective-permute-done.3.near_b_ref, bf16[224,256]{1,0:T(8,128)(2,1)S(1)} %collective-permute-done.1.far_a_ref, ...), custom_call_target="tpu_custom_call" | custom-call | flops 1000000 | bytes 3000000 | tf_op jit(solution)/shard_map/pallas_call | solution.py:376
  (3 shorter events, 0.1 us)
Async XLA Ops:
  1.9 19.4 %all-to-all-start = ((bf16[8,32,512]{2,1,0:T(8,128)(2,1)}), bf16[8,32,512]{2,1,0:T(8,128)(2,1)S(1)}, u32[]{:S(2)}, u32[]{:S(2)}) async-start(bf16[8,32,512]{2,1,0:T(8,128)(2,1)} %bitcast.14), calls=%async_computation | async-start | bytes 524288 | tf_op jit(solution)/shard_map/all_to_all | solution.py:302
  14.6 13.1 %copy-start.5 = (s32[4096]{0:T(1024)S(1)}, s32[4096]{0:T(1024)}, u32[]{:S(2)}) copy-start(s32[4096]{0:T(1024)} %param.8) | copy-start | bytes 49156
  21.3 6.6 %copy-start = (s32[4,3]{1,0:T(4,128)S(1)}, s32[4,3]{1,0:T(4,128)}, u32[]{:S(2)}) copy-start(s32[4,3]{1,0:T(4,128)} %momenta_ref.1) | copy-start | bytes 148
  21.3 6.6 %copy-start.1 = (s32[4]{0:T(128)S(1)}, s32[4]{0:T(128)}, u32[]{:S(2)}) copy-start(s32[4]{0:T(128)} %gammas_ref.1) | copy-start | bytes 52
  22.5 14.7 %all-to-all-start.1 = ((bf16[8,112,512]{2,1,0:T(8,128)(2,1)}), bf16[8,112,512]{2,1,0:T(8,128)(2,1)S(1)}, u32[]{:S(2)}, u32[]{:S(2)}) async-start(bf16[8,112,512]{2,1,0:T(8,128)(2,1)} %shard_map.66.after_ref.rest_0_), calls=%async_computation.1 | async-start | bytes 1835008 | tf_op jit(solution)/shard_map/all_to_all | solution.py:339
  37.2 7.0 %copy-start.2 = (bf16[2,512,768]{2,1,0:T(8,128)(2,1)S(1)}, bf16[2,512,768]{2,1,0:T(8,128)(2,1)}, u32[]{:S(2)}) copy-start(bf16[2,512,768]{2,1,0:T(8,128)(2,1)} %get-tuple-element.35.slab_ref) | copy-start | bytes 4718596
  39.2 6.8 %collective-permute-start = (bf16[2,224,256]{2,1,0:T(8,128)(2,1)S(1)}, bf16[2,224,256]{2,1,0:T(8,128)(2,1)S(1)}, u32[]{:S(2)}, u32[]{:S(2)}) collective-permute-start(bf16[2,224,256]{2,1,0:T(8,128)(2,1)S(1)} %get-tuple-element.36), channel_id=1, source_target_pairs={{0,1},{1,0},{2,3},{3,2},{4,5},{5,4},{6,7},{7,6},{8,9},{9,8},{10,11... | collective-permute-start | bytes 688136 | tf_op jit(solution)/shard_map/ppermute | solution.py:349
  44.2 4.9 %copy-start.3 = (bf16[2,512,768]{2,1,0:T(8,128)(2,1)S(1)}, bf16[2,512,768]{2,1,0:T(8,128)(2,1)}, u32[]{:S(2)}) copy-start(bf16[2,512,768]{2,1,0:T(8,128)(2,1)} %get-tuple-element.31.far_ref) | copy-start | bytes 4718596
  44.2 4.9 %copy-start.4 = (bf16[2,512,768]{2,1,0:T(8,128)(2,1)S(1)}, bf16[2,512,768]{2,1,0:T(8,128)(2,1)}, u32[]{:S(2)}) copy-start(bf16[2,512,768]{2,1,0:T(8,128)(2,1)} %get-tuple-element.32.near_ref) | copy-start | bytes 4718596
  46.0 6.4 %collective-permute-start.1 = (bf16[224,256]{1,0:T(8,128)(2,1)S(1)}, bf16[224,256]{1,0:T(8,128)(2,1)S(1)}, u32[]{:S(2)}, u32[]{:S(2)}) collective-permute-start(bf16[224,256]{1,0:T(8,128)(2,1)S(1)} %get-tuple-element.41), channel_id=1, source_target_pairs={{0,2},{1,3},{2,0},{3,1},{4,6},{5,7},{6,4},{7,5},{8,10},{9,11},{10,... | collective-permute-start | bytes 344072 | tf_op jit(solution)/shard_map/ppermute | solution.py:349
  48.6 5.9 %collective-permute-start.4 = (bf16[224,256]{1,0:T(8,128)(2,1)S(1)}, bf16[224,256]{1,0:T(8,128)(2,1)S(1)}, u32[]{:S(2)}, u32[]{:S(2)}) collective-permute-start(bf16[224,256]{1,0:T(8,128)(2,1)S(1)} %get-tuple-element.37.before_ref), channel_id=1, source_target_pairs={{0,2},{1,3},{2,0},{3,1},{4,6},{5,7},{6,4},{7,5},{8,10},{9,11},{10,... | collective-permute-start | bytes 344072 | tf_op jit(solution)/shard_map/ppermute | solution.py:349
  52.5 2.0 %collective-permute-start.2 = (bf16[224,256]{1,0:T(8,128)(2,1)S(1)}, bf16[224,256]{1,0:T(8,128)(2,1)S(1)}, u32[]{:S(2)}, u32[]{:S(2)}) collective-permute-start(bf16[224,256]{1,0:T(8,128)(2,1)S(1)} %get-tuple-element.42), channel_id=1, source_target_pairs={{0,1},{1,0},{2,3},{3,2},{4,5},{5,4},{6,7},{7,6},{8,9},{9,8},{10,11... | collective-permute-start | bytes 344072 | tf_op jit(solution)/shard_map/ppermute | solution.py:349
  53.2 1.3 %collective-permute-start.3 = (bf16[224,256]{1,0:T(8,128)(2,1)S(1)}, bf16[224,256]{1,0:T(8,128)(2,1)S(1)}, u32[]{:S(2)}, u32[]{:S(2)}) collective-permute-start(bf16[224,256]{1,0:T(8,128)(2,1)S(1)} %get-tuple-element.43), channel_id=1, source_target_pairs={{0,1},{1,0},{2,3},{3,2},{4,5},{5,4},{6,7},{7,6},{8,9},{9,8},{10,11... | collective-permute-start | bytes 344072 | tf_op jit(solution)/shard_map/ppermute | solution.py:349

commit v7 on v6

--- a/solution.py
+++ b/solution.py
@@ -30,7 +30,7 @@
     return lax.broadcasted_iota(jnp.int32, shape, axis)
 
 
-def pack_kernel(route_ref, coefs_ref, counts_ref, out_ref):
+def pack_kernel(route_ref, coefs_ref, counts_ref, out_hbm, out_ref, sems):
     me = lax.axis_index("mode")
     row = route_ref[pl.ds(me // 2, 1), :]
     row = jnp.where(me % 2 == 1, pltpu.roll(row, 64, 1), row)[:, :ITEMS]
@@ -49,10 +49,18 @@
     counts = jnp.broadcast_to(counts_ref[...], (ITEMS, ITEMS)).astype(F32)
     limit = jnp.sum(jnp.where(i == j, counts, 0.0), axis=1, keepdims=True).astype(jnp.int32)
     keep = iota((ITEMS, WIDTH), 1) < limit
-    for part in range(2):
-        block = jnp.where(keep, coefs_ref[:, part, :].astype(F32), 0.0).astype(BF16)
-        packed = jnp.dot(outgoing, block, preferred_element_type=F32)
-        out_ref[:, part * WIDTH : (part + 1) * WIDTH] = packed.astype(BF16)
+    blocks = [jnp.where(keep, coefs_ref[:, part, :].astype(F32), 0.0).astype(BF16) for part in range(2)]
+    writes = []
+    for half in range(2):
+        rows = slice(half * 128, (half + 1) * 128)
+        for part in range(2):
+            packed = jnp.dot(outgoing[rows], blocks[part], preferred_element_type=F32)
+            out_ref[rows, part * WIDTH : (part + 1) * WIDTH] = packed.astype(BF16)
+        write = pltpu.make_async_copy(out_ref.at[rows], out_hbm.at[rows], sems.at[half])
+        write.start()
+        writes.append(write)
+    for write in writes:
+        write.wait()
 
 
 def forward_kernel(got_ref, done_ref, out_ref, sorted_ref, sems):
@@ -297,7 +305,14 @@
 
 def per_device(coefs, counts, route, basis, momenta, gammas):
     packed = kernel_call(
-        pack_kernel, shape((PLANES * 32, 2 * WIDTH)), [VMEM] * 3, 20_000_000, 400_000, limit=60
+        pack_kernel,
+        shape((PLANES * 32, 2 * WIDTH)),
+        [VMEM] * 3,
+        20_000_000,
+        400_000,
+        [pltpu.VMEM((PLANES * 32, 2 * WIDTH), BF16), DMA((2,))],
+        limit=60,
+        out_specs=HBM,
     )(route.reshape(32, 128), coefs.reshape(ITEMS, 2, WIDTH), counts.reshape(1, ITEMS))
     first = lax.all_to_all(
         packed.reshape(PLANES, 32, 2 * WIDTH), "mode", 0, 0, tiled=True, axis_index_groups=Z_GROUPS

time: 56.1 us -> 56.2 us (level)
  no operation moved by 1% of the time
where the time goes in v7:
time: 56.2 us; the launch traced here: 55.9 us
  starting transfers between devices  23.1 us (41%)
  Pallas kernels  20.1 us (36%)
  waiting for transfers between devices  12.4 us (22%)
    all_to_all x1, starting transfers between devices, per_device(): lax.all_to_all(packed.reshape(PLANES, 32, 2 * WIDTH), 'mode', 0, 0, tiled...  9.03 us
    ppermute x5, starting transfers between devices, between(): return lax.ppermute(part, 'space', [(i, i ^ pair) for i in range(4)])  8.9 us
    pallas_call x2, Pallas kernels, sort(): kernel_call(functools.partial(sort_kernel, mask), (slab_shape, slab_shape...  7.81 us
    all_to_all x1, waiting for transfers between devices, per_device(): lax.all_to_all(packed.reshape(PLANES, 32, 2 * WIDTH), 'mode', 0, 0, tiled...  6.73 us
    all_to_all x1, starting transfers between devices, per_device(): lax.all_to_all(onward, 'mode', 0, 0, tiled=True, axis_index_groups=P_GROUPS)  5.13 us
    all_to_all x1, waiting for transfers between devices, per_device(): lax.all_to_all(onward, 'mode', 0, 0, tiled=True, axis_index_groups=P_GROUPS)  4.39 us
    pallas_call x1, Pallas kernels, per_device(): kernel_call(last_kernel, (part_shape, part_shape, wide_shape), [VMEM] * 6...  3.36 us
    pallas_call x1, Pallas kernels, per_device(): kernel_call(pack_kernel, shape((PLANES * 32, 2 * WIDTH)), [VMEM] * 3, 200...  1.91 us
  transfers between devices with their start and end apart: 7, of which 3 were waited for; matrix products, arithmetic and copies ran while one was open for 0% of the time, Pallas kernels for 24%

profile of v7, /device:TPU:1, one launch (start us, length us, event | category | flops | bytes accessed | tf_op | source)
XLA Modules:
  0.0 55.9 jit_solution(1875341739974513083)
XLA Ops:
  0.0 1.9 %shard_map.64 = bf16[256,512]{1,0:T(8,128)(2,1)} custom-call(s32[32,128]{1,0:T(8,128)} %bitcast.19, bf16[64,2,256]{2,1,0:T(2,128)(2,1)} %bitcast.18, s32[1,64]{1,0:T(1,128)} %bitcast.20), custom_call_target="tpu_custom_call" | custom-call | flops 20000000 | bytes 400000 | tf_op jit(solution)/shard_map/pallas_call | solution.py:307
  1.9 9.0 %all-to-all-start = ((bf16[8,32,512]{2,1,0:T(8,128)(2,1)}), bf16[8,32,512]{2,1,0:T(8,128)(2,1)S(1)}, u32[]{:S(2)}, u32[]{:S(2)}) async-start(bf16[8,32,512]{2,1,0:T(8,128)(2,1)} %bitcast.14), calls=%async_computation | async-start | bytes 524288 | tf_op jit(solution)/shard_map/all_to_all | solution.py:317
  10.9 3.6 %shard_map.65 = (bf16[2,512,768]{2,1,0:T(8,128)(2,1)S(1)}, bf16[2,512,768]{2,1,0:T(8,128)(2,1)}, bf16[16,128]{1,0:T(8,128)(2,1)S(1)}) custom-call(bf16[2,512,3072]{2,1,0:T(8,128)(2,1)} %bitcast.12), custom_call_target="tpu_custom_call" | custom-call | flops 5000000 | bytes 6000000 | tf_op jit(solution)/shard_map/pallas_call | solution.py:324
  14.6 0.0 copy-start.5
  14.6 6.7 %all-to-all-done = bf16[8,32,512]{2,1,0:T(8,128)(2,1)S(1)} async-done(((bf16[8,32,512]{2,1,0:T(8,128)(2,1)}), bf16[8,32,512]{2,1,0:T(8,128)(2,1)S(1)}, u32[]{:S(2)}, u32[]{:S(2)}) %all-to-all-start) | async-done | bytes 262176 | tf_op jit(solution)/shard_map/all_to_all | solution.py:317
  21.3 0.0 copy-start
  21.3 0.0 copy-start.1
  21.3 1.2 %shard_map.66.after_ref.rest_0_ = bf16[8,112,512]{2,1,0:T(8,128)(2,1)} custom-call(bf16[256,512]{1,0:T(8,128)(2,1)S(1)} %bitcast.11, bf16[16,128]{1,0:T(8,128)(2,1)S(1)} %get-tuple-element.25.done_ref), custom_call_target="tpu_custom_call" | custom-call | flops 70000000 | bytes 1200000 | tf_op jit(solution)/shard_map/pallas_call | solution.py:336
  22.5 5.1 %all-to-all-start.1 = ((bf16[8,112,512]{2,1,0:T(8,128)(2,1)}), bf16[8,112,512]{2,1,0:T(8,128)(2,1)S(1)}, u32[]{:S(2)}, u32[]{:S(2)}) async-start(bf16[8,112,512]{2,1,0:T(8,128)(2,1)} %shard_map.66.after_ref.rest_0_), calls=%async_computation.1 | async-start | bytes 1835008 | tf_op jit(solution)/shard_map/all_to_all | solution.py:354
  27.7 0.0 copy-done.5
  27.7 0.1 reshape.28
  27.8 0.1 copy.8.route_ref
  27.9 0.0 copy-done
  27.9 0.0 copy-done.1
  27.9 0.8 %shard_map.67 = (bf16[2,7,32,128]{3,2,1,0:T(8,128)(2,1)S(1)}, f32[56,128]{1,0:T(8,128)S(1)}) custom-call(s32[4,3]{1,0:T(4,128)S(1)} %copy-done, s32[4]{0:T(128)S(1)} %copy-done.1, s32[64,128]{1,0:T(8,128)S(1)} %copy.8.route_ref, bf16[8,112,512]{2,1,0:T(8,128)(2,1)} %shard_map.66.after_ref.rest_0_), custom_call_target="tpu_custom_call" | custom-call | flops 2000000 | bytes 200000 | tf_op jit(solution)/shard_map/pallas_call | solution.py:347
  28.7 4.2 %shard_map.68 = (bf16[2,512,768]{2,1,0:T(8,128)(2,1)}, bf16[2,512,768]{2,1,0:T(8,128)(2,1)}, bf16[16,128]{1,0:T(8,128)(2,1)}) custom-call(bf16[2,512,3072]{2,1,0:T(8,128)(2,1)} %bitcast.13, bf16[8,112,512]{2,1,0:T(8,128)(2,1)} %shard_map.66.after_ref.rest_0_), custom_call_target="tpu_custom_call" | custom-call | flops 5000000 | bytes 6000000 | tf_op jit(solution)/shard_map/pallas_call | solution.py:324
  32.8 4.4 %all-to-all-done.1.got_ref = bf16[8,112,512]{2,1,0:T(8,128)(2,1)S(1)} async-done(((bf16[8,112,512]{2,1,0:T(8,128)(2,1)}), bf16[8,112,512]{2,1,0:T(8,128)(2,1)S(1)}, u32[]{:S(2)}, u32[]{:S(2)}) %all-to-all-start.1) | async-done | bytes 917536 | tf_op jit(solution)/shard_map/all_to_all | solution.py:354
  37.2 0.0 copy-start.2
  37.2 1.9 %shard_map.69 = (bf16[2,224,256]{2,1,0:T(8,128)(2,1)S(1)}, bf16[448,512]{1,0:T(8,128)(2,1)S(1)}) custom-call(f32[56,128]{1,0:T(8,128)S(1)} %get-tuple-element.26.table_ref, bf16[8,112,512]{2,1,0:T(8,128)(2,1)S(1)} %all-to-all-done.1.got_ref, bf16[2,7,32,128]{3,2,1,0:T(8,128)(2,1)S(1)} %get-tuple-element.30.placer_ref, ...), custom_call_target="tpu_custom_call" | custom-call | flops 1200000000 | bytes 3000000 | tf_op jit(solution)/shard_map/pallas_call | solution.py:366
  39.2 5.0 %collective-permute-start = (bf16[2,224,256]{2,1,0:T(8,128)(2,1)S(1)}, bf16[2,224,256]{2,1,0:T(8,128)(2,1)S(1)}, u32[]{:S(2)}, u32[]{:S(2)}) collective-permute-start(bf16[2,224,256]{2,1,0:T(8,128)(2,1)S(1)} %get-tuple-element.36), channel_id=1, source_target_pairs={{0,1},{1,0},{2,3},{3,2},{4,5},{5,4},{6,7},{7,6},{8,9},{9,8},{10,11... | collective-permute-start | bytes 688136 | tf_op jit(solution)/shard_map/ppermute | solution.py:364
  44.2 0.0 copy-done.2
  44.2 0.0 copy-start.3
  44.2 0.0 copy-start.4
  44.2 1.8 %shard_map.70.own_ref = f32[2,224,256]{2,1,0:T(8,128)S(1)} custom-call(f32[56,128]{1,0:T(8,128)S(1)} %get-tuple-element.26.table_ref, bf16[448,512]{1,0:T(8,128)(2,1)S(1)} %get-tuple-element.34.coef_ref, bf16[2,512,768]{2,1,0:T(8,128)(2,1)S(1)} %copy-done.2), custom_call_target="tpu_custom_call" | custom-call | flops 1100000000 | bytes 3000000 | tf_op jit(solution)/shard_map/pallas_call | solution.py:374
  46.0 0.0 collective-permute-done.other_ref
  46.0 2.5 %collective-permute-start.1 = (bf16[224,256]{1,0:T(8,128)(2,1)S(1)}, bf16[224,256]{1,0:T(8,128)(2,1)S(1)}, u32[]{:S(2)}, u32[]{:S(2)}) collective-permute-start(bf16[224,256]{1,0:T(8,128)(2,1)S(1)} %get-tuple-element.41), channel_id=1, source_target_pairs={{0,2},{1,3},{2,0},{3,1},{4,6},{5,7},{6,4},{7,5},{8,10},{9,11},{10,... | collective-permute-start | bytes 344072 | tf_op jit(solution)/shard_map/ppermute | solution.py:364
  48.5 0.5 collective-permute-start.4
  49.1 0.0 copy-done.3
  49.1 0.0 copy-done.4
  49.1 3.4 %shard_map.72 = (bf16[224,256]{1,0:T(8,128)(2,1)S(1)}, bf16[224,256]{1,0:T(8,128)(2,1)S(1)}, f32[2,224,256]{2,1,0:T(8,128)S(1)}) custom-call(f32[56,128]{1,0:T(8,128)S(1)} %get-tuple-element.26.table_ref, bf16[8,112,512]{2,1,0:T(8,128)(2,1)S(1)} %all-to-all-done.1.got_ref, bf16[2,7,32,128]{3,2,1,0:T(8,128)(2,1)S(1)} %get-tuple-element.30.placer_ref, ...), custom_call_target="tpu_custom_call" | custom-call | flops 2200000000 | bytes 6000000 | tf_op jit(solution)/shard_map/pallas_call | solution.py:380
  52.5 0.0 collective-permute-done.1.far_a_ref
  52.5 0.7 %collective-permute-start.2 = (bf16[224,256]{1,0:T(8,128)(2,1)S(1)}, bf16[224,256]{1,0:T(8,128)(2,1)S(1)}, u32[]{:S(2)}, u32[]{:S(2)}) collective-permute-start(bf16[224,256]{1,0:T(8,128)(2,1)S(1)} %get-tuple-element.42), channel_id=1, source_target_pairs={{0,1},{1,0},{2,3},{3,2},{4,5},{5,4},{6,7},{7,6},{8,9},{9,8},{10,11... | collective-permute-start | bytes 344072 | tf_op jit(solution)/shard_map/ppermute | solution.py:364
  53.2 0.1 collective-permute-start.3
  53.3 1.3 %collective-permute-done.4.far_b_ref = bf16[224,256]{1,0:T(8,128)(2,1)S(1)} collective-permute-done((bf16[224,256]{1,0:T(8,128)(2,1)S(1)}, bf16[224,256]{1,0:T(8,128)(2,1)S(1)}, u32[]{:S(2)}, u32[]{:S(2)}) %collective-permute-start.4) | collective-permute-done | bytes 114720 | tf_op jit(solution)/shard_map/ppermute | solution.py:364
  54.5 0.0 collective-permute-done.2.near_a_ref
  54.5 0.0 collective-permute-done.3.near_b_ref
  54.5 1.3 %shard_map.73 = f32[2,4,2,7,32,32]{5,4,3,2,1,0:T(8,128)} custom-call(f32[2,224,256]{2,1,0:T(8,128)S(1)} %get-tuple-element.38.own_ref, bf16[224,256]{1,0:T(8,128)(2,1)S(1)} %collective-permute-done.2.near_a_ref, bf16[224,256]{1,0:T(8,128)(2,1)S(1)} %collective-permute-done.3.near_b_ref, bf16[224,256]{1,0:T(8,128)(2,1)S(1)} %collective-permute-done.1.far_a_ref, ...), custom_call_target="tpu_custom_call" | custom-call | flops 1000000 | bytes 3000000 | tf_op jit(solution)/shard_map/pallas_call | solution.py:391
  (3 shorter events, 0.1 us)
Async XLA Ops:
  1.9 19.4 %all-to-all-start = ((bf16[8,32,512]{2,1,0:T(8,128)(2,1)}), bf16[8,32,512]{2,1,0:T(8,128)(2,1)S(1)}, u32[]{:S(2)}, u32[]{:S(2)}) async-start(bf16[8,32,512]{2,1,0:T(8,128)(2,1)} %bitcast.14), calls=%async_computation | async-start | bytes 524288 | tf_op jit(solution)/shard_map/all_to_all | solution.py:317
  14.6 13.1 %copy-start.5 = (s32[4096]{0:T(1024)S(1)}, s32[4096]{0:T(1024)}, u32[]{:S(2)}) copy-start(s32[4096]{0:T(1024)} %param.8) | copy-start | bytes 49156
  21.3 6.6 %copy-start = (s32[4,3]{1,0:T(4,128)S(1)}, s32[4,3]{1,0:T(4,128)}, u32[]{:S(2)}) copy-start(s32[4,3]{1,0:T(4,128)} %momenta_ref.1) | copy-start | bytes 148
  21.3 6.6 %copy-start.1 = (s32[4]{0:T(128)S(1)}, s32[4]{0:T(128)}, u32[]{:S(2)}) copy-start(s32[4]{0:T(128)} %gammas_ref.1) | copy-start | bytes 52
  22.5 14.7 %all-to-all-start.1 = ((bf16[8,112,512]{2,1,0:T(8,128)(2,1)}), bf16[8,112,512]{2,1,0:T(8,128)(2,1)S(1)}, u32[]{:S(2)}, u32[]{:S(2)}) async-start(bf16[8,112,512]{2,1,0:T(8,128)(2,1)} %shard_map.66.after_ref.rest_0_), calls=%async_computation.1 | async-start | bytes 1835008 | tf_op jit(solution)/shard_map/all_to_all | solution.py:354
  37.2 7.0 %copy-start.2 = (bf16[2,512,768]{2,1,0:T(8,128)(2,1)S(1)}, bf16[2,512,768]{2,1,0:T(8,128)(2,1)}, u32[]{:S(2)}) copy-start(bf16[2,512,768]{2,1,0:T(8,128)(2,1)} %get-tuple-element.35.slab_ref) | copy-start | bytes 4718596
  39.2 6.8 %collective-permute-start = (bf16[2,224,256]{2,1,0:T(8,128)(2,1)S(1)}, bf16[2,224,256]{2,1,0:T(8,128)(2,1)S(1)}, u32[]{:S(2)}, u32[]{:S(2)}) collective-permute-start(bf16[2,224,256]{2,1,0:T(8,128)(2,1)S(1)} %get-tuple-element.36), channel_id=1, source_target_pairs={{0,1},{1,0},{2,3},{3,2},{4,5},{5,4},{6,7},{7,6},{8,9},{9,8},{10,11... | collective-permute-start | bytes 688136 | tf_op jit(solution)/shard_map/ppermute | solution.py:364
  44.2 4.9 %copy-start.3 = (bf16[2,512,768]{2,1,0:T(8,128)(2,1)S(1)}, bf16[2,512,768]{2,1,0:T(8,128)(2,1)}, u32[]{:S(2)}) copy-start(bf16[2,512,768]{2,1,0:T(8,128)(2,1)} %get-tuple-element.31.far_ref) | copy-start | bytes 4718596
  44.2 4.9 %copy-start.4 = (bf16[2,512,768]{2,1,0:T(8,128)(2,1)S(1)}, bf16[2,512,768]{2,1,0:T(8,128)(2,1)}, u32[]{:S(2)}) copy-start(bf16[2,512,768]{2,1,0:T(8,128)(2,1)} %get-tuple-element.32.near_ref) | copy-start | bytes 4718596
  46.0 6.4 %collective-permute-start.1 = (bf16[224,256]{1,0:T(8,128)(2,1)S(1)}, bf16[224,256]{1,0:T(8,128)(2,1)S(1)}, u32[]{:S(2)}, u32[]{:S(2)}) collective-permute-start(bf16[224,256]{1,0:T(8,128)(2,1)S(1)} %get-tuple-element.41), channel_id=1, source_target_pairs={{0,2},{1,3},{2,0},{3,1},{4,6},{5,7},{6,4},{7,5},{8,10},{9,11},{10,... | collective-permute-start | bytes 344072 | tf_op jit(solution)/shard_map/ppermute | solution.py:364
  48.5 6.0 %collective-permute-start.4 = (bf16[224,256]{1,0:T(8,128)(2,1)S(1)}, bf16[224,256]{1,0:T(8,128)(2,1)S(1)}, u32[]{:S(2)}, u32[]{:S(2)}) collective-permute-start(bf16[224,256]{1,0:T(8,128)(2,1)S(1)} %get-tuple-element.37.before_ref), channel_id=1, source_target_pairs={{0,2},{1,3},{2,0},{3,1},{4,6},{5,7},{6,4},{7,5},{8,10},{9,11},{10,... | collective-permute-start | bytes 344072 | tf_op jit(solution)/shard_map/ppermute | solution.py:364
  52.5 2.1 %collective-permute-start.2 = (bf16[224,256]{1,0:T(8,128)(2,1)S(1)}, bf16[224,256]{1,0:T(8,128)(2,1)S(1)}, u32[]{:S(2)}, u32[]{:S(2)}) collective-permute-start(bf16[224,256]{1,0:T(8,128)(2,1)S(1)} %get-tuple-element.42), channel_id=1, source_target_pairs={{0,1},{1,0},{2,3},{3,2},{4,5},{5,4},{6,7},{7,6},{8,9},{9,8},{10,11... | collective-permute-start | bytes 344072 | tf_op jit(solution)/shard_map/ppermute | solution.py:364
  53.2 1.4 %collective-permute-start.3 = (bf16[224,256]{1,0:T(8,128)(2,1)S(1)}, bf16[224,256]{1,0:T(8,128)(2,1)S(1)}, u32[]{:S(2)}, u32[]{:S(2)}) collective-permute-start(bf16[224,256]{1,0:T(8,128)(2,1)S(1)} %get-tuple-element.43), channel_id=1, source_target_pairs={{0,1},{1,0},{2,3},{3,2},{4,5},{5,4},{6,7},{7,6},{8,9},{9,8},{10,11... | collective-permute-start | bytes 344072 | tf_op jit(solution)/shard_map/ppermute | solution.py:364
